TPU v7x, 32 devices: a whole 2x2x4 slice. The times are simulated.
32 devices in a mesh: dp: 8 (over z, x), tensor: 4 (over y, core).
Axes of the slice: x: 2, y: 2, z: 4, core: 2. Of those that a mesh axis runs over, the one named last changes fastest.
Arguments:
- tokens: bfloat16 [16384, 768], P(('dp', 'tensor')), may hold values from -6 to 6
- prefix: int32 [16], P('dp'), may hold values from 102 to 512
- cotangent: bfloat16 [16384, 768], P(('dp', 'tensor')), may hold values from -6 to 6
- first_gain: float32 [768], P('dp'), may hold values from 0.1 to 1.9
- first_shift: float32 [768], P('dp'), may hold values from -2 to 2
- qkv_weight: float32 [3, 768, 768], P(None, 'dp', 'tensor'), may hold values from -0.21875 to 0.21875
- qv_bias: float32 [2, 768], P(None, 'dp'), may hold values from -1.2 to 1.2
- out_weight: float32 [768, 768], P(None, 'dp'), may hold values from -0.875 to 0.875
- out_bias: float32 [768], P('dp'), may hold values from -2 to 2
- second_gain: float32 [768], P('dp'), may hold values from 0.1 to 1.9
- second_shift: float32 [768], P('dp'), may hold values from -2 to 2
- fc_weight: float32 [768, 3072], P('dp', 'tensor'), may hold values from -0.21875 to 0.21875
- fc_bias: float32 [3072], P('dp'), may hold values from -3 to 3
- proj_weight: float32 [3072, 768], P('tensor', 'dp'), may hold values from -0.109375 to 0.109375
- proj_bias: float32 [768], P('dp'), may hold values from -2 to 2
Outputs:
- block_out: bfloat16 [16384, 768], P(('dp', 'tensor'))
- input_grad: bfloat16 [16384, 768], P(('dp', 'tensor'))
- first_gain_grad: float32 [768], P('dp')
- first_shift_grad: float32 [768], P('dp')
- qkv_weight_grad: float32 [3, 768, 768], P(None, 'dp', 'tensor')
- qv_bias_grad: float32 [2, 768], P(None, 'dp')
- out_weight_grad: float32 [768, 768], P(None, 'dp')
- out_bias_grad: float32 [768], P('dp')
- second_gain_grad: float32 [768], P('dp')
- second_shift_grad: float32 [768], P('dp')
- fc_weight_grad: float32 [768, 3072], P('dp', 'tensor')
- fc_bias_grad: float32 [3072], P('dp')
- proj_weight_grad: float32 [3072, 768], P('tensor', 'dp')
- proj_bias_grad: float32 [768], P('dp')
All inputs are finite; a program needn't handle non-finite values.
Results may differ from a plain program's by a relative error of at most 0.013.
The roundings to bfloat16 on the way count: a program that leaves them out, or rounds other values in their place, can miss the bound.
Values may be sent and summed in bfloat16 or wider, within the bound.
A program may use at most 128 MiB of HBM per device.

v0:
```python
from functools import partial
import math

import jax
import jax.numpy as jnp
from jax import lax
from jax.sharding import PartitionSpec as P

HD = 64
LEN = 1024


EPSILON = 1e-05


def layer_norm(values, norm_gain, norm_shift):
    average = jnp.mean(values, axis=-1, keepdims=True)
    centred = values - average
    variance = jnp.mean(centred * centred, axis=-1, keepdims=True)
    return centred * lax.rsqrt(variance + EPSILON) * norm_gain + norm_shift


def on_device(
    tokens,
    prefix,
    cotangent,
    first_gain,
    first_shift,
    qkv_weight,
    qv_bias,
    out_weight,
    out_bias,
    second_gain,
    second_shift,
    fc_weight,
    fc_bias,
    proj_weight,
    proj_bias,
):
    low_type = jnp.bfloat16
    full_type = jnp.float32
    gathered = (
        lax.all_gather(qkv_weight.astype(low_type), "dp", axis=1, tiled=True),
        lax.all_gather(out_weight.astype(low_type), "dp", axis=1, tiled=True),
        lax.all_gather(fc_weight.astype(low_type), "dp", axis=0, tiled=True),
        lax.all_gather(proj_weight.astype(low_type), "dp", axis=1, tiled=True),
        lax.all_gather(first_gain.astype(low_type), "dp", axis=0, tiled=True),
        lax.all_gather(first_shift.astype(low_type), "dp", axis=0, tiled=True),
        lax.all_gather(qv_bias.astype(low_type), "dp", axis=1, tiled=True),
        lax.all_gather(out_bias.astype(low_type), "dp", axis=0, tiled=True),
        lax.all_gather(second_gain.astype(low_type), "dp", axis=0, tiled=True),
        lax.all_gather(second_shift.astype(low_type), "dp", axis=0, tiled=True),
        lax.all_gather(fc_bias.astype(low_type), "dp", axis=0, tiled=True),
        lax.all_gather(proj_bias.astype(low_type), "dp", axis=0, tiled=True),
    )
    qkv_full, out_full, fc_local, proj_local = (gathered[0], gathered[1], gathered[2], gathered[3])
    gain_one = gathered[4].astype(full_type)
    shift_one = gathered[5].astype(full_type)
    qv_full = gathered[6]
    out_shift = gathered[7].astype(full_type)
    gain_two = gathered[8].astype(full_type)
    shift_two = gathered[9].astype(full_type)
    fc_shift_full = gathered[10]
    proj_shift = gathered[11].astype(full_type)
    tensor_rank = lax.axis_index("tensor")
    head_cols = qkv_full.shape[2]
    unit_cols = fc_local.shape[1]
    qv_local = lax.dynamic_slice_in_dim(qv_full, tensor_rank * head_cols, head_cols, 1).astype(
        full_type
    )
    fc_shift = lax.dynamic_slice_in_dim(
        fc_shift_full, tensor_rank * unit_cols, unit_cols, 0
    ).astype(full_type)
    out_rows = lax.dynamic_slice_in_dim(out_full, tensor_rank * head_cols, head_cols, 0)
    inputs = tokens.astype(full_type)
    normed_one, norm_one_back = jax.vjp(layer_norm, inputs, gain_one, shift_one)
    gathered_one = lax.all_gather(normed_one.astype(low_type), "tensor", axis=0, tiled=True)
    projected = jnp.einsum("nd,kde->kne", gathered_one, qkv_full, preferred_element_type=full_type)
    queries = (projected[0] + qv_local[0]).astype(low_type)
    key_heads = projected[1].astype(low_type)
    value_heads = (projected[2] + qv_local[1]).astype(low_type)
    rows_all = gathered_one.shape[0]
    block_rows = min(512, LEN)
    per_seq = LEN // block_rows
    block_count = rows_all // block_rows
    heads_local = head_cols // HD
    score_scale = 1.0 / math.sqrt(HD)
    query_blocks = queries.reshape(block_count, block_rows, heads_local, HD)
    key_seqs = key_heads.reshape(rows_all // LEN, LEN, heads_local, HD)
    value_seqs = value_heads.reshape(rows_all // LEN, LEN, heads_local, HD)

    def block_scores(block_index):
        sequence = block_index // per_seq
        offset = block_index % per_seq * block_rows
        key_seq = lax.dynamic_index_in_dim(key_seqs, sequence, 0, keepdims=False)
        value_seq = lax.dynamic_index_in_dim(value_seqs, sequence, 0, keepdims=False)
        prefix_size = lax.dynamic_index_in_dim(prefix, sequence, 0, keepdims=False)
        query_block = lax.dynamic_index_in_dim(query_blocks, block_index, 0, keepdims=False)
        scores = (
            jnp.einsum("qhd,khd->hqk", query_block, key_seq, preferred_element_type=full_type)
            * score_scale
        )
        row_pos = offset + lax.broadcasted_iota(jnp.int32, (block_rows, LEN), 0)
        col_pos = lax.broadcasted_iota(jnp.int32, (block_rows, LEN), 1)
        allowed = (col_pos < prefix_size) | (col_pos <= row_pos)
        scores = jnp.where(allowed[None], scores, -1e30)
        return (scores, sequence, query_block, key_seq, value_seq)

    def forward_block(block_index):
        scores, sequence, query_block, key_seq, value_seq = block_scores(block_index)
        row_peak = jnp.max(scores, axis=-1, keepdims=True)
        weights = jnp.exp(scores - row_peak)
        row_total = jnp.sum(weights, axis=-1, keepdims=True)
        shares = (weights / row_total).astype(low_type)
        context_block = jnp.einsum(
            "hqk,khd->qhd", shares, value_seq, preferred_element_type=full_type
        )
        log_total = (row_peak + jnp.log(row_total))[..., 0]
        return (context_block.astype(low_type).reshape(block_rows, head_cols), log_total)

    context_blocks, log_totals = lax.map(forward_block, jnp.arange(block_count))
    context = context_blocks.reshape(rows_all, head_cols)
    partial_out = jnp.dot(context, out_rows, preferred_element_type=full_type)
    attn_out = lax.psum_scatter(partial_out, "tensor", scatter_dimension=0, tiled=True) + out_shift
    middle = inputs + attn_out
    normed_two, norm_two_back = jax.vjp(layer_norm, middle, gain_two, shift_two)
    gathered_two = lax.all_gather(normed_two.astype(low_type), "tensor", axis=0, tiled=True)
    pre_act = jnp.dot(gathered_two, fc_local, preferred_element_type=full_type) + fc_shift
    activated, gelu_back = jax.vjp(partial(jax.nn.gelu, approximate=True), pre_act)
    hidden = activated.astype(low_type)
    partial_mlp = jnp.dot(hidden, proj_local, preferred_element_type=full_type)
    mlp_out = (
        lax.psum_scatter(
            partial_mlp.astype(jnp.bfloat16), "tensor", scatter_dimension=0, tiled=True
        ).astype(jnp.float32)
        + proj_shift
    )
    block_out = (middle + mlp_out).astype(low_type)
    proj_shift_grad = jnp.sum(cotangent, axis=0, dtype=full_type)
    mlp_grad_all = lax.all_gather(cotangent, "tensor", axis=0, tiled=True)
    proj_grad = jnp.einsum("nf,nd->fd", hidden, mlp_grad_all, preferred_element_type=full_type)
    hidden_grad = jnp.einsum(
        "nd,fd->nf", mlp_grad_all, proj_local, preferred_element_type=full_type
    )
    pre_grad = gelu_back(hidden_grad)[0].astype(low_type)
    fc_shift_local = jnp.sum(pre_grad, axis=0, dtype=full_type)
    fc_shift_grad = lax.dynamic_update_slice_in_dim(
        jnp.zeros(fc_shift_full.shape, full_type), fc_shift_local, tensor_rank * unit_cols, 0
    )
    fc_grad = jnp.einsum("nd,nf->df", gathered_two, pre_grad, preferred_element_type=full_type)
    normed_two_part = jnp.einsum("nf,df->nd", pre_grad, fc_local, preferred_element_type=full_type)
    normed_two_grad = lax.psum_scatter(normed_two_part, "tensor", scatter_dimension=0, tiled=True)
    middle_back, gain_two_grad, shift_two_grad = norm_two_back(normed_two_grad)
    middle_grad = cotangent.astype(full_type) + middle_back
    attn_grad = middle_grad.astype(low_type)
    out_shift_grad = jnp.sum(attn_grad, axis=0, dtype=full_type)
    attn_grad_all = lax.all_gather(attn_grad, "tensor", axis=0, tiled=True)
    out_grad = jnp.einsum("nc,nd->cd", context, attn_grad_all, preferred_element_type=full_type)
    context_grad = jnp.einsum(
        "nd,cd->nc", attn_grad_all, out_rows, preferred_element_type=full_type
    ).astype(low_type)
    grad_blocks = context_grad.reshape(block_count, block_rows, heads_local, HD)

    def backward_block(running, block_index):
        key_grads, value_grads = running
        scores, sequence, query_block, key_seq, value_seq = block_scores(block_index)
        log_total = lax.dynamic_index_in_dim(log_totals, block_index, 0, keepdims=False)
        chances = jnp.exp(scores - log_total[..., None])
        shares = chances.astype(low_type)
        grad_block = lax.dynamic_index_in_dim(grad_blocks, block_index, 0, keepdims=False)
        share_grad = jnp.einsum(
            "qhd,khd->hqk", grad_block, value_seq, preferred_element_type=full_type
        )
        centre = jnp.sum(share_grad * chances, axis=-1, keepdims=True)
        score_grad = (chances * (share_grad - centre)).astype(low_type)
        query_grad = (
            jnp.einsum("hqk,khd->qhd", score_grad, key_seq, preferred_element_type=full_type)
            * score_scale
        )
        key_part = (
            jnp.einsum("hqk,qhd->khd", score_grad, query_block, preferred_element_type=full_type)
            * score_scale
        )
        value_part = jnp.einsum(
            "hqk,qhd->khd", shares, grad_block, preferred_element_type=full_type
        )
        key_old = lax.dynamic_index_in_dim(key_grads, sequence, 0, keepdims=False)
        value_old = lax.dynamic_index_in_dim(value_grads, sequence, 0, keepdims=False)
        key_grads = lax.dynamic_update_index_in_dim(key_grads, key_old + key_part, sequence, 0)
        value_grads = lax.dynamic_update_index_in_dim(
            value_grads, value_old + value_part, sequence, 0
        )
        return (
            (key_grads, value_grads),
            query_grad.astype(low_type).reshape(block_rows, head_cols),
        )

    initial = (jnp.zeros(key_seqs.shape, full_type), jnp.zeros(key_seqs.shape, full_type))
    (key_grads, value_grads), query_grads = lax.scan(
        backward_block, initial, jnp.arange(block_count)
    )
    query_grad = query_grads.reshape(rows_all, head_cols)
    key_grad = key_grads.reshape(rows_all, head_cols).astype(low_type)
    value_grad = value_grads.reshape(rows_all, head_cols).astype(low_type)
    stacked = jnp.stack([query_grad, key_grad, value_grad])
    qkv_grad = jnp.einsum("nd,kne->kde", gathered_one, stacked, preferred_element_type=full_type)
    qv_local_grad = jnp.stack(
        [jnp.sum(query_grad, axis=0, dtype=full_type), jnp.sum(value_grad, axis=0, dtype=full_type)]
    )
    qv_grad = lax.dynamic_update_slice_in_dim(
        jnp.zeros(qv_full.shape, full_type), qv_local_grad, tensor_rank * head_cols, 1
    )
    normed_one_part = jnp.einsum("kne,kde->nd", stacked, qkv_full, preferred_element_type=full_type)
    normed_one_grad = lax.psum_scatter(normed_one_part, "tensor", scatter_dimension=0, tiled=True)
    inputs_back, gain_one_grad, shift_one_grad = norm_one_back(normed_one_grad)
    input_grad = (middle_grad + inputs_back).astype(low_type)
    summed = (
        lax.psum_scatter(qkv_grad, "dp", scatter_dimension=1, tiled=True),
        lax.psum_scatter(out_grad, "dp", scatter_dimension=1, tiled=True),
        lax.psum_scatter(fc_grad, "dp", scatter_dimension=0, tiled=True),
        lax.psum_scatter(proj_grad, "dp", scatter_dimension=1, tiled=True),
        lax.psum_scatter(gain_one_grad, "dp", scatter_dimension=0, tiled=True),
        lax.psum_scatter(shift_one_grad, "dp", scatter_dimension=0, tiled=True),
        lax.psum_scatter(qv_grad, "dp", scatter_dimension=1, tiled=True),
        lax.psum_scatter(out_shift_grad, "dp", scatter_dimension=0, tiled=True),
        lax.psum_scatter(gain_two_grad, "dp", scatter_dimension=0, tiled=True),
        lax.psum_scatter(shift_two_grad, "dp", scatter_dimension=0, tiled=True),
        lax.psum_scatter(fc_shift_grad, "dp", scatter_dimension=0, tiled=True),
        lax.psum_scatter(proj_shift_grad, "dp", scatter_dimension=0, tiled=True),
    )
    rest = lax.psum(
        (summed[4], summed[5], summed[6], summed[7], summed[8], summed[9], summed[10], summed[11]),
        "tensor",
    )
    out_final = lax.all_gather(summed[1], "tensor", axis=0, tiled=True)
    return (
        block_out,
        input_grad,
        rest[0],
        rest[1],
        summed[0],
        rest[2],
        out_final,
        rest[3],
        rest[4],
        rest[5],
        summed[2],
        rest[6],
        summed[3],
        rest[7],
    )


def solution(mesh):
    placed = (
        P(("dp", "tensor"), None),
        P("dp"),
        P(("dp", "tensor"), None),
        P("dp"),
        P("dp"),
        P(None, "dp", "tensor"),
        P(None, "dp"),
        P(None, "dp"),
        P("dp"),
        P("dp"),
        P("dp"),
        P("dp", "tensor"),
        P("dp"),
        P("tensor", "dp"),
        P("dp"),
    )
    return jax.shard_map(
        on_device,
        mesh=mesh,
        in_specs=placed,
        out_specs=(
            P(("dp", "tensor"), None),
            P(("dp", "tensor"), None),
            P("dp"),
            P("dp"),
            P(None, "dp", "tensor"),
            P(None, "dp"),
            P(None, "dp"),
            P("dp"),
            P("dp"),
            P("dp"),
            P("dp", "tensor"),
            P("dp"),
            P("tensor", "dp"),
            P("dp"),
        ),
        check_vma=False,
    )
```

profile of v0, /device:TPU:0, one launch (start us, length us, event | category | flops | bytes accessed | tf_op | source)
XLA Modules:
  0.0 1026.7 jit_solution(6815027488683166389)
XLA Ops:
  17.4 38.8 %all-reduce.15 = (bf16[768]{0:T(1024)(128)(2,1)S(1)}, bf16[768]{0:T(1024)(128)(2,1)S(1)}, bf16[768]{0:T(1024)(128)(2,1)S(1)}, bf16[768]{0:T(1024)(128)(2,1)S(1)}...) all-reduce(bf16[768]{0:T(1024)(128)(2,1)S(1)} %dynamic-update-slice, ...), channel_id=1, replica_groups=mesh['dp'=8,'tensor'=4] {'dp'}, use_global_device_ids=true, to_apply=%add.1 | all-reduce | flops 4608 | bytes 18432
  56.2 2.4 fusion.77
  59.5 16.2 %all-gather = bf16[8,96,2]{1,2,0:T(2,128)(2,1)S(1)} all-gather(bf16[1,96,2]{1,2,0:T(2,128)(2,1)S(1)} %convert_bitcast_fusion.1), channel_id=1, replica_groups=mesh['dp'=8,'tensor'=4] {'dp'}, dimensions={0}, use_global_device_ids=true | all-gather | bytes 3456 | tf_op jit(solution)/shard_map/all_gather | solution.py:49
  76.2 35.7 %all_gather.54 = bf16[3,768,192]{2,0,1:T(4,128)(2,1)S(1)} all-gather(bf16[3,96,192]{2,0,1:T(4,128)(2,1)S(1)} %copy.70), channel_id=1, replica_groups=mesh['dp'=8,'tensor'=4] {'dp'}, dimensions={1}, use_global_device_ids=true | all-gather | bytes 995328 | tf_op jit(solution)/shard_map/all_gather | solution.py:43
  112.8 4.3 fusion.102
  119.1 2.4 squeeze.94
  122.2 3.4 squeeze.93
  127.7 46.0 %while.30 = (s32[]{:T(128)}, bf16[4,512,192]{1,2,0:T(8,128)(2,1)S(1)}, f32[4,3,512]{2,1,0:T(4,128)S(1)}, s32[4]{0:T(128)S(1)}, bf16[2,1024,3,64]{1,3,2,0:T(8,128...) while((s32[]{:T(128)}, ...), condition=%wide.region_5.6_spmd, body=%wide.region_2.5_spmd.sunk | while | flops 422674464 | bytes 22610372 | solution.py:121
  137.0 2.1 fusion.152
  160.0 2.1 fusion.152
  175.8 5.2 fusion.88
  183.2 55.4 %reduce-scatter.16.cloned.1.call-done = f32[512,768]{1,0:T(8,128)} async-done(((f32[2048,768]{1,0:T(8,128)}), f32[512,768]{1,0:T(8,128)}) %reduce-scatter.16.cloned.1.call-update) | async-done | bytes 1572880 | tf_op jit(solution)/shard_map/reduce_scatter | solution.py:124
  243.5 26.0 %all-gather.1 = bf16[8,1,384]{2,1,0:T(2,128)(2,1)S(1)} all-gather(bf16[1,1,384]{2,1,0:T(2,128)(2,1)S(1)} %reshape.263), channel_id=1, replica_groups=mesh['dp'=8,'tensor'=4] {'dp'}, dimensions={0}, use_global_device_ids=true | all-gather | bytes 6912 | tf_op jit(solution)/shard_map/all_gather | solution.py:53
  269.6 13.0 %all-gather.16.cloned.1.call-done = bf16[768,768]{1,0:T(8,128)(2,1)} async-done(((bf16[96,768]{1,0:T(8,128)(2,1)}), bf16[768,768]{1,0:T(8,128)(2,1)}) %all-gather.16.cloned.1.call-update) | async-done | bytes 1179664 | tf_op jit(solution)/shard_map/all_gather | solution.py:45
  282.6 29.4 %all-gather.14.cloned.1.call-done = bf16[2048,768]{1,0:T(8,128)(2,1)} async-done(((bf16[512,768]{1,0:T(8,128)(2,1)}), bf16[2048,768]{1,0:T(8,128)(2,1)}) %all-gather.14.cloned.1.call-update) | async-done | bytes 3145744 | tf_op jit(solution)/shard_map/all_gather | solution.py:127
  312.0 7.5 fusion.103
  319.5 36.4 %all-gather.18.cloned.1.call-done = bf16[768,768]{0,1:T(8,128)(2,1)} async-done(((bf16[768,96]{0,1:T(8,128)(2,1)}), bf16[768,768]{0,1:T(8,128)(2,1)}) %all-gather.18.cloned.1.call-update) | async-done | bytes 1179664 | tf_op jit(solution)/shard_map/all_gather | solution.py:46
  355.9 29.0 %all-gather.20.cloned.1.call-done = bf16[2048,768]{1,0:T(8,128)(2,1)} async-done(((bf16[512,768]{1,0:T(8,128)(2,1)}), bf16[2048,768]{1,0:T(8,128)(2,1)}) %all-gather.20.cloned.1.call-update) | async-done | bytes 3145744 | tf_op jit(solution)/shard_map/all_gather | solution.py:140
  384.9 10.3 %convert_reduce_fusion = (f32[768]{0:T(1024)S(1)}, bf16[2048,768]{1,0:T(8,128)(2,1)S(1)}, bf16[2048,768]{1,0:T(8,128)(2,1)}) fusion(f32[2048,768]{1,0:T(8,128)} %fusion.103, f32[768]{0:T(1024)S(1)} %dynamic-slice_convert_fusion, bf16[2048,768]{1,0:T(8,128)(2,1)} %all-gather.20.cloned.1.call-done, bf16[768,768]{0,1:T(8,128)(2,1)} %all-gather.18.cloned.1.call-done), kind=kOutput, calls=%fused_computation.81 | convolution fusion | flops 2455239936 | bytes 16914432 | tf_op jit(solution)/shard_map/nd,fd->nf/dot_general | solution.py:142
  396.9 4.5 fusion.104
  401.5 6.6 convolution_convert_fusion
  408.3 51.6 %reduce-scatter.20.cloned.1.call-done = f32[512,768]{1,0:T(8,128)} async-done(((f32[2048,768]{1,0:T(8,128)}), f32[512,768]{1,0:T(8,128)}) %reduce-scatter.20.cloned.1.call-update) | async-done | bytes 1572880 | tf_op jit(solution)/shard_map/reduce_scatter | solution.py:152
  462.0 38.5 %reduce-scatter.18.cloned.1.call-done = bf16[512,768]{1,0:T(8,128)(2,1)} async-done(((bf16[2048,768]{1,0:T(8,128)(2,1)}), bf16[512,768]{1,0:T(8,128)(2,1)}) %reduce-scatter.18.cloned.1.call-update) | async-done | bytes 786448 | tf_op jit(solution)/shard_map/reduce_scatter | solution.py:133
  500.5 3.2 fusion.98
  506.1 28.6 %all-gather.22.cloned.1.call-done = bf16[2048,768]{1,0:T(8,128)(2,1)} async-done(((bf16[512,768]{1,0:T(8,128)(2,1)}), bf16[2048,768]{1,0:T(8,128)(2,1)}) %all-gather.22.cloned.1.call-update) | async-done | bytes 3145744 | tf_op jit(solution)/shard_map/all_gather | solution.py:157
  534.7 3.3 convolution_convert_fusion.1
  542.1 71.2 %while.31 = (s32[]{:T(128)}, f32[2,1024,3,64]{1,3,2,0:T(8,128)S(1)}, f32[2,1024,3,64]{1,3,2,0:T(8,128)}, bf16[4,512,192]{1,2,0:T(8,128)(2,1)}, s32[4]{0:T(128)S(...) while((s32[]{:T(128)}, ...), condition=%wide.region_15.16_spmd, body=%wide.region_13.15_spmd.sunk | while | flops 1032060928 | bytes 77058656 | solution.py:199
  553.1 2.5 multiply_reduce_fusion.5
  570.9 2.5 multiply_reduce_fusion.5
  588.7 2.5 multiply_reduce_fusion.5
  606.5 2.5 multiply_reduce_fusion.5
  614.7 2.4 convert_reduce_fusion.4
  618.6 4.1 convolution_bitcast_fusion.1
  629.9 4.6 fusion.83
  634.5 2.8 copy.85
  637.3 4.8 reshape.281
  642.1 7.0 convolution_bitcast_fusion
  649.4 7.0 fusion.105
  656.4 6.9 fusion.106
  665.1 14.9 %reduce-scatter.30.cloned.1.call-done = f32[96,2]{1,0:T(8,128)} async-done(((f32[768,2]{1,0:T(8,128)}), f32[96,2]{1,0:T(8,128)}) %reduce-scatter.30.cloned.1.call-update) | async-done | bytes 784
  680.8 64.2 %reduce-scatter.32.cloned.1.call-done = f32[96,192]{1,0:T(8,128)} async-done(((f32[768,192]{1,0:T(8,128)}), f32[96,192]{1,0:T(8,128)}) %reduce-scatter.32.cloned.1.call-update) | async-done | bytes 73744
  746.0 6.5 all_gather.67
  753.4 60.9 %reduce-scatter.28.cloned.1.call-done = f32[96,576]{1,0:T(8,128)} async-done(((f32[768,576]{1,0:T(8,128)}), f32[96,576]{1,0:T(8,128)}) %reduce-scatter.28.cloned.1.call-update) | async-done | bytes 221200
  816.1 58.0 %reduce-scatter.22.cloned.1.call-done = f32[512,768]{1,0:T(8,128)} async-done(((f32[2048,768]{1,0:T(8,128)}), f32[512,768]{1,0:T(8,128)}) %reduce-scatter.22.cloned.1.call-update) | async-done | bytes 1572880 | tf_op jit(solution)/shard_map/reduce_scatter | solution.py:214
  878.7 38.0 %all-reduce.13 = (f32[768]{0:T(1024)S(1)}, f32[768]{0:T(1024)S(1)}, f32[768]{0:T(1024)S(1)}, f32[768]{0:T(1024)S(1)}, f32[768]{0:T(1024)S(1)}, /*index=5*/f32[3072]{0:T(1024)S(1)}, f32[768]{0:T(1024)S(1)}) all-reduce(f32[768]{0:T(1024)S(1)} %get-tuple-element.400, ...), channel_id=6, replica_groups=mesh['dp'=8,'tensor'=4] {'dp'}, use_global_device_ids=true, to_apply=%region_20.21.clone | all-reduce | flops 7680 | bytes 61440
  917.2 6.7 all-reduce.14
  924.0 23.7 %reduce-scatter.24.cloned.1.call-done = f32[96,768]{1,0:T(8,128)} async-done(((f32[768,768]{1,0:T(8,128)}), f32[96,768]{1,0:T(8,128)}) %reduce-scatter.24.cloned.1.call-update) | async-done | bytes 294928 | tf_op jit(solution)/shard_map/reduce_scatter | solution.py:220
  947.6 72.1 %reduce-scatter.26.cloned.1.call-done = f32[768,96]{0,1:T(8,128)} async-done(((f32[768,768]{0,1:T(8,128)}), f32[768,96]{0,1:T(8,128)}) %reduce-scatter.26.cloned.1.call-update) | async-done | bytes 294928 | tf_op jit(solution)/shard_map/reduce_scatter | solution.py:221
  (333 shorter events, 127.4 us)
Async XLA Ops:
  7.2 51.5 %copy-start.22 = (f32[768,96]{0,1:T(8,128)S(1)}, f32[768,96]{0,1:T(8,128)}, u32[]{:S(2)}) copy-start(f32[768,96]{0,1:T(8,128)} %param.26) | copy-start | bytes 884740
  7.2 52.3 %copy-start.36 = (f32[2,96]{1,0:T(2,128)S(1)}, f32[2,96]{1,0:T(2,128)}, u32[]{:S(2)}) copy-start(f32[2,96]{1,0:T(2,128)} %param.25) | copy-start | bytes 2308
  7.2 68.8 %copy-start.23 = (f32[3,96,192]{2,1,0:T(8,128)S(1)}, f32[3,96,192]{2,1,0:T(8,128)}, u32[]{:S(2)}) copy-start(f32[3,96,192]{2,1,0:T(8,128)} %param.24) | copy-start | bytes 663556
  7.2 105.5 %all-gather.10.cloned.1.call-start = ((), (), s32[]{:S(2)}) async-start(), calls=%async_computation.9 | async-start | bytes 3932160 | tf_op jit(solution)/shard_map/all_gather | solution.py:77
  12.6 63.3 %copy-start.28 = (f32[512]{0:T(512)}, f32[512]{0:T(512)S(1)}, u32[]{:S(2)}) copy-start(f32[512]{0:T(512)S(1)} %broadcast_multiply_fusion.1) | copy-start | bytes 6148
  14.1 42.1 %copy-start.32 = (f32[512]{0:T(512)}, f32[512]{0:T(512)S(1)}, u32[]{:S(2)}) copy-start(f32[512]{0:T(512)S(1)} %fusion.79) | copy-start | bytes 6148
  14.1 61.8 %copy-start.30 = (f32[512]{0:T(512)}, f32[512]{0:T(512)S(1)}, u32[]{:S(2)}) copy-start(f32[512]{0:T(512)S(1)} %fusion.90) | copy-start | bytes 6148
  56.2 19.7 %copy-start.26 = (f32[768]{0:T(1024)}, f32[768]{0:T(1024)S(1)}, u32[]{:S(2)}) copy-start(f32[768]{0:T(1024)S(1)} %convert_element_type.189) | copy-start | bytes 9220
  58.6 117.2 %all-gather.12.cloned.1.call-start = ((), (), s32[]{:S(2)}) async-start(), calls=%async_computation.10 | async-start | bytes 1327104 | tf_op jit(solution)/shard_map/all_gather | solution.py:44
  59.4 179.2 %reduce-scatter.16.cloned.1.call-start = ((), (), s32[]{:S(2)}) async-start(), calls=%async_computation.11 | async-start | bytes 7864320 | tf_op jit(solution)/shard_map/reduce_scatter | solution.py:124
  112.7 4.4 copy-start.20
  125.7 2.0 copy-start.37
  173.7 7.3 copy-start.4
  173.7 7.3 copy-start.9
  175.8 5.3 copy-start.15
  181.1 57.5 %copy-start = (bf16[512,768]{1,0:T(8,128)(2,1)S(1)}, bf16[512,768]{1,0:T(8,128)(2,1)}, u32[]{:S(2)}) copy-start(bf16[512,768]{1,0:T(8,128)(2,1)} %param.19) | copy-start | bytes 2359300
  181.1 101.5 %all-gather.16.cloned.1.call-start = ((), (), s32[]{:S(2)}) async-start(), calls=%async_computation.13 | async-start | bytes 1327104 | tf_op jit(solution)/shard_map/all_gather | solution.py:45
  182.7 129.3 %all-gather.14.cloned.1.call-start = ((), (), s32[]{:S(2)}) async-start(), calls=%async_computation.12 | async-start | bytes 3932160 | tf_op jit(solution)/shard_map/all_gather | solution.py:127
  240.6 2.8 copy-start.34
  241.9 114.1 %all-gather.18.cloned.1.call-start = ((), (), s32[]{:S(2)}) async-start(), calls=%async_computation.14 | async-start | bytes 1327104 | tf_op jit(solution)/shard_map/all_gather | solution.py:46
  242.6 142.3 %all-gather.20.cloned.1.call-start = ((), (), s32[]{:S(2)}) async-start(), calls=%async_computation.16 | async-start | bytes 3932160 | tf_op jit(solution)/shard_map/all_gather | solution.py:140
  243.4 216.6 %reduce-scatter.20.cloned.1.call-start = ((), (), s32[]{:S(2)}) async-start(), calls=%async_computation.17 | async-start | bytes 7864320 | tf_op jit(solution)/shard_map/reduce_scatter | solution.py:152
  384.9 12.0 %copy-start.35 = (bf16[768,768]{1,0:T(8,128)(2,1)S(1)}, bf16[768,768]{1,0:T(8,128)(2,1)}, u32[]{:S(2)}) copy-start(bf16[768,768]{1,0:T(8,128)(2,1)} %all-gather.16.cloned.1.call-done) | copy-start | bytes 3538948
  401.4 99.1 %reduce-scatter.18.cloned.1.call-start = ((), (), s32[]{:S(2)}) async-start(), calls=%async_computation.15 | async-start | bytes 3932160 | tf_op jit(solution)/shard_map/reduce_scatter | solution.py:133
  408.1 126.6 %all-gather.22.cloned.1.call-start = ((), (), s32[]{:S(2)}) async-start(), calls=%async_computation.18 | async-start | bytes 3932160 | tf_op jit(solution)/shard_map/all_gather | solution.py:157
  462.0 42.8 %copy-start.11 = (bf16[512,768]{1,0:T(8,128)(2,1)S(1)}, bf16[512,768]{1,0:T(8,128)(2,1)}, u32[]{:S(2)}) copy-start(bf16[512,768]{1,0:T(8,128)(2,1)} %param.21) | copy-start | bytes 2359300
  506.0 173.9 %reduce-scatter.30.cloned.1.call-start = ((), (), s32[]{:S(2)}) async-start(), calls=%async_computation.23 | async-start | bytes 442368
  539.6 2.5 copy-start.5
  553.1 2.5 copy-start.3
  570.9 2.5 copy-start.3
  588.7 2.5 copy-start.3
  606.5 2.5 copy-start.3
  613.3 5.3 copy-start.16
  618.3 4.4 copy-start.13
  618.4 126.7 %reduce-scatter.32.cloned.1.call-start = ((), (), s32[]{:S(2)}) async-start(), calls=%async_computation.24 | async-start | bytes 884736
  624.0 190.3 %reduce-scatter.28.cloned.1.call-start = ((), (), s32[]{:S(2)}) async-start(), calls=%async_computation.22 | async-start | bytes 2211840
  637.3 4.9 copy-start.21
  642.1 232.1 %reduce-scatter.22.cloned.1.call-start = ((), (), s32[]{:S(2)}) async-start(), calls=%async_computation.19 | async-start | bytes 7864320 | tf_op jit(solution)/shard_map/reduce_scatter | solution.py:214
  649.1 298.5 %reduce-scatter.24.cloned.1.call-start = ((), (), s32[]{:S(2)}) async-start(), calls=%async_computation.20 | async-start | bytes 2654208 | tf_op jit(solution)/shard_map/reduce_scatter | solution.py:220
  656.4 363.3 %reduce-scatter.26.cloned.1.call-start = ((), (), s32[]{:S(2)}) async-start(), calls=%async_computation.21 | async-start | bytes 2654208 | tf_op jit(solution)/shard_map/reduce_scatter | solution.py:221
  663.4 210.7 %copy-start.1 = (bf16[512,768]{1,0:T(8,128)(2,1)S(1)}, bf16[512,768]{1,0:T(8,128)(2,1)}, u32[]{:S(2)}) copy-start(bf16[512,768]{1,0:T(8,128)(2,1)} %param.19) | copy-start | bytes 2359300
  663.4 210.7 %copy-start.27 = (f32[768]{0:T(1024)S(1)}, f32[768]{0:T(1024)}, u32[]{:S(2)}) copy-start(f32[768]{0:T(1024)} %copy-done.26) | copy-start | bytes 9220
  663.4 210.7 %copy-start.29 = (f32[512]{0:T(512)S(1)}, f32[512]{0:T(512)}, u32[]{:S(2)}) copy-start(f32[512]{0:T(512)} %copy-done.28) | copy-start | bytes 6148
  746.0 130.2 %copy-start.33 = (f32[512]{0:T(512)S(1)}, f32[512]{0:T(512)}, u32[]{:S(2)}) copy-start(f32[512]{0:T(512)} %copy-done.32) | copy-start | bytes 6148
  746.0 130.2 %copy-start.31 = (f32[512]{0:T(512)S(1)}, f32[512]{0:T(512)}, u32[]{:S(2)}) copy-start(f32[512]{0:T(512)} %copy-done.30) | copy-start | bytes 6148
  816.1 60.9 %copy-start.12 = (bf16[512,768]{1,0:T(8,128)(2,1)S(1)}, bf16[512,768]{1,0:T(8,128)(2,1)}, u32[]{:S(2)}) copy-start(bf16[512,768]{1,0:T(8,128)(2,1)} %param.21) | copy-start | bytes 2359300
  874.1 2.1 copy-start.6
  874.1 2.9 copy-start.8
  (19 other events, 29.0 us)
Sparse Core Ops, SparseCore 0:
  58.7 25.8 all-gather.9
  87.3 43.2 all-gather.11
  181.2 57.3 reduce-scatter.15
  241.5 41.0 all-gather.15
  284.7 27.2 all-gather.13
  314.8 41.0 all-gather.17
  357.6 27.2 all-gather.19
  401.5 58.3 reduce-scatter.19
  462.5 37.9 reduce-scatter.17
  506.2 28.5 all-gather.21
  618.5 61.4 reduce-scatter.29
  683.4 61.5 reduce-scatter.31
  748.5 65.7 reduce-scatter.27
  816.8 57.2 reduce-scatter.21
  878.0 69.5 reduce-scatter.23
  951.5 68.1 reduce-scatter.25
where the time goes:
time: 1030 us
  waiting for transfers between devices  577 us (56%)
  blocking collectives  168 us (16%)
  matrix products  114 us (11%)
  local copies, waits for them, and re-layouts  63.9 us (6%)
  other arithmetic  53.3 us (5%)
  loops' own time  31.9 us (3%)
  between operations  17.1 us (2%)
    unnamed x19, waiting for transfers between devices  141 us
    unnamed x2, blocking collectives  76.8 us
    reduce_scatter x1, waiting for transfers between devices, on_device(): lax.psum_scatter(proj_grad, 'dp', scatter_dimension=1, tiled=True)  72.1 us
    reduce_scatter x1, waiting for transfers between devices, on_device(): lax.psum_scatter(normed_one_part, 'tensor', scatter_dimension=0, tiled=True)  58 us
    reduce_scatter x1, waiting for transfers between devices, on_device(): lax.psum_scatter(partial_out, 'tensor', scatter_dimension=0, tiled=True)  55.4 us
    reduce_scatter x1, waiting for transfers between devices, on_device(): lax.psum_scatter(normed_two_part, 'tensor', scatter_dimension=0, tiled=True)  51.6 us
    reduce_scatter x1, waiting for transfers between devices, on_device(): lax.psum_scatter(partial_mlp.astype(jnp.bfloat16), 'tensor', scatter_dime...  38.5 us
    all_gather x1, waiting for transfers between devices, on_device(): lax.all_gather(proj_weight.astype(low_type), 'dp', axis=1, tiled=True)  36.4 us
  transfers between devices with their start and end apart: 16, of which 14 were waited for; matrix products, arithmetic and copies ran while one was open for 12% of the time, Pallas kernels for 0%

commit v1 on v0

v1 whole, which is shorter than its diff:
```python
import functools
import math

import jax
import jax.numpy as jnp
from jax import lax
from jax.experimental import pallas as pl
from jax.experimental.pallas import tpu as pltpu
from jax.sharding import PartitionSpec as P

MESH = pl.DeviceIdType.MESH
LOW, FULL = jnp.bfloat16, jnp.float32
EPSILON = 1e-05
HD = 64
GROUPS, ZN, XN = 8, 4, 2
SEMS = 120
VEC = 16

GAIN1, SHIFT1, OUTB, GAIN2, SHIFT2, PROJB, QKVB, FCB = 0, 1, 2, 3, 4, 5, 6, 8


def dot(a, b):
    return jnp.dot(a, b, preferred_element_type=FULL)


def dot_nt(a, b):
    return lax.dot_general(a, b, (((1,), (1,)), ((), ())), preferred_element_type=FULL)


def dot_tn(a, b):
    return lax.dot_general(a, b, (((0,), (0,)), ((), ())), preferred_element_type=FULL)


def block_kernel(repeat, seq_len, *refs):
    (
        tok_h, cot_h, vec_h, wq_h, wo_h, wf_h, wp_h, prefix_s,
        bo_ref, ig_ref, gq_ref, go_ref, gf_ref, gp_ref, vo_ref,
        Wq, Wo, Wf, Wp, Go, Gp,
        RqA1, RqB1, RqA2, RqB2, Rq3,
        RfA1, RfB1, RfA2, RfB2, Rf3,
        RpA1, RpB1, RpA2, RpB2, Rp3,
        Ro1, Ro2, Ro3,
        TOK, COT, N1F, N2F, RS1, RS2, N1, N2, T0, T1,
        QP, KP, VP, CTX, DO, DQ, LSEC, LSER, DELR,
        MID, S0, V0, V1, H, GPR, PG,
        VR, VF, VG, VX, VR1, VR2,
        ss, rs, ls,
    ) = refs
    half = seq_len // 2
    width = TOK.shape[1]
    rblk = 256
    nrb = seq_len // rblk
    dp = lax.axis_index("dp")
    t = lax.axis_index("tensor")
    s, sub = dp // repeat, dp % repeat
    z, x = s // XN, s % XN
    y, c = t // 2, t % 2
    oy, oc, ox = 1 - y, 1 - c, 1 - x

    def at(zz, xx, tt):
        return ((zz * XN + xx) * repeat + sub, tt)

    def zdev(k):
        return at((z + k) % ZN, x, t)

    xdev = at(z, ox, t)
    ydev = at(z, x, oy * 2 + c)
    cdev = at(z, x, y * 2 + oc)
    gdev = at(z, x, oy * 2 + oc)
    others = [(((s + k) % GROUPS) * repeat + sub, t) for k in range(1, GROUPS)]

    made = []

    def copy(src, dst, dev):
        k = len(made)

        def make():
            return pltpu.make_async_remote_copy(
                src_ref=src, dst_ref=dst, send_sem=ss.at[k], recv_sem=rs.at[k],
                device_id=dev, device_id_type=MESH,
            )

        made.append(make)
        return make

    def start(makes):
        for m in makes:
            m().start()

    def landed(makes):
        for m in makes:
            m().wait_recv()

    def sent(makes):
        for m in makes:
            m().wait_send()

    barrier = pltpu.get_barrier_semaphore()
    peers = others + [cdev, ydev, gdev]
    for d in peers:
        pl.semaphore_signal(barrier, inc=1, device_id=d, device_id_type=MESH)

    local = [
        pltpu.make_async_copy(vec_h, VR.at[s], ls.at[0]),
        pltpu.make_async_copy(wo_h, Wo.at[z, x, y], ls.at[1]),
        pltpu.make_async_copy(wq_h, Wq.at[y, z, x], ls.at[2]),
        pltpu.make_async_copy(tok_h, TOK, ls.at[3]),
        pltpu.make_async_copy(cot_h, COT.at[c], ls.at[4]),
        pltpu.make_async_copy(wf_h, Wf.at[y, z, x], ls.at[5]),
        pltpu.make_async_copy(wp_h, Wp.at[y, z, x], ls.at[6]),
    ]
    for cp in local:
        cp.start()
    pl.semaphore_wait(barrier, len(peers))

    vec_c = [copy(VR.at[s], VR.at[s], d) for d in others]
    cot_c = [copy(COT.at[c], COT.at[c], cdev)]
    hr = wq_h.shape[0] // 2
    halves = (pl.ds(0, hr), pl.ds(hr, hr))

    def gather(W):
        zs = [[copy(W.at[y, z, x, r], W.at[y, z, x, r], zdev(k)) for k in range(1, ZN)] for r in halves]
        a, b = halves
        one = [
            [copy(W.at[y, :, x, a], W.at[y, :, x, a], xdev)],
            [copy(W.at[y, :, x, b], W.at[y, :, x, b], ydev)],
        ]
        two = [
            [copy(W.at[y, :, :, a], W.at[y, :, :, a], ydev)],
            [copy(W.at[:, :, x, b], W.at[:, :, x, b], xdev)],
        ]
        return zs, one, two

    ow = [
        [copy(Wo.at[z, x, y], Wo.at[z, x, y], xdev)],
        [copy(Wo.at[z, :, y], Wo.at[z, :, y], ydev)],
        [copy(Wo.at[z], Wo.at[z], zdev(k)) for k in range(1, ZN)],
    ]
    qw, pw, fw = gather(Wq), gather(Wp), gather(Wf)

    def z_go(w):
        for h in range(2):
            start(w[0][h])

    def one_go(w):
        for h in range(2):
            landed(w[0][h])
            start(w[1][h])

    def two_go(w):
        for h in range(2):
            landed(w[1][h])
            start(w[2][h])

    def all_in(w):
        for h in range(2):
            landed(w[2][h])

    local[0].wait()
    start(vec_c)
    local[1].wait()
    start(ow[0])
    local[2].wait()
    z_go(qw)
    local[4].wait()
    start(cot_c)
    local[3].wait()

    def row_tile(i, n=128):
        return pl.ds(pl.multiple_of(i * n, n), n)

    @pl.loop(0, half // 128)
    def _(i):
        r = row_tile(i)
        v = TOK[r, :].astype(FULL)
        v = v - jnp.mean(v, axis=-1, keepdims=True)
        rstd = lax.rsqrt(jnp.mean(v * v, axis=-1, keepdims=True) + EPSILON)
        N1F[r, :] = v * rstd
        RS1[r, :] = jnp.broadcast_to(rstd, (128, 128))

    local[5].wait()
    local[6].wait()
    landed(vec_c)
    vf = VR[0].astype(FULL)
    for g in range(1, GROUPS):
        vf = vf + VR[g].astype(FULL)
    VF[...] = vf
    VG[...] = jnp.zeros(VG.shape, FULL)

    def vrow(i):
        return VF[i : i + 1, :]

    @pl.loop(0, half // 128)
    def _(i):
        r = row_tile(i)
        N1[c, r, :] = (N1F[r, :] * vrow(GAIN1) + vrow(SHIFT1)).astype(LOW)

    n1_c = [copy(N1.at[c], N1.at[c], cdev)]
    start(n1_c)
    landed(ow[0])
    start(ow[1])
    landed(cot_c)

    def transpose_all(source, target):
        @pl.loop(0, nrb)
        def _(i):
            h, off = i // (half // rblk), i % (half // rblk)
            rows = pl.ds(pl.multiple_of(off * rblk, rblk), rblk)
            cols = pl.ds(pl.multiple_of(i * rblk, rblk), rblk)
            for k in range(width // rblk):
                target[k * rblk : (k + 1) * rblk, cols] = source[h, rows, k * rblk : (k + 1) * rblk].T

    transpose_all(COT, T0)
    one_go(qw)
    z_go(fw)
    two_go(qw)
    landed(n1_c)
    landed(ow[1])
    one_go(fw)
    z_go(pw)
    all_in(qw)

    def low_lanes(v):
        return lax.broadcasted_iota(jnp.int32, v.shape, 1) < HD

    def tile(v, i):
        return v[:, i * 128 : (i + 1) * 128]

    def roll(v):
        return pltpu.roll(v, HD, 1)

    @pl.loop(0, nrb)
    def _(i):
        h, off = i // (half // rblk), i % (half // rblk)
        rows = pl.ds(pl.multiple_of(off * rblk, rblk), rblk)
        out = pl.ds(pl.multiple_of(i * rblk, rblk), rblk)
        n = N1[h, rows, :]
        got = []
        for b in range(2):
            got.append(dot(n, Wq[b].reshape(width, Wq.shape[-1])) + VF[QKVB + b : QKVB + b + 1, : Wq.shape[-1]])
            QP[b, out, :] = (tile(got[b], 0).astype(LOW).astype(FULL) * 0.125).astype(LOW)
            KP[b, out, :] = tile(got[b], 1).astype(LOW)
            VP[b, out, :] = tile(got[b], 2).astype(LOW)
        first = low_lanes(tile(got[0], 3))
        q = jnp.where(first, tile(got[0], 3), roll(tile(got[1], 3)))
        QP[2, out, :] = (q.astype(LOW).astype(FULL) * 0.125).astype(LOW)
        KP[2, out, :] = jnp.where(first, roll(tile(got[0], 3)), tile(got[1], 3)).astype(LOW)
        VP[2, out, :] = jnp.where(first, tile(got[0], 4), roll(tile(got[1], 4))).astype(LOW)

    prefix = prefix_s[y]
    LSEC[...] = jnp.zeros(LSEC.shape, FULL)

    def lane_part(v, e):
        lane = lax.broadcasted_iota(jnp.int32, v.shape, 1)
        keep = lane < HD if e == 0 else lane >= HD
        return jnp.where(keep, v, jnp.zeros_like(v))

    @pl.loop(0, 3)
    def _(p):
        for b in range(nrb):
            rows = pl.ds(b * rblk, rblk)
            cols = max(half, (b + 1) * rblk)
            q = QP[p, rows, :]
            keys, values = KP[p, :cols, :], VP[p, :cols, :]
            query = b * rblk + lax.broadcasted_iota(jnp.int32, (rblk, 1), 0)
            limit = jnp.maximum(prefix - 1, query)
            key = lax.broadcasted_iota(jnp.int32, (rblk, cols), 1)
            parts = []
            for e in range(2):
                sc = dot_nt(lane_part(q, e), keys)
                sc = jnp.where(key <= limit, sc, -1e30)
                peak = jnp.max(sc, axis=-1, keepdims=True)
                w = jnp.exp(sc - peak)
                total = jnp.sum(w, axis=-1, keepdims=True)
                parts.append(dot(w.astype(LOW), values) * (1.0 / total))
                lane = lax.broadcasted_iota(jnp.int32, (rblk, 128), 1)
                LSEC[rows, :] = jnp.where(lane == 2 * p + e, peak + jnp.log(total), LSEC[rows, :])
            CTX[p, rows, :] = jnp.where(low_lanes(parts[0]), parts[0], parts[1]).astype(LOW)

        @pl.when(p == 0)
        def _():
            two_go(fw)

        @pl.when(p == 1)
        def _():
            one_go(pw)

    start(ow[2])
    two_go(pw)
    for b in range(nrb):
        lt = LSEC[b * rblk : (b + 1) * rblk, :].T
        for h in range(6):
            LSER[h, :, b * rblk : (b + 1) * rblk] = lt[h : h + 1, :]
    landed(ow[2])

    def wide(ref, rows):
        return jnp.concatenate([ref[0, rows, :], ref[1, rows, :], ref[2, rows, :]], axis=1)

    def split_rows(make_block, away, home, copies):
        per = half // rblk
        for which, target in ((oc, away), (c, home)):

            @pl.loop(0, per)
            def _(j):
                rows = pl.ds(pl.multiple_of(j * rblk, rblk), rblk)
                flat = pl.ds(pl.multiple_of((which * per + j) * rblk, rblk), rblk)
                target[rows, :] = make_block(which, rows, flat)

            if target is away:
                start(copies)

    po_c = [copy(S0, V0, cdev)]
    split_rows(
        lambda h, rows, flat: dot_nt(wide(CTX, flat), Wo[...].reshape(width, Wo.shape[-1])), S0, MID, po_c
    )
    landed(po_c)

    @pl.loop(0, half // 128)
    def _(i):
        r = row_tile(i)
        m = TOK[r, :].astype(FULL) + (MID[r, :] + V0[r, :] + vrow(OUTB))
        MID[r, :] = m
        v = m - jnp.mean(m, axis=-1, keepdims=True)
        rstd = lax.rsqrt(jnp.mean(v * v, axis=-1, keepdims=True) + EPSILON)
        n = v * rstd
        N2F[r, :] = n
        RS2[r, :] = jnp.broadcast_to(rstd, (128, 128))
        N2[c, r, :] = (n * vrow(GAIN2) + vrow(SHIFT2)).astype(LOW)

    n2_c = [copy(N2.at[c], N2.at[c], cdev)]
    start(n2_c)
    landed(n2_c)
    all_in(fw)

    root = math.sqrt(2.0 / math.pi)

    @pl.loop(0, nrb * 2)
    def _(k):
        b, i = k // nrb, k % nrb
        h, off = i // (half // rblk), i % (half // rblk)
        rows = pl.ds(pl.multiple_of(off * rblk, rblk), rblk)
        flat = pl.ds(pl.multiple_of(i * rblk, rblk), rblk)
        u = dot(N2[h, rows, :], Wf[b].reshape(width, width)) + VF[pl.ds(FCB + b, 1), :]
        uu = u * u
        th = jnp.tanh(root * u * (1.0 + 0.044715 * uu))
        H[b, flat, :] = (0.5 * u * (1.0 + th)).astype(LOW)
        GPR[b, flat, :] = 0.5 * (1.0 + th) + (0.5 * root) * u * (1.0 - th * th) * (1.0 + 0.134145 * uu)

    def weight_grad(left_t, right, G, columns):
        @pl.loop(0, 4)
        def _(k):
            b, m = k // 2, k % 2
            rows = pl.ds(pl.multiple_of(m * (width // 2), width // 2), width // 2)
            g = dot(left_t[rows, :], right[b, :, :columns])
            g = g.astype(LOW).reshape(ZN // 2, XN, width // GROUPS, columns)
            G[b, pl.ds(m * (ZN // 2), ZN // 2), :, :, :columns] = g

    def reduce_copies(G, cols, A1, B1, A2, B2, R3):
        a, b = halves
        one = [
            [copy(G.at[:, :, ox, a, cols], A1, xdev)],
            [copy(G.at[oy, :, :, b, cols], B1, ydev)],
        ]
        two = [
            [copy(G.at[oy, :, x, a, cols], A2, ydev)],
            [copy(G.at[y, :, ox, b, cols], B2, xdev)],
        ]
        three = [
            [copy(G.at[y, (z + k) % ZN, x, r, cols], R3.at[k - 1, r], zdev(k)) for k in range(1, ZN)]
            for r in halves
        ]

        def add(target, source):
            target[...] = (target[...].astype(FULL) + source[...].astype(FULL)).astype(LOW)

        def go():
            start(one[0])
            start(one[1])

        def second():
            landed(one[0])

            @pl.loop(0, ZN)
            def _(k):
                add(G.at[oy, k, x, a, cols], A1.at[oy, k])

            start(two[0])
            landed(one[1])

            @pl.loop(0, ZN)
            def _(k):
                add(G.at[y, k, ox, b, cols], B1.at[k, ox])

            start(two[1])

            @pl.loop(0, ZN)
            def _(k):
                add(G.at[y, k, x, a, cols], A1.at[y, k])
                add(G.at[y, k, x, b, cols], B1.at[k, x])

        def third():
            for h, R in ((0, A2), (1, B2)):
                landed(two[h])

                @pl.loop(0, ZN)
                def _(k):
                    add(G.at[y, k, x, halves[h], cols], R.at[k])

                start(three[h])

        def last(out):
            for h in range(2):
                landed(three[h])
                r = halves[h]
                v = G[y, z, x, r, cols].astype(FULL)
                for k in range(ZN - 1):
                    v = v + R3[k, r, :].astype(FULL)
                out[r, :] = v

        return go, second, third, last

    every = pl.ds(0, width)
    rp = reduce_copies(Gp, every, RpA1, RpB1, RpA2, RpB2, Rp3)
    weight_grad(T0, H, Gp, width)
    rp[0]()
    transpose_all(N2, T1)
    all_in(pw)

    @pl.loop(0, nrb * 2)
    def _(k):
        b, i = k // nrb, k % nrb
        h, off = i // (half // rblk), i % (half // rblk)
        rows = pl.ds(pl.multiple_of(off * rblk, rblk), rblk)
        flat = pl.ds(pl.multiple_of(i * rblk, rblk), rblk)
        g = (dot(COT[h, rows, :], Wp[b].reshape(width, width)) * GPR[b, flat, :]).astype(LOW)
        PG[b, flat, :] = g
        VG[pl.ds(FCB + b, 1), :] += jnp.sum(g.astype(FULL), axis=0, keepdims=True)

    p2_c = [copy(S0, V1, cdev)]
    home2, homem, home1 = GPR.at[0, pl.ds(0, half)], GPR.at[0, pl.ds(half, half)], GPR.at[1, pl.ds(0, half)]
    awaym = GPR.at[1, pl.ds(half, half)]

    def pair_nt(A, W, columns):
        def block(h, rows, flat):
            return dot_nt(A[0, flat, :columns], W[0].reshape(width, W.shape[-1])) + dot_nt(
                A[1, flat, :columns], W[1].reshape(width, W.shape[-1])
            )

        return block

    sent(po_c)
    split_rows(pair_nt(PG, Wf, width), S0, home2, p2_c)
    pm_c = [copy(awaym, V0, cdev)]
    split_rows(pair_nt(H, Wp, width), awaym, homem, pm_c)
    for group in pw[0] + pw[1] + pw[2]:
        sent(group)
    weight_grad(T1, PG, Wp, width)
    rf = reduce_copies(Wp, every, RfA1, RfB1, RfA2, RfB2, Rf3)
    rf[0]()
    landed(p2_c)

    sent(n2_c)

    def norm_back(dy, n, rstd, gain):
        e = dy * gain
        return (e - jnp.mean(e, axis=-1, keepdims=True) - n * jnp.mean(e * n, axis=-1, keepdims=True)) * rstd

    def add_row(i, v):
        VG[i : i + 1, :] += jnp.sum(v, axis=0, keepdims=True)

    @pl.loop(0, half // 128)
    def _(i):
        r = row_tile(i)
        dy = GPR[0, r, :] + V1[r, :]
        n = N2F[r, :]
        add_row(GAIN2, dy * n)
        add_row(SHIFT2, dy)
        cot = COT[c, r, :].astype(FULL)
        add_row(PROJB, cot)
        g = cot + norm_back(dy, n, RS2[r, 0:1], vrow(GAIN2))
        N2F[r, :] = g
        low = g.astype(LOW)
        add_row(OUTB, low.astype(FULL))
        N2[c, r, :] = low

    ag_c = [copy(N2.at[c], N2.at[c], cdev)]
    start(ag_c)
    rp[1]()
    landed(pm_c)

    @pl.loop(0, half // 128)
    def _(i):
        r = row_tile(i)
        far = row_tile(i + half // 128)
        bo_ref[r, :] = (MID[r, :] + (GPR[0, far, :] + V0[r, :] + vrow(PROJB))).astype(LOW)

    landed(ag_c)

    @pl.loop(0, nrb)
    def _(i):
        h, off = i // (half // rblk), i % (half // rblk)
        rows = pl.ds(pl.multiple_of(off * rblk, rblk), rblk)
        flat = pl.ds(pl.multiple_of(i * rblk, rblk), rblk)
        g = dot(N2[h, rows, :], Wo[...].reshape(width, Wo.shape[-1])).astype(LOW)
        row = lax.broadcasted_iota(jnp.int32, (8, 128), 0)
        lane = lax.broadcasted_iota(jnp.int32, (8, 128), 1)
        pick = jnp.where(lane // HD == row, 1.0, 0.0).astype(LOW)
        for p in range(3):
            gp = tile(g, p)
            DO[p, flat, :] = gp
            prod = gp.astype(FULL) * CTX[p, flat, :].astype(FULL)
            high = prod.astype(LOW)
            rest = (prod - high.astype(FULL)).astype(LOW)
            d = dot_nt(pick, high) + dot_nt(pick, rest)
            for e in range(2):
                DELR[2 * p + e, :, flat] = d[e : e + 1, :]

    transpose_all(N2, T0)

    @pl.loop(0, 2)
    def _(m):
        rows = pl.ds(pl.multiple_of(m * (width // 2), width // 2), width // 2)
        g = dot(T0[rows, :], wide(CTX, pl.ds(0, seq_len)))
        g = g.astype(LOW).reshape(ZN // 2, XN, 2, width // (2 * GROUPS), Wo.shape[-1])
        Go[pl.ds(m * (ZN // 2), ZN // 2)] = g

    ro = [
        [copy(Go.at[(z + k) % ZN], Ro1.at[k - 1], zdev(k)) for k in range(1, ZN)],
        [copy(Go.at[z, :, oy], Ro2, ydev)],
        [copy(Go.at[z, ox, y], Ro3, xdev)],
        [copy(go_ref.at[t], go_ref.at[t], d) for d in (cdev, ydev, gdev)],
    ]
    start(ro[0])

    @pl.loop(0, 3)
    def _(p):
        DQ[...] = jnp.zeros(DQ.shape, FULL)
        for b in range(nrb):
            rows = pl.ds(b * rblk, rblk)
            first = 0 if b * rblk < half else b * rblk
            n = seq_len - first
            keys, values = KP[p, rows, :], VP[p, rows, :]
            queries, grads = QP[p, first:, :], DO[p, first:, :]
            key = b * rblk + lax.broadcasted_iota(jnp.int32, (rblk, 1), 0)
            limit = jnp.where(key < prefix, 0, key)
            query = first + lax.broadcasted_iota(jnp.int32, (rblk, n), 1)
            dk, dv = [], []
            for e in range(2):
                ke, ve = lane_part(keys, e), lane_part(values, e)
                sc = dot_nt(ke, queries) - LSER[2 * p + e, :, first:]
                w = jnp.exp(jnp.where(query >= limit, sc, -1e30))
                dw = dot_nt(ve, grads) - DELR[2 * p + e, :, first:]
                ds = (w * dw).astype(LOW)
                dv.append(dot(w.astype(LOW), grads))
                dk.append(dot(ds, queries))
                DQ[first:, :] += dot_tn(ds, ke)
            KP[p, rows, :] = jnp.where(low_lanes(dk[0]), dk[0], dk[1]).astype(LOW)
            VP[p, rows, :] = jnp.where(low_lanes(dv[0]), dv[0], dv[1]).astype(LOW)
        QP[p, :, :] = (DQ[...] * 0.125).astype(LOW)

        @pl.when(p == 0)
        def _():
            rf[1]()
            rp[2]()

        @pl.when(p == 1)
        def _():
            rf[2]()

    landed(ro[0])
    for i in range(2):
        for j in range(2):
            v = Go[z, i, j].astype(FULL)
            for k in range(ZN - 1):
                v = v + Ro1[k, i, j].astype(FULL)
            Go[z, i, j] = v.astype(LOW)
    start(ro[1])

    @pl.loop(0, nrb)
    def _(i):
        flat = pl.ds(pl.multiple_of(i * rblk, rblk), rblk)
        for b in range(2):
            for k, ref in enumerate((QP, KP, VP)):
                H[b, flat, k * 128 : (k + 1) * 128] = ref[b, flat, :]
        q, k, v = (ref[2, flat, :].astype(FULL) for ref in (QP, KP, VP))
        first = low_lanes(q)
        H[0, flat, 384:512] = jnp.where(first, q, roll(k)).astype(LOW)
        H[1, flat, 384:512] = jnp.where(first, roll(q), k).astype(LOW)
        H[0, flat, 512:640] = jnp.where(first, v, 0.0).astype(LOW)
        H[1, flat, 512:640] = jnp.where(first, roll(v), 0.0).astype(LOW)
        for b in range(2):
            VG[QKVB + b : QKVB + b + 1, : Wq.shape[-1]] += jnp.sum(
                H[b, flat, : Wq.shape[-1]].astype(FULL), axis=0, keepdims=True
            )

    packed = Wq.shape[-1]
    for group in fw[0] + fw[1] + fw[2]:
        sent(group)
    transpose_all(N1, T1)
    weight_grad(T1, H, Wf, packed)
    rq = reduce_copies(Wf, pl.ds(0, packed), RqA1, RqB1, RqA2, RqB2, Rq3)
    rq[0]()
    p1_c = [copy(S0, V1, cdev)]
    sent(p2_c)
    split_rows(pair_nt(H, Wq, packed), S0, home1, p1_c)
    landed(ro[1])
    for i in range(2):
        Go[z, i, y] = (Go[z, i, y].astype(FULL) + Ro2[i].astype(FULL)).astype(LOW)
    start(ro[2])
    rp[3](gp_ref)
    landed(p1_c)

    @pl.loop(0, half // 128)
    def _(i):
        r = row_tile(i)
        dy = GPR[1, r, :] + V1[r, :]
        n = N1F[r, :]
        add_row(GAIN1, dy * n)
        add_row(SHIFT1, dy)
        ig_ref[r, :] = (N2F[r, :] + norm_back(dy, n, RS1[r, 0:1], vrow(GAIN1))).astype(LOW)

    hv = VEC // 2
    VX[...] = VG[...].reshape(2, hv, width)
    v_c = [copy(VX.at[oy], VR1, ydev)]
    start(v_c)
    rq[1]()
    landed(ro[2])
    go_ref[t] = Go[z, x, y].astype(FULL) + Ro3[...].astype(FULL)
    start(ro[3])
    landed(v_c)
    VR2[s] = VX[y] + VR1[...]
    v2_c = [copy(VR2.at[s], VR2.at[s], d) for d in others]
    start(v2_c)
    rf[3](gf_ref)
    landed(v2_c)
    total = VR2[0]
    for g in range(1, GROUPS):
        total = total + VR2[g]
    vo_ref[t] = total
    v3_c = [copy(vo_ref.at[t], vo_ref.at[t], d) for d in (cdev, ydev, gdev)]
    start(v3_c)
    rq[2]()
    landed(v3_c)
    landed(ro[3])
    rq[3](gq_ref)

    waited = {id(m) for m in po_c + n2_c + p2_c}
    for w in (pw, fw):
        for part in w:
            for group in part:
                waited |= {id(m) for m in group}
    sent([m for m in made if id(m) not in waited])


def gather_groups(v, axis, repeat, groups):
    if repeat == 1:
        return v
    return lax.all_gather(v, "dp", axis=axis, axis_index_groups=groups, tiled=True)


def scatter_groups(v, axis, repeat, groups):
    if repeat == 1:
        return v
    return lax.psum_scatter(v, "dp", scatter_dimension=axis, axis_index_groups=groups, tiled=True)


def on_device(
    dp_size,
    tokens,
    prefix,
    cotangent,
    first_gain,
    first_shift,
    qkv_weight,
    qv_bias,
    out_weight,
    out_bias,
    second_gain,
    second_shift,
    fc_weight,
    fc_bias,
    proj_weight,
    proj_bias,
):
    repeat = dp_size // GROUPS
    groups = [[g * repeat + i for i in range(repeat)] for g in range(GROUPS)]
    half, width = tokens.shape
    seq_len = 2 * half
    s = lax.axis_index("dp") // repeat
    t = lax.axis_index("tensor")
    y, c = t // 2, t % 2

    def whole(v, axis):
        return gather_groups(v.astype(LOW), axis, repeat, groups)

    wq, wo, wf, wp = whole(qkv_weight, 1), whole(out_weight, 1), whole(fc_weight, 0), whole(proj_weight, 1)
    rows = wf.shape[0]
    cols = wq.shape[2]
    pair = 2 * HD
    zero = jnp.zeros((rows, HD), LOW)
    wq = jnp.concatenate(
        [wq[0, :, :pair], wq[1, :, :pair], wq[2, :, :pair], wq[0, :, pair:], wq[1, :, pair:], wq[2, :, pair:], zero],
        axis=1,
    )
    low_rows = lax.dynamic_slice_in_dim(wo, c * cols, cols, 0)
    high_rows = lax.dynamic_slice_in_dim(wo, (2 + c) * cols, cols, 0)
    wo = jnp.concatenate([low_rows[:pair], high_rows[:pair], low_rows[pair:], high_rows[pair:]], axis=0)
    wo = lax.dynamic_slice_in_dim(wo, y * (rows // 2), rows // 2, 1).T
    wp = wp.T

    def spread(v):
        return lax.dynamic_update_slice_in_dim(jnp.zeros((v.shape[0] * GROUPS,), LOW), v, s * v.shape[0], 0)

    vectors = [spread(whole(v, 0)) for v in (first_gain, first_shift, out_bias, second_gain, second_shift, proj_bias)]
    qb = whole(qv_bias, 1)
    qb = [spread(qb[0]), spread(qb[1])]
    fb = spread(whole(fc_bias, 0)).reshape(4, width)
    fill = jnp.zeros((pair,), LOW)
    for b in range(2):
        q, v = (lax.dynamic_slice_in_dim(r, (2 * b + c) * cols, cols, 0) for r in qb)
        vectors.append(jnp.concatenate([q[:pair], fill, v[:pair], q[pair:], fill[:HD], v[pair:], fill[:HD], fill]))
    for b in range(2):
        vectors.append(lax.dynamic_index_in_dim(fb, 2 * b + c, 0, keepdims=False))
    vec = jnp.stack(vectors + [jnp.zeros((width,), LOW)] * (VEC - len(vectors)))

    packed, own = wq.shape[1], wo.shape[1]
    hr = rows // 2
    ANY = pl.BlockSpec(memory_space=pl.ANY)
    IN_VMEM = pl.BlockSpec(memory_space=pltpu.VMEM)

    def reduce_space(lanes):
        return [
            pltpu.VMEM((2, ZN, hr, lanes), LOW),
            pltpu.VMEM((ZN, XN, hr, lanes), LOW),
            pltpu.VMEM((ZN, hr, lanes), LOW),
            pltpu.VMEM((ZN, hr, lanes), LOW),
            pltpu.VMEM((ZN - 1, rows, lanes), LOW),
        ]

    token_low = pltpu.VMEM((2, half, width), LOW)
    token_full = pltpu.VMEM((half, width), FULL)
    units = pltpu.VMEM((2, seq_len, width), LOW)
    heads = pltpu.VMEM((3, seq_len, pair), LOW)
    scratch = (
        [
            pltpu.VMEM((2, ZN, XN, rows, packed), LOW),
            pltpu.VMEM((ZN, XN, 2, hr, own), LOW),
            pltpu.VMEM((2, ZN, XN, rows, width), LOW),
            pltpu.VMEM((2, ZN, XN, rows, width), LOW),
            pltpu.VMEM((ZN, XN, 2, hr, own), LOW),
            pltpu.VMEM((2, ZN, XN, rows, width), LOW),
        ]
        + reduce_space(packed)
        + reduce_space(width)
        + reduce_space(width)
        + [
            pltpu.VMEM((ZN - 1, XN, 2, hr, own), LOW),
            pltpu.VMEM((XN, hr, own), LOW),
            pltpu.VMEM((hr, own), LOW),
        ]
        + [
            pltpu.VMEM((half, width), LOW),
            token_low,
            token_full,
            token_full,
            pltpu.VMEM((half, 128), FULL),
            pltpu.VMEM((half, 128), FULL),
            token_low,
            token_low,
            pltpu.VMEM((width, seq_len), LOW),
            pltpu.VMEM((width, seq_len), LOW),
        ]
        + [heads] * 5
        + [
            pltpu.VMEM((seq_len, pair), FULL),
            pltpu.VMEM((seq_len, 128), FULL),
            pltpu.VMEM((6, 1, seq_len), FULL),
            pltpu.VMEM((6, 1, seq_len), FULL),
        ]
        + [token_full] * 4
        + [units, pltpu.VMEM((2, seq_len, width), FULL), units]
        + [
            pltpu.VMEM((GROUPS, VEC, width), LOW),
            pltpu.VMEM((VEC, width), FULL),
            pltpu.VMEM((VEC, width), FULL),
            pltpu.VMEM((2, VEC // 2, width), FULL),
            pltpu.VMEM((VEC // 2, width), FULL),
            pltpu.VMEM((GROUPS, VEC // 2, width), FULL),
        ]
        + [
            pltpu.SemaphoreType.DMA((SEMS,)),
            pltpu.SemaphoreType.DMA((SEMS,)),
            pltpu.SemaphoreType.DMA((8,)),
        ]
    )
    out_shape = [
        jax.ShapeDtypeStruct((half, width), LOW),
        jax.ShapeDtypeStruct((half, width), LOW),
        jax.ShapeDtypeStruct((rows, packed), FULL),
        jax.ShapeDtypeStruct((4, hr, own), FULL),
        jax.ShapeDtypeStruct((rows, width), FULL),
        jax.ShapeDtypeStruct((rows, width), FULL),
        jax.ShapeDtypeStruct((4, VEC // 2, width), FULL),
    ]
    bo, ig, gq, go, gf, gp, vo = pl.pallas_call(
        functools.partial(block_kernel, repeat, seq_len),
        out_shape=out_shape,
        in_specs=[ANY] * 7 + [pl.BlockSpec(memory_space=pltpu.SMEM)],
        out_specs=[IN_VMEM] * 7,
        scratch_shapes=scratch,
        compiler_params=pltpu.CompilerParams(
            collective_id=0, has_side_effects=True, vmem_limit_bytes=62 * 1024 * 1024
        ),
    )(tokens, cotangent, vec, wq, wo, wf, wp, prefix)

    def scatter(v, axis):
        return scatter_groups(v, axis, repeat, groups)

    def part(v):
        n = v.shape[-1] // GROUPS
        return lax.dynamic_slice_in_dim(v, s * n, n, v.ndim - 1)

    third = gq[:, 3 * pair :]
    gq = jnp.stack(
        [
            jnp.concatenate([gq[:, k * pair : (k + 1) * pair], third[:, k * HD : (k + 1) * HD]], axis=1)
            for k in range(3)
        ]
    )
    go = jnp.transpose(go.reshape(2, 2, hr, own), (1, 3, 0, 2)).reshape(2, own, rows)
    tail = own - 2 * pair
    go = jnp.concatenate(
        [
            v
            for b in range(2)
            for core in range(2)
            for v in (
                go[core, b * pair : (b + 1) * pair],
                go[core, 2 * pair + b * (tail // 2) : 2 * pair + (b + 1) * (tail // 2)],
            )
        ],
        axis=0,
    )
    both = vo[0] + vo[1]
    plain = [scatter(part(both[i]), 0) for i in (GAIN1, SHIFT1, OUTB, GAIN2, SHIFT2, PROJB)]

    def unpack(k):
        return jnp.concatenate(
            [
                v
                for b in range(2)
                for core in range(2)
                for v in (
                    vo[core, QKVB + b, k * pair : (k + 1) * pair],
                    vo[core, QKVB + b, 3 * pair + k * HD : 3 * pair + (k + 1) * HD],
                )
            ]
        )

    gqb = scatter(part(jnp.stack([unpack(0), unpack(2)])), 1)
    gfb = scatter(part(jnp.concatenate([vo[2, 0], vo[3, 0], vo[2, 1], vo[3, 1]])), 0)
    return (
        bo,
        ig,
        plain[0],
        plain[1],
        scatter(gq, 1),
        gqb,
        scatter(go, 1),
        plain[2],
        plain[3],
        plain[4],
        scatter(gf, 0),
        gfb,
        scatter(gp.T, 1),
        plain[5],
    )


def solution(mesh):
    placed = (
        P(("dp", "tensor"), None),
        P("dp"),
        P(("dp", "tensor"), None),
        P("dp"),
        P("dp"),
        P(None, "dp", "tensor"),
        P(None, "dp"),
        P(None, "dp"),
        P("dp"),
        P("dp"),
        P("dp"),
        P("dp", "tensor"),
        P("dp"),
        P("tensor", "dp"),
        P("dp"),
    )
    return jax.shard_map(
        functools.partial(on_device, mesh.shape["dp"]),
        mesh=mesh,
        in_specs=placed,
        out_specs=(placed[0], placed[0]) + placed[3:],
        check_vma=False,
    )
```

time: 1030 us -> 198 us (0.19)
  waiting for transfers between devices: 577 us -> 0 us
  Pallas kernels: 0 us -> 170 us
  blocking collectives: 168 us -> 0 us
  matrix products: 114 us -> 0 us
  other arithmetic: 53.3 us -> 5.92 us
  local copies, waits for them, and re-layouts: 63.9 us -> 19.6 us
  loops' own time: 31.9 us -> 0 us
  between operations: 17.1 us -> 0.98 us
    reduce_scatter x6 -> x0, waiting for transfers between devices: 299 us -> none  [the longest x1 72.1 us: on_device(): lax.psum_scatter(proj_grad, 'dp', scatter_dimension=1, tiled=True)]
    pallas_call x0 -> x1, Pallas kernels: none -> 170 us  [on_device(): pl.pallas_call(functools.partial(block_kernel, repeat, seq_len), out_shap...]
    unnamed x19 -> x0, waiting for transfers between devices: 141 us -> none
    all_gather x7 -> x0, waiting for transfers between devices: 136 us -> none  [the longest x1 36.4 us: on_device(): lax.all_gather(proj_weight.astype(low_type), 'dp', axis=1, tiled=True)]
    dot_general x38 -> x0, matrix products: 106 us -> none  [the longest x1 10.3 us: on_device(): jnp.einsum('nd,fd->nf', mlp_grad_all, proj_local, preferred_element_type=...]
    all_gather x4 -> x0, blocking collectives: 84.3 us -> none  [the longest x1 35.7 us: on_device(): lax.all_gather(qkv_weight.astype(low_type), 'dp', axis=1, tiled=True)]
    unnamed x2 -> x0, blocking collectives: 76.8 us -> none
    another operation x2 -> x0, loops' own time: 31.9 us -> none  [the longest x1 16 us: on_device(): lax.scan(backward_block, initial, jnp.arange(block_count))]
  transfers between devices with their start and end apart: 16 -> 0, of which waited for: 14 -> 0; matrix products, arithmetic and copies ran while one was open for 12% -> 0% of each run, Pallas kernels for 0% -> 0%
where the time goes in v1:
time: 198 us; the launch traced here: 197 us
  Pallas kernels  170 us (86%)
  local copies, waits for them, and re-layouts  19.6 us (10%)
  other arithmetic  5.92 us (3%)
    pallas_call x1, Pallas kernels, on_device(): pl.pallas_call(functools.partial(block_kernel, repeat, seq_len), out_shap...  170 us
    unnamed x36, local copies, waits for them, and re-layouts  8.89 us

profile of v1, /device:TPU:0, one launch (start us, length us, event | category | flops | bytes accessed | tf_op | source)
XLA Modules:
  0.0 196.9 jit_solution(17270995135149860373)
XLA Ops:
  0.7 1.0 convert_element_type.45
  1.7 0.1 constant_dynamic-slice_fusion.8
  1.8 0.1 constant_dynamic-slice_fusion
  1.9 0.7 fusion.3.refs_4_
  2.6 0.7 copy-done.8
  3.3 0.2 dynamic_update_slice.41
  3.6 0.7 copy-done.9
  4.2 0.2 dynamic_update_slice.40
  4.6 0.2 dynamic_update_slice.39
  4.9 0.1 concatenate.34
  5.0 0.1 concatenate.33
  5.1 0.6 copy-done.10
  5.8 0.2 dynamic_update_slice.34
  6.0 0.5 copy-done.11
  6.4 0.2 dynamic_update_slice.35
  6.6 0.5 copy-done.12
  7.1 0.2 dynamic_update_slice.36
  7.3 0.5 copy-done.13
  7.8 0.2 dynamic_update_slice.37
  7.9 0.5 copy-done.14
  8.4 0.2 dynamic_update_slice.38
  8.6 0.5 copy-done.15
  9.1 0.1 dynamic_update_slice.33
  9.3 1.3 stack.69.refs_2_
  10.7 0.8 concatenate.35.refs_3_
  11.4 0.1 copy-done.4
  11.5 0.7 convert_bitcast_fusion.refs_6_
  12.2 0.7 convert_element_type.46.refs_5_
  12.9 170.4 %shard_map.254 = (bf16[512,768]{1,0:T(8,128)(2,1)}, bf16[512,768]{1,0:T(8,128)(2,1)}, f32[96,640]{1,0:T(8,128)}, f32[4,48,384]{2,1,0:T(8,128)}, f32[96,768]{1,0:...) custom-call(bf16[512,768]{1,0:T(8,128)(2,1)} %refs_0_.1, bf16[512,768]{1,0:T(8,128)(2,1)} %refs_1_.1, ...), custom_call_target="tpu_custom_call" | custom-call | tf_op jit(solution)/shard_map/pallas_call | solution.py:805
  183.3 0.9 slice_reduce_fusion
  184.1 0.7 fusion.6
  184.8 0.8 slice_add_fusion
  185.6 0.6 fusion.12
  186.2 0.6 fusion.10
  186.8 1.0 copy.29
  187.9 0.8 concatenate.42
  188.7 0.8 slice_bitcast_fusion.14
  189.5 0.8 slice_bitcast_fusion.15
  190.4 0.6 fusion.7
  191.2 0.7 pad_maximum_fusion
  192.0 0.6 fusion.8
  192.6 0.9 copy.43
  193.4 0.5 copy-done
  194.0 0.9 copy.44
  194.9 0.2 copy-done.7
  195.1 0.7 copy.45
  195.8 0.4 copy-done.6
  196.2 0.7 copy.46
  (67 shorter events, 0.8 us)
Async XLA Ops:
  1.6 8.9 %copy-start.3 = (f32[3,96,192]{2,1,0:T(8,128)S(1)}, f32[3,96,192]{2,1,0:T(8,128)}, u32[]{:S(2)}) copy-start(f32[3,96,192]{2,1,0:T(8,128)} %param.20) | copy-start | bytes 663556
  2.6 0.7 copy-start.8
  3.5 0.7 copy-start.9
  5.1 0.7 copy-start.10
  5.8 0.7 copy-start.11
  6.4 0.7 copy-start.12
  7.1 0.7 copy-start.13
  7.8 0.7 copy-start.14
  8.4 0.7 copy-start.15
  10.6 1.0 copy-start.4
  10.6 1.6 copy-start.5
  187.9 3.2 %copy-start.2 = (f32[96,640]{1,0:T(8,128)S(1)}, f32[96,640]{1,0:T(8,128)}, u32[]{:S(2)}) copy-start(f32[96,640]{1,0:T(8,128)} %get-tuple-element.24) | copy-start | bytes 737284
  191.1 1.5 copy-start.1
  192.6 1.4 copy-start
  194.0 1.1 copy-start.7
  195.1 1.1 copy-start.6

commit v2 on v1

v2 whole, which is shorter than its diff:
```python
import functools
import math

import jax
import jax.numpy as jnp
from jax import lax
from jax.experimental import pallas as pl
from jax.experimental.pallas import tpu as pltpu
from jax.sharding import PartitionSpec as P

MESH = pl.DeviceIdType.MESH
LOW, FULL = jnp.bfloat16, jnp.float32
EPSILON = 1e-05
HD = 64
GROUPS, ZN, XN = 8, 4, 2
SEMS = 200
VEC = 16

GAIN1, SHIFT1, QKVB, OUTB, GAIN2, SHIFT2, PROJB, FCB = 0, 1, 2, 8, 9, 10, 11, 12


def dot(a, b):
    return jnp.dot(a, b, preferred_element_type=FULL)


def dot_nt(a, b):
    return lax.dot_general(a, b, (((1,), (1,)), ((), ())), preferred_element_type=FULL)


def dot_tn(a, b):
    return lax.dot_general(a, b, (((0,), (0,)), ((), ())), preferred_element_type=FULL)


def block_kernel(repeat, seq_len, *refs):
    (
        tok_h, prefix_s, cot_h, gain1_h, shift1_h, wq_h, qvb_h, wo_h, outb_h,
        gain2_h, shift2_h, wf_h, fcb_h, wp_h, projb_h,
        bo_h, ig_h, gq_ref, go_ref, gf_ref, gp_ref, vo_ref,
        Wq, Wo, Wf, Wp, Go, Gp,
        RqA1, RqB1, RqA2, RqB2, Rq3,
        RfA1, RfB1, RfA2, RfB2, Rf3,
        RpA1, RpB1, RpA2, RpB2, RpA3, RpB3,
        Ro1, Ro2, Ro3,
        TOK, COT, N1F, N2F, RS1, RS2, N1, N2, T0, T1,
        QP, KP, VP, CTX, DO, DQ, LSEC, LSER, DELR,
        MID, S0, V0, V1, H, GPR, PG,
        SV, SB, SC, SQ, SO, SF, SP, SW,
        VR, VF, VG, VZ, VO,
        ss, rs, ls,
    ) = refs
    half = seq_len // 2
    width = TOK.shape[1]
    rblk = 256
    nrb = seq_len // rblk
    dp = lax.axis_index("dp")
    t = lax.axis_index("tensor")
    s, sub = dp // repeat, dp % repeat
    z, x = s // XN, s % XN
    y, c = t // 2, t % 2
    oy, oc, ox = 1 - y, 1 - c, 1 - x

    def at(zz, xx, tt):
        return ((zz * XN + xx) * repeat + sub, tt)

    def zdev(k):
        return at((z + k) % ZN, x, t)

    xdev = at(z, ox, t)
    ydev = at(z, x, oy * 2 + c)
    cdev = at(z, x, y * 2 + oc)
    gdev = at(z, x, oy * 2 + oc)
    near = [xdev, ydev, cdev, gdev] + [at(z, ox, i * 2 + j) for i, j in ((y, oc), (oy, c), (oy, oc))]
    others = [(((s + k) % GROUPS) * repeat + sub, t) for k in range(1, GROUPS)]

    made = []

    def copy(src, dst, dev):
        k = len(made)

        def make():
            return pltpu.make_async_remote_copy(
                src_ref=src, dst_ref=dst, send_sem=ss.at[k], recv_sem=rs.at[k],
                device_id=dev, device_id_type=MESH,
            )

        made.append(make)
        return make

    def start(makes):
        for m in makes:
            m().start()

    def landed(makes):
        for m in makes:
            m().wait_recv()

    def sent(makes):
        for m in makes:
            m().wait_send()

    barrier = pltpu.get_barrier_semaphore()
    peers = others + [d for i, d in enumerate(near) if i != 0]
    for d in peers:
        pl.semaphore_signal(barrier, inc=1, device_id=d, device_id_type=MESH)

    brought = [
        (wq_h, SQ), (qvb_h, SB), (fcb_h, SC.at[0]),
        (gain1_h, SV.at[0]), (shift1_h, SV.at[1]), (outb_h, SV.at[2]),
        (gain2_h, SV.at[3]), (shift2_h, SV.at[4]), (projb_h, SV.at[5]),
        (wo_h, SO), (tok_h, TOK), (cot_h, COT.at[c]), (wf_h, SF), (wp_h, SP),
    ]
    local = [pltpu.make_async_copy(a, b, ls.at[i]) for i, (a, b) in enumerate(brought)]
    for cp in local:
        cp.start()

    lanes96 = SV.shape[1]
    VG[...] = jnp.zeros(VG.shape, FULL)
    for cp in local[1:9]:
        cp.wait()
    VG[0:6, :lanes96] = SV[0:6, :]
    VG[6:8, :lanes96] = SB[...]
    for j in range(4):
        VG[8 + j : 9 + j, :lanes96] = SC[:, j * lanes96 : (j + 1) * lanes96]
    VR[s] = VG[:, :128].astype(LOW)
    VG[...] = jnp.zeros(VG.shape, FULL)
    local[0].wait()
    q3 = SQ[...]
    Wq[y, z, x] = jnp.concatenate(
        [q3[0, :, :128], q3[1, :, :128], q3[2, :, :128]]
        + [q3[k, :, 128:] for k in range(3)]
        + [jnp.zeros((q3.shape[1], HD), FULL)],
        axis=1,
    ).astype(LOW)
    local[9].wait()
    turned = pltpu.roll(SO[...], (width - c * (width // 4)) % width, 1)
    last = jnp.concatenate([turned[:, 128:192], turned[:, 512:576]], axis=1)
    mine = jnp.concatenate([turned[:, 0:128], turned[:, 384:512], last], axis=1).astype(LOW)
    SW[0] = mine[: SW.shape[1]]
    SW[1] = mine[SW.shape[1] :]
    Wo[z, x, y] = SW[y]
    local[12].wait()
    Wf[y, z, x] = SF[...].astype(LOW)
    local[13].wait()
    Wp[y, z, x] = SP[...].astype(LOW)
    local[10].wait()
    local[11].wait()
    pl.semaphore_wait(barrier, len(peers))

    vec_c = [copy(VR.at[s], VR.at[s], d) for d in others]
    cot_c = [copy(COT.at[c], COT.at[c], cdev)]
    hr = wq_h.shape[1] // 2
    third = hr // 3
    pairs = (
        (pl.ds(0, third), pl.ds(third, third)),
        (pl.ds(2 * third, 2 * third), pl.ds(4 * third, 2 * third)),
    )

    def gather(W):
        steps = []
        for a, b in pairs:
            zs = [copy(W.at[y, z, x, r], W.at[y, z, x, r], zdev(k)) for k in range(1, ZN) for r in (a, b)]
            one = [
                copy(W.at[y, :, x, a], W.at[y, :, x, a], xdev),
                copy(W.at[y, :, x, b], W.at[y, :, x, b], ydev),
            ]
            two = [
                copy(W.at[y, :, :, a], W.at[y, :, :, a], ydev),
                copy(W.at[:, :, x, b], W.at[:, :, x, b], xdev),
            ]
            steps.append((zs, one, two))
        return steps

    def gather_wide(W):
        steps = []
        for a, b in pairs:
            near = [
                copy(W.at[y, z, x, a], W.at[y, z, x, a], xdev),
                copy(W.at[y, z, x, b], W.at[y, z, x, b], ydev),
            ]
            zs = [copy(W.at[y, z, :, a], W.at[y, z, :, a], zdev(k)) for k in range(1, ZN)]
            zs += [copy(W.at[:, z, x, b], W.at[:, z, x, b], zdev(k)) for k in range(1, ZN)]
            far = [
                copy(W.at[y, :, :, a], W.at[y, :, :, a], ydev),
                copy(W.at[:, :, x, b], W.at[:, :, x, b], xdev),
            ]
            steps.append((near, zs, far))
        return steps

    ow = [
        (
            [copy(Wo.at[z, x, y], Wo.at[z, x, y], zdev(k)) for k in range(1, ZN)],
            [copy(Wo.at[:, x, y], Wo.at[:, x, y], xdev)],
            [copy(Wo.at[:, :, y], Wo.at[:, :, y], ydev)],
        )
    ]
    qw, pw, fw = gather(Wq), gather_wide(Wp), gather(Wf)

    def z_go(w, i):
        start(w[i][0])

    def one_go(w, i):
        landed(w[i][0])
        start(w[i][1])

    def two_go(w, i):
        landed(w[i][1])
        start(w[i][2])

    def all_in(w):
        for step in w:
            landed(step[2])

    def sent_all(w):
        for step in w:
            for group in step:
                sent(group)

    start(vec_c)
    z_go(qw, 0)
    z_go(pw, 0)
    z_go(pw, 1)
    start(cot_c)

    def row_tile(i, n=128):
        return pl.ds(pl.multiple_of(i * n, n), n)

    @pl.loop(0, half // 128)
    def _(i):
        r = row_tile(i)
        v = TOK[r, :].astype(FULL)
        v = v - jnp.mean(v, axis=-1, keepdims=True)
        rstd = lax.rsqrt(jnp.mean(v * v, axis=-1, keepdims=True) + EPSILON)
        N1F[r, :] = v * rstd
        RS1[r, :] = jnp.broadcast_to(rstd, (128, 128))

    landed(vec_c)

    def widen(v):
        return jnp.concatenate([v, jnp.zeros((v.shape[0], width - v.shape[1]), FULL)], axis=1)

    pieces = [widen(VR[g].astype(FULL)) for g in range(GROUPS)]
    plain = pieces[0]
    for g in range(1, GROUPS):
        plain = plain + pltpu.roll(pieces[g], g * lanes96, 1)
    VF[GAIN1 : SHIFT1 + 1, :] = plain[0:2]
    VF[OUTB : PROJB + 1, :] = plain[2:6]
    place = lax.broadcasted_iota(jnp.int32, (1, width), 1)

    def lanes(v, first, last, shift):
        v = jnp.where((place >= first) & (place < last), v, 0.0)
        return pltpu.roll(v, shift % width, 1) if shift % width else v

    for b in range(2):
        a0, a1 = (widen(VR[2 * (2 * b + c) + i].astype(FULL)) for i in range(2))
        a1 = pltpu.roll(a1, lanes96, 1)
        qb, vb = a0[6:7] + a1[6:7], a0[7:8] + a1[7:8]
        VF[QKVB + b : QKVB + b + 1, :] = (
            lanes(qb, 0, 128, 0) + lanes(qb, 128, 192, 256) + lanes(vb, 0, 128, 256) + lanes(vb, 128, 192, 384)
        )
        a1 = pltpu.roll(a1, 3 * lanes96, 1)
        row = a0[8:9] + a1[8:9]
        for j in range(1, 4):
            row = row + pltpu.roll(a0[8 + j : 9 + j] + a1[8 + j : 9 + j], j * lanes96, 1)
        VF[FCB + b : FCB + b + 1, :] = row

    def vrow(i):
        return VF[i : i + 1, :]

    @pl.loop(0, half // 128)
    def _(i):
        r = row_tile(i)
        N1[c, r, :] = (N1F[r, :] * vrow(GAIN1) + vrow(SHIFT1)).astype(LOW)

    n1_c = [copy(N1.at[c], N1.at[c], cdev)]
    start(n1_c)
    landed(cot_c)

    def transpose_all(source, target):
        @pl.loop(0, nrb)
        def _(i):
            h, off = i // (half // rblk), i % (half // rblk)
            rows = pl.ds(pl.multiple_of(off * rblk, rblk), rblk)
            cols = pl.ds(pl.multiple_of(i * rblk, rblk), rblk)
            for k in range(width // rblk):
                target[k * rblk : (k + 1) * rblk, cols] = source[h, rows, k * rblk : (k + 1) * rblk].T

    one_go(qw, 0)
    z_go(qw, 1)
    transpose_all(COT, T0)
    two_go(qw, 0)
    z_go(fw, 0)
    one_go(qw, 1)
    z_go(fw, 1)
    z_go(ow, 0)
    landed(n1_c)
    two_go(qw, 1)
    one_go(pw, 0)
    one_go(fw, 0)
    all_in(qw)
    one_go(pw, 1)

    def low_lanes(v):
        return lax.broadcasted_iota(jnp.int32, v.shape, 1) < HD

    def tile(v, i):
        return v[:, i * 128 : (i + 1) * 128]

    def roll(v):
        return pltpu.roll(v, HD, 1)

    @pl.loop(0, nrb)
    def _(i):
        h, off = i // (half // rblk), i % (half // rblk)
        rows = pl.ds(pl.multiple_of(off * rblk, rblk), rblk)
        out = pl.ds(pl.multiple_of(i * rblk, rblk), rblk)
        n = N1[h, rows, :]
        got = []
        for b in range(2):
            got.append(dot(n, Wq[b].reshape(width, Wq.shape[-1])) + VF[QKVB + b : QKVB + b + 1, : Wq.shape[-1]])
            QP[b, out, :] = (tile(got[b], 0).astype(LOW).astype(FULL) * 0.125).astype(LOW)
            KP[b, out, :] = tile(got[b], 1).astype(LOW)
            VP[b, out, :] = tile(got[b], 2).astype(LOW)
        first = low_lanes(tile(got[0], 3))
        q = jnp.where(first, tile(got[0], 3), roll(tile(got[1], 3)))
        QP[2, out, :] = (q.astype(LOW).astype(FULL) * 0.125).astype(LOW)
        KP[2, out, :] = jnp.where(first, roll(tile(got[0], 3)), tile(got[1], 3)).astype(LOW)
        VP[2, out, :] = jnp.where(first, tile(got[0], 4), roll(tile(got[1], 4))).astype(LOW)

    prefix = prefix_s[y]
    LSEC[...] = jnp.zeros(LSEC.shape, FULL)

    def lane_part(v, e):
        lane = lax.broadcasted_iota(jnp.int32, v.shape, 1)
        keep = lane < HD if e == 0 else lane >= HD
        return jnp.where(keep, v, jnp.zeros_like(v))

    def meanwhile(p, b, plan):
        for (pp, bb), steps in plan.items():
            if bb == b:

                @pl.when(p == pp)
                def _(steps=steps):
                    for step in steps:
                        step()

    fetch = {
        (0, 0): [lambda: one_go(fw, 1), lambda: one_go(ow, 0)],
        (0, 1): [lambda: two_go(fw, 0)],
        (1, 1): [lambda: two_go(fw, 1), lambda: two_go(ow, 0)],
        (2, 1): [lambda: two_go(pw, 0)],
    }

    @pl.loop(0, 3)
    def _(p):
        for b in range(nrb):
            rows = pl.ds(b * rblk, rblk)
            cols = max(half, (b + 1) * rblk)
            q = QP[p, rows, :]
            keys, values = KP[p, :cols, :], VP[p, :cols, :]
            query = b * rblk + lax.broadcasted_iota(jnp.int32, (rblk, 1), 0)
            limit = jnp.maximum(prefix - 1, query)
            key = lax.broadcasted_iota(jnp.int32, (rblk, cols), 1)
            parts = []
            for e in range(2):
                sc = dot_nt(lane_part(q, e), keys)
                sc = jnp.where(key <= limit, sc, -1e30)
                peak = jnp.max(sc, axis=-1, keepdims=True)
                w = jnp.exp(sc - peak)
                total = jnp.sum(w, axis=-1, keepdims=True)
                parts.append(dot(w.astype(LOW), values) * (1.0 / total))
                lane = lax.broadcasted_iota(jnp.int32, (rblk, 128), 1)
                LSEC[rows, :] = jnp.where(lane == 2 * p + e, peak + jnp.log(total), LSEC[rows, :])
            CTX[p, rows, :] = jnp.where(low_lanes(parts[0]), parts[0], parts[1]).astype(LOW)
            meanwhile(p, b, fetch)

    for b in range(nrb):
        lt = LSEC[b * rblk : (b + 1) * rblk, :].T
        for h in range(6):
            LSER[h, :, b * rblk : (b + 1) * rblk] = lt[h : h + 1, :]
    all_in(ow)

    def wide(ref, rows):
        return jnp.concatenate([ref[0, rows, :], ref[1, rows, :], ref[2, rows, :]], axis=1)

    def split_rows(make_block, away, home, copies):
        per = half // rblk
        for which, target in ((oc, away), (c, home)):

            @pl.loop(0, per)
            def _(j):
                rows = pl.ds(pl.multiple_of(j * rblk, rblk), rblk)
                flat = pl.ds(pl.multiple_of((which * per + j) * rblk, rblk), rblk)
                target[rows, :] = make_block(which, rows, flat)

            if target is away:
                start(copies)

    po_c = [copy(S0, V0, cdev)]
    split_rows(
        lambda h, rows, flat: dot_nt(wide(CTX, flat), Wo[...].reshape(width, Wo.shape[-1])), S0, MID, po_c
    )
    two_go(pw, 1)
    landed(po_c)

    @pl.loop(0, half // 128)
    def _(i):
        r = row_tile(i)
        m = TOK[r, :].astype(FULL) + (MID[r, :] + V0[r, :] + vrow(OUTB))
        MID[r, :] = m
        v = m - jnp.mean(m, axis=-1, keepdims=True)
        rstd = lax.rsqrt(jnp.mean(v * v, axis=-1, keepdims=True) + EPSILON)
        n = v * rstd
        N2F[r, :] = n
        RS2[r, :] = jnp.broadcast_to(rstd, (128, 128))
        N2[c, r, :] = (n * vrow(GAIN2) + vrow(SHIFT2)).astype(LOW)

    n2_c = [copy(N2.at[c], N2.at[c], cdev)]
    start(n2_c)
    landed(n2_c)
    all_in(fw)

    root = math.sqrt(2.0 / math.pi)

    @pl.loop(0, nrb * 2)
    def _(k):
        b, i = k // nrb, k % nrb
        h, off = i // (half // rblk), i % (half // rblk)
        rows = pl.ds(pl.multiple_of(off * rblk, rblk), rblk)
        flat = pl.ds(pl.multiple_of(i * rblk, rblk), rblk)
        u = dot(N2[h, rows, :], Wf[b].reshape(width, width)) + VF[pl.ds(FCB + b, 1), :]
        uu = u * u
        th = jnp.tanh(root * u * (1.0 + 0.044715 * uu))
        H[b, flat, :] = (0.5 * u * (1.0 + th)).astype(LOW)
        GPR[b, flat, :] = 0.5 * (1.0 + th) + (0.5 * root) * u * (1.0 - th * th) * (1.0 + 0.134145 * uu)

    def weight_grad(left_t, right, G, first, last):
        @pl.loop(0, 4)
        def _(k):
            b, m = k // 2, k % 2
            rows = pl.ds(pl.multiple_of(m * (width // 2), width // 2), width // 2)
            g = dot(left_t[rows, :], right[b, :, first:last])
            g = g.astype(LOW).reshape(ZN // 2, XN, width // GROUPS, last - first)
            G[b, pl.ds(m * (ZN // 2), ZN // 2), :, :, first:last] = g

    every = pl.ds(0, width)
    by_rows = [pairs[0] + (pl.ds(0, third), every), pairs[1] + (pl.ds(third, 2 * third), every)]

    def reduce_copies(G, plan, A1, B1, A2, B2, R3):
        steps = []
        for a, b, r, cols in plan:
            one = [
                copy(G.at[:, :, ox, a, cols], A1.at[:, :, r, cols], xdev),
                copy(G.at[oy, :, :, b, cols], B1.at[:, :, r, cols], ydev),
            ]
            two = [
                copy(G.at[oy, :, x, a, cols], A2.at[:, r, cols], ydev),
                copy(G.at[y, :, ox, b, cols], B2.at[:, r, cols], xdev),
            ]
            three = [
                copy(G.at[y, (z + k) % ZN, x, q, cols], R3.at[k - 1, q, cols], zdev(k))
                for k in range(1, ZN)
                for q in (a, b)
            ]
            steps.append((a, b, r, cols, one, two, three))

        def add(target, source):
            target[...] = (target[...].astype(FULL) + source[...].astype(FULL)).astype(LOW)

        def go(i):
            start(steps[i][4])

        def second(i):
            a, b, r, cols, one, two, three = steps[i]
            landed(one[:1])

            @pl.loop(0, ZN)
            def _(k):
                add(G.at[oy, k, x, a, cols], A1.at[oy, k, r, cols])

            start(two[:1])
            landed(one[1:])

            @pl.loop(0, ZN)
            def _(k):
                add(G.at[y, k, ox, b, cols], B1.at[k, ox, r, cols])

            start(two[1:])

            @pl.loop(0, ZN)
            def _(k):
                add(G.at[y, k, x, a, cols], A1.at[y, k, r, cols])
                add(G.at[y, k, x, b, cols], B1.at[k, x, r, cols])

        def third_step(i):
            a, b, r, cols, one, two, three = steps[i]
            landed(two)

            @pl.loop(0, ZN)
            def _(k):
                add(G.at[y, k, x, a, cols], A2.at[k, r, cols])
                add(G.at[y, k, x, b, cols], B2.at[k, r, cols])

            start(three)

        def last(i, out):
            a, b, r, cols, one, two, three = steps[i]
            landed(three)
            for q in (a, b):
                v = G[y, z, x, q, cols].astype(FULL)
                for k in range(ZN - 1):
                    v = v + R3[k, q, cols].astype(FULL)
                out[q, cols] = v

        return go, second, third_step, last

    def reduce_wide(G, plan, A1, B1, A2, B2, A3, B3):
        steps = []
        for a, b, r, cols in plan:
            one = [
                copy(G.at[oy, :, :, a, cols], A1.at[:, :, r, cols], ydev),
                copy(G.at[:, :, ox, b, cols], B1.at[:, :, r, cols], xdev),
            ]
            two = [copy(G.at[y, (z + k) % ZN, :, a, cols], A2.at[k - 1, :, r, cols], zdev(k)) for k in range(1, ZN)]
            two += [copy(G.at[:, (z + k) % ZN, x, b, cols], B2.at[k - 1, :, r, cols], zdev(k)) for k in range(1, ZN)]
            three = [
                copy(G.at[y, z, ox, a, cols], A3.at[r, cols], xdev),
                copy(G.at[oy, z, x, b, cols], B3.at[r, cols], ydev),
            ]
            steps.append((a, b, r, cols, one, two, three))

        def add(target, sources):
            v = target[...].astype(FULL)
            for source in sources:
                v = v + source[...].astype(FULL)
            target[...] = v.astype(LOW)

        def go(i):
            start(steps[i][4])

        def second(i):
            a, b, r, cols, one, two, three = steps[i]
            landed(one)

            @pl.loop(0, ZN)
            def _(k):
                for j in range(2):
                    add(G.at[y, k, j, a, cols], [A1.at[k, j, r, cols]])
                    add(G.at[j, k, x, b, cols], [B1.at[j, k, r, cols]])

            start(two)

        def third_step(i):
            a, b, r, cols, one, two, three = steps[i]
            landed(two)
            for j in range(2):
                add(G.at[y, z, j, a, cols], [A2.at[k, j, r, cols] for k in range(ZN - 1)])
                add(G.at[j, z, x, b, cols], [B2.at[k, j, r, cols] for k in range(ZN - 1)])
            start(three)

        def last(i, out):
            a, b, r, cols, one, two, three = steps[i]
            landed(three)
            for q, R in ((a, A3), (b, B3)):
                out[q, cols] = G[y, z, x, q, cols].astype(FULL) + R[r, cols].astype(FULL)

        return go, second, third_step, last

    rp = reduce_wide(Gp, by_rows, RpA1, RpB1, RpA2, RpB2, RpA3, RpB3)
    weight_grad(T0, H, Gp, 0, width)
    transpose_all(N2, T1)
    all_in(pw)
    rp[0](0)
    rp[0](1)

    @pl.loop(0, nrb * 2)
    def _(k):
        b, i = k // nrb, k % nrb
        h, off = i // (half // rblk), i % (half // rblk)
        rows = pl.ds(pl.multiple_of(off * rblk, rblk), rblk)
        flat = pl.ds(pl.multiple_of(i * rblk, rblk), rblk)
        g = (dot(COT[h, rows, :], Wp[b].reshape(width, width)) * GPR[b, flat, :]).astype(LOW)
        PG[b, flat, :] = g
        VG[pl.ds(FCB + b, 1), :] += jnp.sum(g.astype(FULL), axis=0, keepdims=True)

    p2_c = [copy(S0, V1, cdev)]
    home2, homem, home1 = GPR.at[0, pl.ds(0, half)], GPR.at[0, pl.ds(half, half)], GPR.at[1, pl.ds(0, half)]
    awaym = GPR.at[1, pl.ds(half, half)]

    def pair_nt(A, W, columns):
        def block(h, rows, flat):
            return dot_nt(A[0, flat, :columns], W[0].reshape(width, W.shape[-1])) + dot_nt(
                A[1, flat, :columns], W[1].reshape(width, W.shape[-1])
            )

        return block

    sent(po_c)
    split_rows(pair_nt(PG, Wf, width), S0, home2, p2_c)
    pm_c = [copy(awaym, V0, cdev)]
    split_rows(pair_nt(H, Wp, width), awaym, homem, pm_c)
    sent_all(pw)
    rp[1](0)
    weight_grad(T1, PG, Wp, 0, width)
    rf = reduce_copies(Wp, by_rows, RfA1, RfB1, RfA2, RfB2, Rf3)
    rf[0](0)
    rf[0](1)
    landed(p2_c)

    sent(n2_c)

    def norm_back(dy, n, rstd, gain):
        e = dy * gain
        return (e - jnp.mean(e, axis=-1, keepdims=True) - n * jnp.mean(e * n, axis=-1, keepdims=True)) * rstd

    def add_row(i, v):
        VG[i : i + 1, :] += jnp.sum(v, axis=0, keepdims=True)

    @pl.loop(0, half // 128)
    def _(i):
        r = row_tile(i)
        dy = GPR[0, r, :] + V1[r, :]
        n = N2F[r, :]
        add_row(GAIN2, dy * n)
        add_row(SHIFT2, dy)
        cot = COT[c, r, :].astype(FULL)
        add_row(PROJB, cot)
        g = cot + norm_back(dy, n, RS2[r, 0:1], vrow(GAIN2))
        N2F[r, :] = g
        low = g.astype(LOW)
        add_row(OUTB, low.astype(FULL))
        N2[c, r, :] = low

    ag_c = [copy(N2.at[c], N2.at[c], cdev)]
    start(ag_c)

    def vector_copies(first, last):
        r = pl.ds(first, last - first)
        over_z = [copy(VG.at[r], VZ.at[k - 1, r], zdev(k)) for k in range(1, ZN)]
        mine = VO.at[y * 2 + x, c, r]
        return r, over_z, mine, [copy(mine, mine, d) for d in near]

    def vector_second(v):
        r, over_z, mine, over_near = v
        landed(over_z)
        mine[...] = VG[r, :] + VZ[0, r, :] + VZ[1, r, :] + VZ[2, r, :]
        start(over_near)

    def vector_last(v):
        r, over_z, mine, over_near = v
        landed(over_near)
        for core in range(2):
            vo_ref[core, r, :] = VO[0, core, r, :] + VO[1, core, r, :] + VO[2, core, r, :] + VO[3, core, r, :]

    late, early = vector_copies(0, 8), vector_copies(8, VEC)
    start(early[1])
    transpose_all(N1, T1)
    rp[1](1)
    landed(pm_c)

    @pl.loop(0, half // 128)
    def _(i):
        r = row_tile(i)
        far = row_tile(i + half // 128)
        TOK[r, :] = (MID[r, :] + (GPR[0, far, :] + V0[r, :] + vrow(PROJB))).astype(LOW)

    out_c = [pltpu.make_async_copy(TOK, bo_h, ls.at[0]), pltpu.make_async_copy(N1.at[c], ig_h, ls.at[1])]
    out_c[0].start()
    landed(ag_c)

    @pl.loop(0, nrb)
    def _(i):
        h, off = i // (half // rblk), i % (half // rblk)
        rows = pl.ds(pl.multiple_of(off * rblk, rblk), rblk)
        flat = pl.ds(pl.multiple_of(i * rblk, rblk), rblk)
        g = dot(N2[h, rows, :], Wo[...].reshape(width, Wo.shape[-1])).astype(LOW)
        row = lax.broadcasted_iota(jnp.int32, (8, 128), 0)
        lane = lax.broadcasted_iota(jnp.int32, (8, 128), 1)
        pick = jnp.where(lane // HD == row, 1.0, 0.0).astype(LOW)
        for p in range(3):
            gp = tile(g, p)
            DO[p, flat, :] = gp
            prod = gp.astype(FULL) * CTX[p, flat, :].astype(FULL)
            high = prod.astype(LOW)
            rest = (prod - high.astype(FULL)).astype(LOW)
            d = dot_nt(pick, high) + dot_nt(pick, rest)
            for e in range(2):
                DELR[2 * p + e, :, flat] = d[e : e + 1, :]

    transpose_all(N2, T0)

    @pl.loop(0, 2)
    def _(m):
        rows = pl.ds(pl.multiple_of(m * (width // 2), width // 2), width // 2)
        g = dot(T0[rows, :], wide(CTX, pl.ds(0, seq_len)))
        g = g.astype(LOW).reshape(ZN // 2, XN, 2, width // (2 * GROUPS), Wo.shape[-1])
        Go[pl.ds(m * (ZN // 2), ZN // 2)] = g

    ro = [
        [copy(Go.at[:, :, oy], Ro1, ydev)],
        [copy(Go.at[:, ox, y], Ro2, xdev)],
        [copy(Go.at[(z + k) % ZN, x, y], Ro3.at[k - 1], zdev(k)) for k in range(1, ZN)],
        [copy(go_ref.at[t], go_ref.at[t], d) for d in (cdev, ydev, gdev)],
    ]
    start(ro[0])

    def ro_second():
        landed(ro[0])

        @pl.loop(0, ZN)
        def _(k):
            for i in range(XN):
                Go[k, i, y] = (Go[k, i, y].astype(FULL) + Ro1[k, i].astype(FULL)).astype(LOW)

        start(ro[1])

    def ro_third():
        landed(ro[1])

        @pl.loop(0, ZN)
        def _(k):
            Go[k, x, y] = (Go[k, x, y].astype(FULL) + Ro2[k].astype(FULL)).astype(LOW)

        start(ro[2])

    def ro_last():
        landed(ro[2])
        v = Go[z, x, y].astype(FULL)
        for k in range(ZN - 1):
            v = v + Ro3[k].astype(FULL)
        go_ref[t] = v
        start(ro[3])

    def attention_back(p, plan):
        DQ[...] = jnp.zeros(DQ.shape, FULL)
        for b in range(nrb):
            rows = pl.ds(b * rblk, rblk)
            first = 0 if b * rblk < half else b * rblk
            n = seq_len - first
            keys, values = KP[p, rows, :], VP[p, rows, :]
            queries, grads = QP[p, first:, :], DO[p, first:, :]
            key = b * rblk + lax.broadcasted_iota(jnp.int32, (rblk, 1), 0)
            limit = jnp.where(key < prefix, 0, key)
            query = first + lax.broadcasted_iota(jnp.int32, (rblk, n), 1)
            dk, dv = [], []
            for e in range(2):
                ke, ve = lane_part(keys, e), lane_part(values, e)
                sc = dot_nt(ke, queries) - LSER[2 * p + e, :, first:]
                w = jnp.exp(jnp.where(query >= limit, sc, -1e30))
                dw = dot_nt(ve, grads) - DELR[2 * p + e, :, first:]
                ds = (w * dw).astype(LOW)
                dv.append(dot(w.astype(LOW), grads))
                dk.append(dot(ds, queries))
                DQ[first:, :] += dot_tn(ds, ke)
            KP[p, rows, :] = jnp.where(low_lanes(dk[0]), dk[0], dk[1]).astype(LOW)
            VP[p, rows, :] = jnp.where(low_lanes(dv[0]), dv[0], dv[1]).astype(LOW)
            meanwhile(p, b, plan)
        QP[p, :, :] = (DQ[...] * 0.125).astype(LOW)

    away = {
        (0, 3): [lambda: rf[1](0), ro_second],
        (1, 2): [lambda: rf[1](1), ro_third],
        (2, 0): [lambda: rp[2](0)],
        (2, 1): [lambda: rf[2](0)],
        (2, 3): [lambda: rf[2](1)],
    }

    @pl.loop(0, 2)
    def _(p):
        attention_back(p, away)

    packed = Wq.shape[-1]
    sent_all(fw)

    @pl.loop(0, nrb)
    def _(i):
        flat = pl.ds(pl.multiple_of(i * rblk, rblk), rblk)
        for b in range(2):
            for k, ref in enumerate((QP, KP, VP)):
                g = ref[b, flat, :]
                H[b, flat, k * 128 : (k + 1) * 128] = g
                VG[QKVB + b : QKVB + b + 1, k * 128 : (k + 1) * 128] += jnp.sum(g.astype(FULL), axis=0, keepdims=True)

    both = (pl.ds(0, hr), pl.ds(hr, hr), pl.ds(0, hr))
    by_lanes = [both + (pl.ds(0, 384),), both + (pl.ds(384, packed - 384),)]
    weight_grad(T1, H, Wf, 0, 384)
    rq = reduce_copies(Wf, by_lanes, RqA1, RqB1, RqA2, RqB2, Rq3)
    rq[0](0)
    attention_back(2, away)

    @pl.loop(0, nrb)
    def _(i):
        flat = pl.ds(pl.multiple_of(i * rblk, rblk), rblk)
        q, k, v = (ref[2, flat, :].astype(FULL) for ref in (QP, KP, VP))
        first = low_lanes(q)
        packs = (
            (jnp.where(first, q, roll(k)), jnp.where(first, v, 0.0)),
            (jnp.where(first, roll(q), k), jnp.where(first, roll(v), 0.0)),
        )
        for b in range(2):
            for j in range(2):
                at_j = slice(384 + 128 * j, 512 + 128 * j)
                H[b, flat, at_j] = packs[b][j].astype(LOW)
                VG[QKVB + b : QKVB + b + 1, at_j] += jnp.sum(packs[b][j], axis=0, keepdims=True)

    weight_grad(T1, H, Wf, 384, packed)
    rq[0](1)

    p1_c = [copy(S0, V1, cdev)]
    sent(p2_c)
    split_rows(pair_nt(H, Wq, packed), S0, home1, p1_c)
    rq[1](0)
    rp[2](1)
    vector_second(early)
    landed(p1_c)

    sent(n1_c)

    @pl.loop(0, half // 128)
    def _(i):
        r = row_tile(i)
        dy = GPR[1, r, :] + V1[r, :]
        n = N1F[r, :]
        add_row(GAIN1, dy * n)
        add_row(SHIFT1, dy)
        N1[c, r, :] = (N2F[r, :] + norm_back(dy, n, RS1[r, 0:1], vrow(GAIN1))).astype(LOW)

    out_c[1].start()

    start(late[1])
    rq[1](1)
    rq[2](0)
    ro_last()
    vector_second(late)
    rp[3](0, gp_ref)
    rp[3](1, gp_ref)
    rq[2](1)
    rf[3](0, gf_ref)
    rf[3](1, gf_ref)
    vector_last(early)
    landed(ro[3])
    rq[3](0, gq_ref)
    vector_last(late)
    rq[3](1, gq_ref)

    waited = {id(m) for m in po_c + n2_c + p2_c + n1_c}
    for w in (pw, fw):
        for step in w:
            for group in step:
                waited |= {id(m) for m in group}
    sent([m for m in made if id(m) not in waited])
    for cp in out_c:
        cp.wait()


def gather_groups(v, axis, repeat, groups):
    if repeat == 1:
        return v
    return lax.all_gather(v, "dp", axis=axis, axis_index_groups=groups, tiled=True)


def scatter_groups(v, axis, repeat, groups):
    if repeat == 1:
        return v
    return lax.psum_scatter(v, "dp", scatter_dimension=axis, axis_index_groups=groups, tiled=True)


def on_device(
    dp_size,
    tokens,
    prefix,
    cotangent,
    first_gain,
    first_shift,
    qkv_weight,
    qv_bias,
    out_weight,
    out_bias,
    second_gain,
    second_shift,
    fc_weight,
    fc_bias,
    proj_weight,
    proj_bias,
):
    repeat = dp_size // GROUPS
    groups = [[g * repeat + i for i in range(repeat)] for g in range(GROUPS)]
    half, width = tokens.shape
    seq_len = 2 * half

    def whole(v, axis):
        return gather_groups(v.astype(LOW), axis, repeat, groups).astype(FULL) if repeat > 1 else v

    params = [
        whole(first_gain, 0), whole(first_shift, 0), whole(qkv_weight, 1), whole(qv_bias, 1), whole(out_weight, 1),
        whole(out_bias, 0), whole(second_gain, 0), whole(second_shift, 0), whole(fc_weight, 0), whole(fc_bias, 0),
        whole(proj_weight, 1), whole(proj_bias, 0),
    ]
    params[4], params[10] = params[4].T, params[10].T
    rows = params[8].shape[0]
    cols = params[2].shape[2]
    units = params[8].shape[1]
    pair = 2 * HD
    packed, own = 3 * cols + HD, 2 * cols
    hr = rows // 2
    ANY = pl.BlockSpec(memory_space=pl.ANY)
    IN_VMEM = pl.BlockSpec(memory_space=pltpu.VMEM)

    def reduce_space(lanes):
        return [
            pltpu.VMEM((2, ZN, hr, lanes), LOW),
            pltpu.VMEM((ZN, XN, hr, lanes), LOW),
            pltpu.VMEM((ZN, hr, lanes), LOW),
            pltpu.VMEM((ZN, hr, lanes), LOW),
            pltpu.VMEM((ZN - 1, rows, lanes), LOW),
        ]

    token_low = pltpu.VMEM((2, half, width), LOW)
    token_full = pltpu.VMEM((half, width), FULL)
    unit_low = pltpu.VMEM((2, seq_len, width), LOW)
    heads = pltpu.VMEM((3, seq_len, pair), LOW)
    scratch = (
        [
            pltpu.VMEM((2, ZN, XN, rows, packed), LOW),
            pltpu.VMEM((ZN, XN, 2, hr, own), LOW),
            pltpu.VMEM((2, ZN, XN, rows, width), LOW),
            pltpu.VMEM((2, ZN, XN, rows, width), LOW),
            pltpu.VMEM((ZN, XN, 2, hr, own), LOW),
            pltpu.VMEM((2, ZN, XN, rows, width), LOW),
        ]
        + reduce_space(packed)
        + reduce_space(width)
        + [
            pltpu.VMEM((ZN, XN, hr, width), LOW),
            pltpu.VMEM((2, ZN, hr, width), LOW),
            pltpu.VMEM((ZN - 1, XN, hr, width), LOW),
            pltpu.VMEM((ZN - 1, 2, hr, width), LOW),
            pltpu.VMEM((hr, width), LOW),
            pltpu.VMEM((hr, width), LOW),
        ]
        + [
            pltpu.VMEM((ZN, XN, hr, own), LOW),
            pltpu.VMEM((ZN, hr, own), LOW),
            pltpu.VMEM((ZN - 1, hr, own), LOW),
        ]
        + [
            pltpu.VMEM((half, width), LOW),
            token_low,
            token_full,
            token_full,
            pltpu.VMEM((half, 128), FULL),
            pltpu.VMEM((half, 128), FULL),
            token_low,
            token_low,
            pltpu.VMEM((width, seq_len), LOW),
            pltpu.VMEM((width, seq_len), LOW),
        ]
        + [heads] * 5
        + [
            pltpu.VMEM((seq_len, pair), FULL),
            pltpu.VMEM((seq_len, 128), FULL),
            pltpu.VMEM((6, 1, seq_len), FULL),
            pltpu.VMEM((6, 1, seq_len), FULL),
        ]
        + [token_full] * 4
        + [unit_low, pltpu.VMEM((2, seq_len, width), FULL), unit_low]
        + [
            pltpu.VMEM((8, rows), FULL),
            pltpu.VMEM((2, rows), FULL),
            pltpu.VMEM((1, 4 * rows), FULL),
            pltpu.VMEM((3, rows, cols), FULL),
            pltpu.VMEM((rows, width), FULL),
            pltpu.VMEM((rows, units), FULL),
            pltpu.VMEM((rows, units), FULL),
            pltpu.VMEM((2, hr, own), LOW),
            pltpu.VMEM((GROUPS, VEC, 128), LOW),
            pltpu.VMEM((VEC, width), FULL),
            pltpu.VMEM((VEC, width), FULL),
            pltpu.VMEM((ZN - 1, VEC, width), FULL),
        ]
        + [pltpu.VMEM((4, 2, VEC, width), FULL)]
        + [
            pltpu.SemaphoreType.DMA((SEMS,)),
            pltpu.SemaphoreType.DMA((SEMS,)),
            pltpu.SemaphoreType.DMA((16,)),
        ]
    )
    out_shape = [
        jax.ShapeDtypeStruct((half, width), LOW),
        jax.ShapeDtypeStruct((half, width), LOW),
        jax.ShapeDtypeStruct((rows, packed), FULL),
        jax.ShapeDtypeStruct((4, hr, own), FULL),
        jax.ShapeDtypeStruct((rows, width), FULL),
        jax.ShapeDtypeStruct((rows, width), FULL),
        jax.ShapeDtypeStruct((2, VEC, width), FULL),
    ]
    grown = pl.pallas_call(
        functools.partial(block_kernel, repeat, seq_len),
        out_shape=out_shape,
        in_specs=[ANY, pl.BlockSpec(memory_space=pltpu.SMEM)] + [ANY] * 13,
        out_specs=[ANY] * 2 + [IN_VMEM] * 5,
        scratch_shapes=scratch,
        compiler_params=pltpu.CompilerParams(
            collective_id=0, has_side_effects=True, vmem_limit_bytes=62 * 1024 * 1024
        ),
    )(tokens, prefix, cotangent, *params)

    vector = jax.ShapeDtypeStruct((rows,), FULL)
    small = (2, 3, 5, 7, 8, 9, 11, 13)
    results = pl.pallas_call(
        functools.partial(unpack_kernel, repeat),
        out_shape=[
            out_shape[0],
            out_shape[1],
            vector,
            vector,
            jax.ShapeDtypeStruct((3, rows, cols), FULL),
            jax.ShapeDtypeStruct((2, rows), FULL),
            jax.ShapeDtypeStruct((rows, width), FULL),
            vector,
            vector,
            vector,
            jax.ShapeDtypeStruct((rows, units), FULL),
            jax.ShapeDtypeStruct((4 * rows,), FULL),
            jax.ShapeDtypeStruct((rows, units), FULL),
            vector,
        ],
        in_specs=[ANY] * 7,
        out_specs=[IN_VMEM if i in small else ANY for i in range(14)],
        scratch_shapes=[
            pltpu.VMEM((rows, packed), FULL),
            pltpu.VMEM((4, hr, own), FULL),
            pltpu.VMEM((2, VEC, width), FULL),
            pltpu.VMEM((3, rows, cols), FULL),
            pltpu.VMEM((rows, width), FULL),
            pltpu.VMEM((half, width), LOW),
            pltpu.VMEM((half, width), LOW),
            pltpu.VMEM((rows, units), FULL),
            pltpu.VMEM((rows, units), FULL),
            pltpu.SemaphoreType.DMA((13,)),
        ],
        compiler_params=pltpu.CompilerParams(vmem_limit_bytes=62 * 1024 * 1024),
    )(*grown)
    results = [v.T if i in (6, 12) else v for i, v in enumerate(results)]
    along = (None, None, 0, 0, 1, 1, 1, 0, 0, 0, 0, 0, 1, 0)
    return tuple(
        v if repeat == 1 or axis is None else scatter_groups(v, axis, repeat, groups)
        for v, axis in zip(results, along, strict=True)
    )


def unpack_kernel(
    repeat, bo, ig, gq_h, go_h, gf, gp, vo_h,
    bo_out, ig_out, gain1, shift1, wq_h, qvb, wo_h, outb, gain2, shift2, wf, fcb, wp, projb,
    gq, go, vo, wq, wo, b1, b2, w1, w2, sems,
):
    moves = [(vo_h, vo), (gq_h, gq), (go_h, go), (ig, b2), (bo, b1), (gf, w1), (gp, w2)]
    moves += [(wq, wq_h), (wo, wo_h), (b2, ig_out), (b1, bo_out), (w1, wf), (w2, wp)]
    moves = [pltpu.make_async_copy(a, b, sems.at[i]) for i, (a, b) in enumerate(moves)]
    for cp in moves[:7]:
        cp.start()
    for i in range(3, 7):
        moves[i].wait()
        moves[i + 6].start()
    moves[1].wait()
    for k in range(3):
        wq[k] = jnp.concatenate(
            [gq[:, k * 128 : (k + 1) * 128], gq[:, 384 + k * HD : 384 + (k + 1) * HD]], axis=1
        )
    moves[7].start()
    moves[2].wait()
    m = [jnp.concatenate([go[core], go[2 + core]], axis=0) for core in range(2)]
    wo[...] = jnp.concatenate(
        [
            v
            for b in range(2)
            for core in range(2)
            for v in (m[core][:, b * 128 : (b + 1) * 128], m[core][:, 256 + b * HD : 256 + (b + 1) * HD])
        ],
        axis=1,
    )
    moves[8].start()
    moves[0].wait()
    s = lax.axis_index("dp") // repeat
    width = vo.shape[2]
    n = gain1.shape[0]
    both = pltpu.roll(vo[0] + vo[1], (GROUPS - s) % GROUPS * n, 1)
    for i, out in ((GAIN1, gain1), (SHIFT1, shift1), (OUTB, outb), (GAIN2, gain2), (SHIFT2, shift2), (PROJB, projb)):
        out[...] = both[i, :n]
    owner = s // 2
    core, b, odd = owner % 2, owner // 2, s % 2
    place = lax.broadcasted_iota(jnp.int32, (1, width), 1)

    def lanes(v, first, last, shift):
        v = jnp.where((place >= first) & (place < last), v, 0.0)
        return pltpu.roll(v, shift % width, 1) if shift % width else v

    row = vo[core, pl.ds(QKVB + b, 1), :]
    q = lanes(row, 0, 128, 0) + lanes(row, 384, 448, -256)
    v = lanes(row, 256, 384, -256) + lanes(row, 512, 576, -384)
    back = (width - odd * n) % width
    qvb[0:1, :] = pltpu.roll(q, back, 1)[:, :n]
    qvb[1:2, :] = pltpu.roll(v, back, 1)[:, :n]
    row = vo[core, pl.ds(FCB + b, 1), :]
    fcb[...] = pltpu.roll(row, odd * (width // 2), 1)[0, : width // 2]
    for i in range(7, 13):
        moves[i].wait()


def solution(mesh):
    placed = (
        P(("dp", "tensor"), None),
        P("dp"),
        P(("dp", "tensor"), None),
        P("dp"),
        P("dp"),
        P(None, "dp", "tensor"),
        P(None, "dp"),
        P(None, "dp"),
        P("dp"),
        P("dp"),
        P("dp"),
        P("dp", "tensor"),
        P("dp"),
        P("tensor", "dp"),
        P("dp"),
    )
    return jax.shard_map(
        functools.partial(on_device, mesh.shape["dp"]),
        mesh=mesh,
        in_specs=placed,
        out_specs=(placed[0], placed[0]) + placed[3:],
        check_vma=False,
    )
```

time: 198 us -> 165 us (0.83)
  local copies, waits for them, and re-layouts: 19.6 us -> 0 us
  Pallas kernels: 170 us -> 163 us
  other arithmetic: 5.92 us -> 0 us
    pallas_call x1, Pallas kernels: 170 us -> 159 us  [on_device(): pl.pallas_call(functools.partial(block_kernel, repeat, seq_len), out_shap...]
    unnamed x36 -> x0, local copies, waits for them, and re-layouts: 8.89 us -> none
    pallas_call x0 -> x1, Pallas kernels: none -> 3.64 us  [on_device(): pl.pallas_call(functools.partial(unpack_kernel, repeat), out_shape=[out_s...]
where the time goes in v2:
time: 165 us; the launch traced here: 163 us
  Pallas kernels  163 us (99%)
    pallas_call x1, Pallas kernels, on_device(): pl.pallas_call(functools.partial(block_kernel, repeat, seq_len), out_shap...  159 us
    pallas_call x1, Pallas kernels, on_device(): pl.pallas_call(functools.partial(unpack_kernel, repeat), out_shape=[out_s...  3.64 us

profile of v2, /device:TPU:0, one launch (start us, length us, event | category | flops | bytes accessed | tf_op | source)
XLA Modules:
  0.0 163.5 jit_solution(8263135594278732356)
XLA Ops:
  0.7 159.0 %shard_map.254 = (bf16[512,768]{1,0:T(8,128)(2,1)}, bf16[512,768]{1,0:T(8,128)(2,1)}, f32[96,640]{1,0:T(8,128)}, f32[4,48,384]{2,1,0:T(8,128)}, f32[96,768]{1,0:...) custom-call(bf16[512,768]{1,0:T(8,128)(2,1)} %refs_0_.1, s32[2]{0:T(128)} %refs_1_.1, bf16[512,768]{1,0:T(8,128)(2,1)} %refs_2_.1, ...), custom_call_target="tpu_custom_call" | custom-call | tf_op jit(solution)/shard_map/pallas_call | solution.py:996
  159.7 3.6 %shard_map.255 = (bf16[512,768]{1,0:T(8,128)(2,1)}, bf16[512,768]{1,0:T(8,128)(2,1)}, f32[96]{0:T(128)}, f32[96]{0:T(128)}, f32[3,96,192]{2,1,0:T(8,128)}, /*ind...) custom-call(bf16[512,768]{1,0:T(8,128)(2,1)} %get-tuple-element.35.b, ...), custom_call_target="tpu_custom_call" | custom-call | tf_op jit(solution)/shard_map/pallas_call | solution.py:1009

commit v3 on v2

--- a/solution.py
+++ b/solution.py
@@ -13,7 +13,7 @@
 EPSILON = 1e-05
 HD = 64
 GROUPS, ZN, XN = 8, 4, 2
-SEMS = 200
+SEMS = 224
 VEC = 16
 
 GAIN1, SHIFT1, QKVB, OUTB, GAIN2, SHIFT2, PROJB, FCB = 0, 1, 2, 8, 9, 10, 11, 12
@@ -35,16 +35,16 @@
     (
         tok_h, prefix_s, cot_h, gain1_h, shift1_h, wq_h, qvb_h, wo_h, outb_h,
         gain2_h, shift2_h, wf_h, fcb_h, wp_h, projb_h,
-        bo_h, ig_h, gq_ref, go_ref, gf_ref, gp_ref, vo_ref,
-        Wq, Wo, Wf, Wp, Go, Gp,
+        bo_h, ig_h, gq_ref, go_ref, gf_h, gp_h, vo_ref,
+        Wq, Wo, Wf, Wp, Go, Gp, Gf,
         RqA1, RqB1, RqA2, RqB2, Rq3,
         RfA1, RfB1, RfA2, RfB2, Rf3,
         RpA1, RpB1, RpA2, RpB2, RpA3, RpB3,
         Ro1, Ro2, Ro3,
-        TOK, COT, N1F, N2F, RS1, RS2, N1, N2, T0, T1,
-        QP, KP, VP, CTX, DO, DQ, LSEC, LSER, DELR,
-        MID, S0, V0, V1, H, GPR, PG,
-        SV, SB, SC, SQ, SO, SF, SP, SW,
+        TOK, COT, N1F, N2F, RS, N1, N2, T0, T1,
+        QP, KP, VP, CTX, DO, DQ, LSER, DELR,
+        MID, V0, V1, H, GPR, PG,
+        SV, SB, SC, SQ, SW, CTXP, WOP,
         VR, VF, VG, VZ, VO,
         ss, rs, ls,
     ) = refs
@@ -103,6 +103,7 @@
     for d in peers:
         pl.semaphore_signal(barrier, inc=1, device_id=d, device_id_type=MESH)
 
+    SO, SF, SP = (GPR.at[0, pl.ds(i * wo_h.shape[0], wo_h.shape[0])] for i in range(3))
     brought = [
         (wq_h, SQ), (qvb_h, SB), (fcb_h, SC.at[0]),
         (gain1_h, SV.at[0]), (shift1_h, SV.at[1]), (outb_h, SV.at[2]),
@@ -155,7 +156,9 @@
         (pl.ds(2 * third, 2 * third), pl.ds(4 * third, 2 * third)),
     )
 
-    def gather(W):
+    thin = [(pl.ds(2 * i * third, third), pl.ds((2 * i + 1) * third, third)) for i in range(3)]
+
+    def gather(W, pairs):
         steps = []
         for a, b in pairs:
             zs = [copy(W.at[y, z, x, r], W.at[y, z, x, r], zdev(k)) for k in range(1, ZN) for r in (a, b)]
@@ -193,7 +196,7 @@
             [copy(Wo.at[:, :, y], Wo.at[:, :, y], ydev)],
         )
     ]
-    qw, pw, fw = gather(Wq), gather_wide(Wp), gather(Wf)
+    qw, pw, fw = gather(Wq, thin), gather_wide(Wp), gather(Wf, thin)
 
     def z_go(w, i):
         start(w[i][0])
@@ -203,8 +206,10 @@
         start(w[i][1])
 
     def two_go(w, i):
-        landed(w[i][1])
-        start(w[i][2])
+        n = len(w[i][1]) // len(w[i][2])
+        for k, after in enumerate(w[i][2]):
+            landed(w[i][1][k * n : (k + 1) * n])
+            start([after])
 
     def all_in(w):
         for step in w:
@@ -231,9 +236,10 @@
         v = v - jnp.mean(v, axis=-1, keepdims=True)
         rstd = lax.rsqrt(jnp.mean(v * v, axis=-1, keepdims=True) + EPSILON)
         N1F[r, :] = v * rstd
-        RS1[r, :] = jnp.broadcast_to(rstd, (128, 128))
+        RS[r, 0:1] = rstd
 
     landed(vec_c)
+    z_go(qw, 1)
 
     def widen(v):
         return jnp.concatenate([v, jnp.zeros((v.shape[0], width - v.shape[1]), FULL)], axis=1)
@@ -273,7 +279,6 @@
 
     n1_c = [copy(N1.at[c], N1.at[c], cdev)]
     start(n1_c)
-    landed(cot_c)
 
     def transpose_all(source, target):
         @pl.loop(0, nrb)
@@ -284,20 +289,22 @@
             for k in range(width // rblk):
                 target[k * rblk : (k + 1) * rblk, cols] = source[h, rows, k * rblk : (k + 1) * rblk].T
 
+    landed(cot_c)
     one_go(qw, 0)
-    z_go(qw, 1)
     transpose_all(COT, T0)
+    one_go(qw, 1)
+    z_go(qw, 2)
     two_go(qw, 0)
     z_go(fw, 0)
-    one_go(qw, 1)
+    two_go(qw, 1)
+    z_go(ow, 0)
+    one_go(qw, 2)
     z_go(fw, 1)
-    z_go(ow, 0)
     landed(n1_c)
-    two_go(qw, 1)
-    one_go(pw, 0)
+    two_go(qw, 2)
+    z_go(fw, 2)
     one_go(fw, 0)
     all_in(qw)
-    one_go(pw, 1)
 
     def low_lanes(v):
         return lax.broadcasted_iota(jnp.int32, v.shape, 1) < HD
@@ -326,7 +333,18 @@
         KP[2, out, :] = jnp.where(first, roll(tile(got[0], 3)), tile(got[1], 3)).astype(LOW)
         VP[2, out, :] = jnp.where(first, tile(got[0], 4), roll(tile(got[1], 4))).astype(LOW)
 
+        @pl.when(i == 0)
+        def _():
+            one_go(ow, 0)
+            one_go(fw, 1)
+            one_go(pw, 0)
+
+        @pl.when(i == 2)
+        def _():
+            two_go(fw, 0)
+
     prefix = prefix_s[y]
+    LSEC = DQ
     LSEC[...] = jnp.zeros(LSEC.shape, FULL)
 
     def lane_part(v, e):
@@ -336,18 +354,33 @@
 
     def meanwhile(p, b, plan):
         for (pp, bb), steps in plan.items():
-            if bb == b:
+            if bb != b:
+                continue
+            if isinstance(p, int):
+                for step in steps:
+                    step()
+            else:
 
                 @pl.when(p == pp)
                 def _(steps=steps):
                     for step in steps:
                         step()
 
+    ctx_c = [copy(CTX.at[p, pl.ds(oc * half, half)], CTXP.at[p], cdev) for p in range(3)]
+    wo_c = [copy(Wo, WOP, cdev)]
+
+    def share_out():
+        all_in(ow)
+        start(wo_c)
+
     fetch = {
-        (0, 0): [lambda: one_go(fw, 1), lambda: one_go(ow, 0)],
-        (0, 1): [lambda: two_go(fw, 0)],
-        (1, 1): [lambda: two_go(fw, 1), lambda: two_go(ow, 0)],
-        (2, 1): [lambda: two_go(pw, 0)],
+        (0, 0): [lambda: one_go(fw, 2), lambda: two_go(ow, 0)],
+        (0, 1): [lambda: two_go(fw, 1), lambda: one_go(pw, 1)],
+        (0, 3): [lambda: start(ctx_c[0:1])],
+        (1, 2): [lambda: two_go(fw, 2)],
+        (1, 3): [lambda: start(ctx_c[1:2]), lambda: two_go(pw, 0)],
+        (2, 1): [share_out],
+        (2, 3): [lambda: start(ctx_c[2:3])],
     }
 
     @pl.loop(0, 3)
@@ -377,12 +410,10 @@
         lt = LSEC[b * rblk : (b + 1) * rblk, :].T
         for h in range(6):
             LSER[h, :, b * rblk : (b + 1) * rblk] = lt[h : h + 1, :]
-    all_in(ow)
-
     def wide(ref, rows):
         return jnp.concatenate([ref[0, rows, :], ref[1, rows, :], ref[2, rows, :]], axis=1)
 
-    def split_rows(make_block, away, home, copies):
+    def split_rows(make_block, away, home, copies, plus=None):
         per = half // rblk
         for which, target in ((oc, away), (c, home)):
 
@@ -390,35 +421,38 @@
             def _(j):
                 rows = pl.ds(pl.multiple_of(j * rblk, rblk), rblk)
                 flat = pl.ds(pl.multiple_of((which * per + j) * rblk, rblk), rblk)
-                target[rows, :] = make_block(which, rows, flat)
+                block = make_block(which, rows, flat)
+                target[rows, :] = block if plus is None or target is away else block + plus[rows, :]
 
             if target is away:
                 start(copies)
 
-    po_c = [copy(S0, V0, cdev)]
-    split_rows(
-        lambda h, rows, flat: dot_nt(wide(CTX, flat), Wo[...].reshape(width, Wo.shape[-1])), S0, MID, po_c
-    )
-    two_go(pw, 1)
-    landed(po_c)
-
-    @pl.loop(0, half // 128)
-    def _(i):
-        r = row_tile(i)
-        m = TOK[r, :].astype(FULL) + (MID[r, :] + V0[r, :] + vrow(OUTB))
+    parts = [GPR.at[b, pl.ds(i * half, half)] for b in range(2) for i in range(2)]
+    landed(wo_c)
+    landed(ctx_c)
+
+    @pl.loop(0, half // rblk)
+    def _(j):
+        r = pl.ds(pl.multiple_of(j * rblk, rblk), rblk)
+        flat = pl.ds(pl.multiple_of((c * (half // rblk) + j) * rblk, rblk), rblk)
+        o = dot_nt(wide(CTX, flat), Wo[...].reshape(width, Wo.shape[-1]))
+        o = o + dot_nt(wide(CTXP, r), WOP[...].reshape(width, Wo.shape[-1]))
+        m = TOK[r, :].astype(FULL) + (o + vrow(OUTB))
         MID[r, :] = m
         v = m - jnp.mean(m, axis=-1, keepdims=True)
         rstd = lax.rsqrt(jnp.mean(v * v, axis=-1, keepdims=True) + EPSILON)
         n = v * rstd
         N2F[r, :] = n
-        RS2[r, :] = jnp.broadcast_to(rstd, (128, 128))
+        RS[r, 1:2] = rstd
         N2[c, r, :] = (n * vrow(GAIN2) + vrow(SHIFT2)).astype(LOW)
 
     n2_c = [copy(N2.at[c], N2.at[c], cdev)]
     start(n2_c)
+    two_go(pw, 1)
     landed(n2_c)
     all_in(fw)
 
+    parts = [GPR.at[b, pl.ds(i * half, half)] for b in range(2) for i in range(2)]
     root = math.sqrt(2.0 / math.pi)
 
     @pl.loop(0, nrb * 2)
@@ -429,9 +463,9 @@
         flat = pl.ds(pl.multiple_of(i * rblk, rblk), rblk)
         u = dot(N2[h, rows, :], Wf[b].reshape(width, width)) + VF[pl.ds(FCB + b, 1), :]
         uu = u * u
-        th = jnp.tanh(root * u * (1.0 + 0.044715 * uu))
-        H[b, flat, :] = (0.5 * u * (1.0 + th)).astype(LOW)
-        GPR[b, flat, :] = 0.5 * (1.0 + th) + (0.5 * root) * u * (1.0 - th * th) * (1.0 + 0.134145 * uu)
+        a = 0.5 * jnp.tanh(u * (root + (root * 0.044715) * uu)) + 0.5
+        H[b, flat, :] = (u * a).astype(LOW)
+        GPR[b, flat, :] = a * (1.0 + (1.0 - a) * (u * (2.0 * root + (2.0 * root * 0.134145) * uu)))
 
     def weight_grad(left_t, right, G, first, last):
         @pl.loop(0, 4)
@@ -567,10 +601,19 @@
 
     rp = reduce_wide(Gp, by_rows, RpA1, RpB1, RpA2, RpB2, RpA3, RpB3)
     weight_grad(T0, H, Gp, 0, width)
+    rp[0](0)
     transpose_all(N2, T1)
     all_in(pw)
-    rp[0](0)
     rp[0](1)
+
+
+    def pair_nt(A, W, columns):
+        def block(h, rows, flat):
+            return dot_nt(A[0, flat, :columns], W[0].reshape(width, W.shape[-1])) + dot_nt(
+                A[1, flat, :columns], W[1].reshape(width, W.shape[-1])
+            )
+
+        return block
 
     @pl.loop(0, nrb * 2)
     def _(k):
@@ -582,26 +625,11 @@
         PG[b, flat, :] = g
         VG[pl.ds(FCB + b, 1), :] += jnp.sum(g.astype(FULL), axis=0, keepdims=True)
 
-    p2_c = [copy(S0, V1, cdev)]
-    home2, homem, home1 = GPR.at[0, pl.ds(0, half)], GPR.at[0, pl.ds(half, half)], GPR.at[1, pl.ds(0, half)]
-    awaym = GPR.at[1, pl.ds(half, half)]
-
-    def pair_nt(A, W, columns):
-        def block(h, rows, flat):
-            return dot_nt(A[0, flat, :columns], W[0].reshape(width, W.shape[-1])) + dot_nt(
-                A[1, flat, :columns], W[1].reshape(width, W.shape[-1])
-            )
-
-        return block
-
-    sent(po_c)
-    split_rows(pair_nt(PG, Wf, width), S0, home2, p2_c)
-    pm_c = [copy(awaym, V0, cdev)]
-    split_rows(pair_nt(H, Wp, width), awaym, homem, pm_c)
-    sent_all(pw)
+    p2_c = [copy(parts[3], V1, cdev)]
+    split_rows(pair_nt(PG, Wf, width), parts[3], parts[0], p2_c)
     rp[1](0)
-    weight_grad(T1, PG, Wp, 0, width)
-    rf = reduce_copies(Wp, by_rows, RfA1, RfB1, RfA2, RfB2, Rf3)
+    weight_grad(T1, PG, Gf, 0, width)
+    rf = reduce_copies(Gf, by_rows, RfA1, RfB1, RfA2, RfB2, Rf3)
     rf[0](0)
     rf[0](1)
     landed(p2_c)
@@ -624,7 +652,7 @@
         add_row(SHIFT2, dy)
         cot = COT[c, r, :].astype(FULL)
         add_row(PROJB, cot)
-        g = cot + norm_back(dy, n, RS2[r, 0:1], vrow(GAIN2))
+        g = cot + norm_back(dy, n, RS[r, 1:2], vrow(GAIN2))
         N2F[r, :] = g
         low = g.astype(LOW)
         add_row(OUTB, low.astype(FULL))
@@ -651,21 +679,22 @@
         for core in range(2):
             vo_ref[core, r, :] = VO[0, core, r, :] + VO[1, core, r, :] + VO[2, core, r, :] + VO[3, core, r, :]
 
-    late, early = vector_copies(0, 8), vector_copies(8, VEC)
+    late, early = vector_copies(0, 4), vector_copies(8, VEC)
     start(early[1])
+    pm_c = [copy(parts[1], V0, cdev)]
+    split_rows(pair_nt(H, Wp, width), parts[1], MID, pm_c, MID)
+    rp[1](1)
     transpose_all(N1, T1)
-    rp[1](1)
+    landed(ag_c)
     landed(pm_c)
 
     @pl.loop(0, half // 128)
     def _(i):
         r = row_tile(i)
-        far = row_tile(i + half // 128)
-        TOK[r, :] = (MID[r, :] + (GPR[0, far, :] + V0[r, :] + vrow(PROJB))).astype(LOW)
+        TOK[r, :] = (MID[r, :] + (V0[r, :] + vrow(PROJB))).astype(LOW)
 
     out_c = [pltpu.make_async_copy(TOK, bo_h, ls.at[0]), pltpu.make_async_copy(N1.at[c], ig_h, ls.at[1])]
     out_c[0].start()
-    landed(ag_c)
 
     @pl.loop(0, nrb)
     def _(i):
@@ -757,11 +786,10 @@
         QP[p, :, :] = (DQ[...] * 0.125).astype(LOW)
 
     away = {
-        (0, 3): [lambda: rf[1](0), ro_second],
-        (1, 2): [lambda: rf[1](1), ro_third],
-        (2, 0): [lambda: rp[2](0)],
-        (2, 1): [lambda: rf[2](0)],
-        (2, 3): [lambda: rf[2](1)],
+        (0, 0): [lambda: rf[1](0)],
+        (1, 0): [lambda: rf[1](1)],
+        (1, 1): [lambda: rf[2](0)],
+        (1, 2): [ro_second],
     }
 
     @pl.loop(0, 2)
@@ -780,11 +808,17 @@
                 H[b, flat, k * 128 : (k + 1) * 128] = g
                 VG[QKVB + b : QKVB + b + 1, k * 128 : (k + 1) * 128] += jnp.sum(g.astype(FULL), axis=0, keepdims=True)
 
-    both = (pl.ds(0, hr), pl.ds(hr, hr), pl.ds(0, hr))
-    by_lanes = [both + (pl.ds(0, 384),), both + (pl.ds(384, packed - 384),)]
+    by_lanes = [(pl.ds(0, hr), pl.ds(hr, hr), pl.ds(0, hr), pl.ds(0, 384))]
+    rest = pl.ds(384, packed - 384)
+    by_lanes += [pairs[1] + (pl.ds(third, 2 * third), rest), pairs[0] + (pl.ds(0, third), rest)]
     weight_grad(T1, H, Wf, 0, 384)
     rq = reduce_copies(Wf, by_lanes, RqA1, RqB1, RqA2, RqB2, Rq3)
     rq[0](0)
+    away = {
+        (2, 0): [lambda: rp[2](0), lambda: rf[2](1)],
+        (2, 1): [ro_third],
+        (2, 3): [lambda: rq[1](0)],
+    }
     attention_back(2, away)
 
     @pl.loop(0, nrb)
@@ -804,13 +838,12 @@
 
     weight_grad(T1, H, Wf, 384, packed)
     rq[0](1)
-
-    p1_c = [copy(S0, V1, cdev)]
-    sent(p2_c)
-    split_rows(pair_nt(H, Wq, packed), S0, home1, p1_c)
-    rq[1](0)
+    rq[0](2)
+
+    p1_c = [copy(parts[1], V1, cdev)]
+    sent(pm_c)
+    split_rows(pair_nt(H, Wq, packed), parts[1], parts[2], p1_c)
     rp[2](1)
-    vector_second(early)
     landed(p1_c)
 
     sent(n1_c)
@@ -822,31 +855,38 @@
         n = N1F[r, :]
         add_row(GAIN1, dy * n)
         add_row(SHIFT1, dy)
-        N1[c, r, :] = (N2F[r, :] + norm_back(dy, n, RS1[r, 0:1], vrow(GAIN1))).astype(LOW)
+        N1[c, r, :] = (N2F[r, :] + norm_back(dy, n, RS[r, 0:1], vrow(GAIN1))).astype(LOW)
 
     out_c[1].start()
 
     start(late[1])
+    rq[2](0)
+    vector_second(early)
     rq[1](1)
-    rq[2](0)
+    rq[1](2)
     ro_last()
-    vector_second(late)
+    gp_ref, gf_ref = MID.at[pl.ds(0, 2 * hr)], MID.at[pl.ds(2 * hr, 2 * hr)]
+    out_c += [pltpu.make_async_copy(gp_ref, gp_h, ls.at[2]), pltpu.make_async_copy(gf_ref, gf_h, ls.at[3])]
     rp[3](0, gp_ref)
     rp[3](1, gp_ref)
-    rq[2](1)
+    out_c[2].start()
     rf[3](0, gf_ref)
     rf[3](1, gf_ref)
+    out_c[3].start()
+    rq[2](1)
+    rq[2](2)
+    vector_second(late)
     vector_last(early)
     landed(ro[3])
     rq[3](0, gq_ref)
     vector_last(late)
     rq[3](1, gq_ref)
-
-    waited = {id(m) for m in po_c + n2_c + p2_c + n1_c}
-    for w in (pw, fw):
-        for step in w:
-            for group in step:
-                waited |= {id(m) for m in group}
+    rq[3](2, gq_ref)
+
+    waited = {id(m) for m in n2_c + pm_c + n1_c}
+    for step in fw:
+        for group in step:
+            waited |= {id(m) for m in group}
     sent([m for m in made if id(m) not in waited])
     for cp in out_c:
         cp.wait()
@@ -925,6 +965,7 @@
             pltpu.VMEM((2, ZN, XN, rows, width), LOW),
             pltpu.VMEM((2, ZN, XN, rows, width), LOW),
             pltpu.VMEM((ZN, XN, 2, hr, own), LOW),
+            pltpu.VMEM((2, ZN, XN, rows, width), LOW),
             pltpu.VMEM((2, ZN, XN, rows, width), LOW),
         ]
         + reduce_space(packed)
@@ -948,7 +989,6 @@
             token_full,
             token_full,
             pltpu.VMEM((half, 128), FULL),
-            pltpu.VMEM((half, 128), FULL),
             token_low,
             token_low,
             pltpu.VMEM((width, seq_len), LOW),
@@ -957,21 +997,19 @@
         + [heads] * 5
         + [
             pltpu.VMEM((seq_len, pair), FULL),
-            pltpu.VMEM((seq_len, 128), FULL),
             pltpu.VMEM((6, 1, seq_len), FULL),
             pltpu.VMEM((6, 1, seq_len), FULL),
         ]
-        + [token_full] * 4
+        + [token_full] * 3
         + [unit_low, pltpu.VMEM((2, seq_len, width), FULL), unit_low]
         + [
             pltpu.VMEM((8, rows), FULL),
             pltpu.VMEM((2, rows), FULL),
             pltpu.VMEM((1, 4 * rows), FULL),
             pltpu.VMEM((3, rows, cols), FULL),
-            pltpu.VMEM((rows, width), FULL),
-            pltpu.VMEM((rows, units), FULL),
-            pltpu.VMEM((rows, units), FULL),
             pltpu.VMEM((2, hr, own), LOW),
+            pltpu.VMEM((3, half, pair), LOW),
+            pltpu.VMEM((ZN, XN, 2, hr, own), LOW),
             pltpu.VMEM((GROUPS, VEC, 128), LOW),
             pltpu.VMEM((VEC, width), FULL),
             pltpu.VMEM((VEC, width), FULL),
@@ -997,7 +1035,7 @@
         functools.partial(block_kernel, repeat, seq_len),
         out_shape=out_shape,
         in_specs=[ANY, pl.BlockSpec(memory_space=pltpu.SMEM)] + [ANY] * 13,
-        out_specs=[ANY] * 2 + [IN_VMEM] * 5,
+        out_specs=[ANY] * 2 + [IN_VMEM] * 2 + [ANY] * 2 + [IN_VMEM],
         scratch_shapes=scratch,
         compiler_params=pltpu.CompilerParams(
             collective_id=0, has_side_effects=True, vmem_limit_bytes=62 * 1024 * 1024

time: 165 us -> 149 us (0.903)
  Pallas kernels: 163 us -> 148 us
    pallas_call x1, Pallas kernels: 159 us -> 144 us  [on_device(): pl.pallas_call(functools.partial(block_kernel, repeat, seq_len), out_shap...]
where the time goes in v3:
time: 149 us
  Pallas kernels  148 us (99%)
    pallas_call x1, Pallas kernels, on_device(): pl.pallas_call(functools.partial(block_kernel, repeat, seq_len), out_shap...  144 us
    pallas_call x1, Pallas kernels, on_device(): pl.pallas_call(functools.partial(unpack_kernel, repeat), out_shape=[out_s...  3.64 us

profile of v3, /device:TPU:0, one launch (start us, length us, event | category | flops | bytes accessed | tf_op | source)
XLA Modules:
  0.0 148.9 jit_solution(12897657237844847287)
XLA Ops:
  0.7 144.4 %shard_map.254 = (bf16[512,768]{1,0:T(8,128)(2,1)}, bf16[512,768]{1,0:T(8,128)(2,1)}, f32[96,640]{1,0:T(8,128)}, f32[4,48,384]{2,1,0:T(8,128)}, f32[96,768]{1,0:...) custom-call(bf16[512,768]{1,0:T(8,128)(2,1)} %refs_0_.1, s32[2]{0:T(128)} %refs_1_.1, bf16[512,768]{1,0:T(8,128)(2,1)} %refs_2_.1, ...), custom_call_target="tpu_custom_call" | custom-call | tf_op jit(solution)/shard_map/pallas_call | solution.py:1034
  145.1 3.6 %shard_map.255 = (bf16[512,768]{1,0:T(8,128)(2,1)}, bf16[512,768]{1,0:T(8,128)(2,1)}, f32[96]{0:T(128)}, f32[96]{0:T(128)}, f32[3,96,192]{2,1,0:T(8,128)}, /*ind...) custom-call(bf16[512,768]{1,0:T(8,128)(2,1)} %get-tuple-element.35.b, ...), custom_call_target="tpu_custom_call" | custom-call | tf_op jit(solution)/shard_map/pallas_call | solution.py:1047

commit v4 on v3

--- a/solution.py
+++ b/solution.py
@@ -13,7 +13,7 @@
 EPSILON = 1e-05
 HD = 64
 GROUPS, ZN, XN = 8, 4, 2
-SEMS = 224
+SEMS = 134
 VEC = 16
 
 GAIN1, SHIFT1, QKVB, OUTB, GAIN2, SHIFT2, PROJB, FCB = 0, 1, 2, 8, 9, 10, 11, 12
@@ -33,19 +33,19 @@
 
 def block_kernel(repeat, seq_len, *refs):
     (
-        tok_h, prefix_s, cot_h, gain1_h, shift1_h, wq_h, qvb_h, wo_h, outb_h,
+        tok_h, prefix_h, cot_h, gain1_h, shift1_h, wq_h, qvb_h, wo_h, outb_h,
         gain2_h, shift2_h, wf_h, fcb_h, wp_h, projb_h,
-        bo_h, ig_h, gq_ref, go_ref, gf_h, gp_h, vo_ref,
+        bo_h, ig_h, gq_h, go_h, gf_h, gp_h, vo_h,
         Wq, Wo, Wf, Wp, Go, Gp, Gf,
         RqA1, RqB1, RqA2, RqB2, Rq3,
         RfA1, RfB1, RfA2, RfB2, Rf3,
-        RpA1, RpB1, RpA2, RpB2, RpA3, RpB3,
+        RpA1, RpB1, RpA2, RpB2, RpA3, RpB3, RpEA, RpEB,
         Ro1, Ro2, Ro3,
         TOK, COT, N1F, N2F, RS, N1, N2, T0, T1,
         QP, KP, VP, CTX, DO, DQ, LSER, DELR,
         MID, V0, V1, H, GPR, PG,
         SV, SB, SC, SQ, SW, CTXP, WOP,
-        VR, VF, VG, VZ, VO,
+        VR, VF, VG, VZ, VO, gq_ref, go_ref, vo_ref, prefix_s,
         ss, rs, ls,
     ) = refs
     half = seq_len // 2
@@ -72,31 +72,146 @@
     near = [xdev, ydev, cdev, gdev] + [at(z, ox, i * 2 + j) for i, j in ((y, oc), (oy, c), (oy, oc))]
     others = [(((s + k) % GROUPS) * repeat + sub, t) for k in range(1, GROUPS)]
 
-    made = []
-
-    def copy(src, dst, dev):
-        k = len(made)
-
-        def make():
+    count = [0]
+    pending = []
+
+    class Copy:
+        def __init__(self, src, dst, dev, recv=None, alone=True):
+            self.k = count[0]
+            count[0] += 1
+            self.parts = src, dst, dev, self.k if recv is None else recv.k
+            if alone:
+                pending.append(self)
+
+        def made(self):
+            src, dst, dev, recv = self.parts
             return pltpu.make_async_remote_copy(
-                src_ref=src, dst_ref=dst, send_sem=ss.at[k], recv_sem=rs.at[k],
+                src_ref=src, dst_ref=dst, send_sem=ss.at[self.k], recv_sem=rs.at[recv],
                 device_id=dev, device_id_type=MESH,
             )
 
-        made.append(make)
-        return make
-
-    def start(makes):
-        for m in makes:
-            m().start()
-
-    def landed(makes):
-        for m in makes:
-            m().wait_recv()
-
-    def sent(makes):
-        for m in makes:
-            m().wait_send()
+        def start(self):
+            self.made().start()
+
+        def landed(self):
+            self.made().wait_recv()
+
+        def sent(self):
+            self.made().wait_send()
+
+    class Group:
+        def __init__(self, moves, every):
+            k = count[0]
+            count[0] += 1
+            self.moves = [Copy(*m, alone=False) for m in moves]
+            for m in self.moves:
+                m.k, m.parts = k, m.parts[:3] + (k,)
+            count[0] = k + 1
+            self.every = Copy(every, every, moves[0][2], alone=False)
+            self.every.k, self.every.parts = k, self.every.parts[:3] + (k,)
+            count[0] = k + 1
+            pending.append(self)
+
+        def start(self):
+            for m in self.moves:
+                m.start()
+
+        def landed(self):
+            self.every.landed()
+
+        def sent(self):
+            self.every.sent()
+
+    class ZGather:
+        def __init__(self, block):
+            self.to = [Copy(block(z), block(z), zdev(k), alone=False) for k in range(1, ZN)]
+            self.up = Copy(block(0), block(0), at(3, x, t), self.to[2], False)
+            self.down = Copy(block(3), block(3), at(0, x, t), self.to[0], False)
+            pending.append(self)
+
+        def each(self, act):
+            act(self.to[1])
+            pl.when(z != 3)(lambda: act(self.to[0]))
+            pl.when(z != 0)(lambda: act(self.to[2]))
+
+        def start(self):
+            self.each(lambda m: m.start())
+
+        def middle(self):
+            def go_on(onward):
+                landed(self.to[1:2])
+                onward.start()
+
+            pl.when(z == 2)(lambda: go_on(self.up))
+            pl.when(z == 1)(lambda: go_on(self.down))
+
+        def landed(self):
+            pl.when((z == 0) | (z == 3))(self.to[1].landed)
+            self.to[0].landed()
+            self.to[2].landed()
+
+        def sent(self):
+            self.each(lambda m: m.sent())
+            pl.when(z == 2)(self.up.sent)
+            pl.when(z == 1)(self.down.sent)
+
+    class ZReduce:
+        def __init__(self, block, arrived, extra):
+            self.block, self.extra = block, extra
+            self.to = [Copy(block((z + k) % ZN), arrived(k - 1), zdev(k), alone=False) for k in range(1, ZN)]
+            self.up = Copy(block(3), extra, at(1, x, t), alone=False)
+            self.down = Copy(block(0), extra, at(2, x, t), alone=False)
+            pending.append(self)
+
+            def none(slot):
+                arrived(slot)[...] = jnp.zeros(extra.shape, LOW)
+
+            pl.when(z == 0)(lambda: none(0))
+            pl.when(z == 3)(lambda: none(2))
+
+        def start(self):
+            pl.when(z != 3)(self.to[0].start)
+            pl.when(z != 0)(self.to[2].start)
+            pl.when(z == 0)(self.up.start)
+            pl.when(z == 3)(self.down.start)
+            pl.when((z == 0) | (z == 3))(self.to[1].start)
+
+        def middle(self):
+            def go_on(arrival, owner):
+                landed([arrival])
+                target = self.block(owner)
+                target[...] = (target[...].astype(FULL) + self.extra[...].astype(FULL)).astype(LOW)
+                self.to[1].start()
+
+            pl.when(z == 1)(lambda: go_on(self.up, 3))
+            pl.when(z == 2)(lambda: go_on(self.down, 0))
+
+        def landed(self):
+            self.to[1].landed()
+            pl.when(z != 0)(self.to[0].landed)
+            pl.when(z != 3)(self.to[2].landed)
+
+        def sent(self):
+            self.to[1].sent()
+            pl.when(z != 3)(self.to[0].sent)
+            pl.when(z != 0)(self.to[2].sent)
+            pl.when(z == 0)(self.up.sent)
+            pl.when(z == 3)(self.down.sent)
+
+    def copy(src, dst, dev):
+        return Copy(src, dst, dev)
+
+    def start(moves):
+        for m in moves:
+            m.start()
+
+    def landed(moves):
+        for m in moves:
+            m.landed()
+
+    def sent(moves):
+        for m in moves:
+            m.sent()
 
     barrier = pltpu.get_barrier_semaphore()
     peers = others + [d for i, d in enumerate(near) if i != 0]
@@ -109,6 +224,7 @@
         (gain1_h, SV.at[0]), (shift1_h, SV.at[1]), (outb_h, SV.at[2]),
         (gain2_h, SV.at[3]), (shift2_h, SV.at[4]), (projb_h, SV.at[5]),
         (wo_h, SO), (tok_h, TOK), (cot_h, COT.at[c]), (wf_h, SF), (wp_h, SP),
+        (prefix_h, prefix_s),
     ]
     local = [pltpu.make_async_copy(a, b, ls.at[i]) for i, (a, b) in enumerate(brought)]
     for cp in local:
@@ -132,6 +248,84 @@
         + [jnp.zeros((q3.shape[1], HD), FULL)],
         axis=1,
     ).astype(LOW)
+    pl.semaphore_wait(barrier, len(peers))
+
+    vec_c = [Group([(VR.at[s], VR.at[s], d) for d in others], VR.at[pl.ds(0, GROUPS - 1)])]
+    cot_c = [copy(COT.at[c], COT.at[c], cdev)]
+    hr = wq_h.shape[1] // 2
+    third = hr // 3
+    pairs = (
+        (pl.ds(0, third), pl.ds(third, third)),
+        (pl.ds(2 * third, 2 * third), pl.ds(4 * third, 2 * third)),
+    )
+
+    thin = [(pl.ds(2 * i * third, third), pl.ds((2 * i + 1) * third, third)) for i in range(3)]
+
+    def gather(W, pairs):
+        steps = []
+        for a, b in pairs:
+            r = pl.ds(a.start, a.size + b.size)
+            mine = W.at[y, z, x, r]
+            zs = [Group([(mine, mine, zdev(k)) for k in range(1, ZN)], W.at[y, pl.ds(0, ZN - 1), x, r])]
+            one = [
+                copy(W.at[y, :, x, a], W.at[y, :, x, a], xdev),
+                copy(W.at[y, :, x, b], W.at[y, :, x, b], ydev),
+            ]
+            two = [
+                copy(W.at[y, :, :, a], W.at[y, :, :, a], ydev),
+                copy(W.at[:, :, x, b], W.at[:, :, x, b], xdev),
+            ]
+            steps.append((zs, one, two))
+        return steps
+
+    def gather_wide(W):
+        steps = []
+        for a, b in pairs:
+            near = [
+                copy(W.at[y, z, x, a], W.at[y, z, x, a], xdev),
+                copy(W.at[y, z, x, b], W.at[y, z, x, b], ydev),
+            ]
+            zs = [ZGather(lambda i, a=a: W.at[y, i, :, a]), ZGather(lambda i, b=b: W.at[:, i, x, b])]
+            far = [
+                copy(W.at[y, :, :, a], W.at[y, :, :, a], ydev),
+                copy(W.at[:, :, x, b], W.at[:, :, x, b], xdev),
+            ]
+            steps.append((near, zs, far))
+        return steps
+
+    ow = [
+        (
+            [Group([(Wo.at[z, x, y], Wo.at[z, x, y], zdev(k)) for k in range(1, ZN)], Wo.at[pl.ds(0, ZN - 1), x, y])],
+            [copy(Wo.at[:, x, y], Wo.at[:, x, y], xdev)],
+            [copy(Wo.at[:, :, y], Wo.at[:, :, y], ydev)],
+        )
+    ]
+    qw, pw, fw = gather(Wq, thin), gather_wide(Wp), gather(Wf, thin)
+
+    def z_go(w, i):
+        start(w[i][0])
+
+    def one_go(w, i):
+        landed(w[i][0])
+        start(w[i][1])
+
+    def two_go(w, i):
+        n = len(w[i][1]) // len(w[i][2])
+        for k, after in enumerate(w[i][2]):
+            landed(w[i][1][k * n : (k + 1) * n])
+            start([after])
+
+    def all_in(w):
+        for step in w:
+            landed(step[2])
+
+    def sent_all(w):
+        for step in w:
+            for group in step:
+                sent(group)
+
+    start(vec_c)
+    z_go(qw, 0)
     local[9].wait()
     turned = pltpu.roll(SO[...], (width - c * (width // 4)) % width, 1)
     last = jnp.concatenate([turned[:, 128:192], turned[:, 512:576]], axis=1)
@@ -145,83 +339,7 @@
     Wp[y, z, x] = SP[...].astype(LOW)
     local[10].wait()
     local[11].wait()
-    pl.semaphore_wait(barrier, len(peers))
-
-    vec_c = [copy(VR.at[s], VR.at[s], d) for d in others]
-    cot_c = [copy(COT.at[c], COT.at[c], cdev)]
-    hr = wq_h.shape[1] // 2
-    third = hr // 3
-    pairs = (
-        (pl.ds(0, third), pl.ds(third, third)),
-        (pl.ds(2 * third, 2 * third), pl.ds(4 * third, 2 * third)),
-    )
-
-    thin = [(pl.ds(2 * i * third, third), pl.ds((2 * i + 1) * third, third)) for i in range(3)]
-
-    def gather(W, pairs):
-        steps = []
-        for a, b in pairs:
-            zs = [copy(W.at[y, z, x, r], W.at[y, z, x, r], zdev(k)) for k in range(1, ZN) for r in (a, b)]
-            one = [
-                copy(W.at[y, :, x, a], W.at[y, :, x, a], xdev),
-                copy(W.at[y, :, x, b], W.at[y, :, x, b], ydev),
-            ]
-            two = [
-                copy(W.at[y, :, :, a], W.at[y, :, :, a], ydev),
-                copy(W.at[:, :, x, b], W.at[:, :, x, b], xdev),
-            ]
-            steps.append((zs, one, two))
-        return steps
-
-    def gather_wide(W):
-        steps = []
-        for a, b in pairs:
-            near = [
-                copy(W.at[y, z, x, a], W.at[y, z, x, a], xdev),
-                copy(W.at[y, z, x, b], W.at[y, z, x, b], ydev),
-            ]
-            zs = [copy(W.at[y, z, :, a], W.at[y, z, :, a], zdev(k)) for k in range(1, ZN)]
-            zs += [copy(W.at[:, z, x, b], W.at[:, z, x, b], zdev(k)) for k in range(1, ZN)]
-            far = [
-                copy(W.at[y, :, :, a], W.at[y, :, :, a], ydev),
-                copy(W.at[:, :, x, b], W.at[:, :, x, b], xdev),
-            ]
-            steps.append((near, zs, far))
-        return steps
-
-    ow = [
-        (
-            [copy(Wo.at[z, x, y], Wo.at[z, x, y], zdev(k)) for k in range(1, ZN)],
-            [copy(Wo.at[:, x, y], Wo.at[:, x, y], xdev)],
-            [copy(Wo.at[:, :, y], Wo.at[:, :, y], ydev)],
-        )
-    ]
-    qw, pw, fw = gather(Wq, thin), gather_wide(Wp), gather(Wf, thin)
-
-    def z_go(w, i):
-        start(w[i][0])
-
-    def one_go(w, i):
-        landed(w[i][0])
-        start(w[i][1])
-
-    def two_go(w, i):
-        n = len(w[i][1]) // len(w[i][2])
-        for k, after in enumerate(w[i][2]):
-            landed(w[i][1][k * n : (k + 1) * n])
-            start([after])
-
-    def all_in(w):
-        for step in w:
-            landed(step[2])
-
-    def sent_all(w):
-        for step in w:
-            for group in step:
-                sent(group)
-
-    start(vec_c)
-    z_go(qw, 0)
+    local[14].wait()
     z_go(pw, 0)
     z_go(pw, 1)
     start(cot_c)
@@ -238,8 +356,8 @@
         N1F[r, :] = v * rstd
         RS[r, 0:1] = rstd
 
+    z_go(qw, 1)
     landed(vec_c)
-    z_go(qw, 1)
 
     def widen(v):
         return jnp.concatenate([v, jnp.zeros((v.shape[0], width - v.shape[1]), FULL)], axis=1)
@@ -373,14 +491,20 @@
         all_in(ow)
         start(wo_c)
 
+    def pass_on(i):
+        for m in pw[i][1]:
+            m.middle()
+
     fetch = {
         (0, 0): [lambda: one_go(fw, 2), lambda: two_go(ow, 0)],
         (0, 1): [lambda: two_go(fw, 1), lambda: one_go(pw, 1)],
         (0, 3): [lambda: start(ctx_c[0:1])],
+        (1, 1): [lambda: pass_on(0)],
         (1, 2): [lambda: two_go(fw, 2)],
-        (1, 3): [lambda: start(ctx_c[1:2]), lambda: two_go(pw, 0)],
+        (1, 3): [lambda: start(ctx_c[1:2])],
+        (2, 0): [lambda: two_go(pw, 0)],
         (2, 1): [share_out],
-        (2, 3): [lambda: start(ctx_c[2:3])],
+        (2, 3): [lambda: start(ctx_c[2:3]), lambda: pass_on(1)],
     }
 
     @pl.loop(0, 3)
@@ -392,11 +516,13 @@
             keys, values = KP[p, :cols, :], VP[p, :cols, :]
             query = b * rblk + lax.broadcasted_iota(jnp.int32, (rblk, 1), 0)
             limit = jnp.maximum(prefix - 1, query)
-            key = lax.broadcasted_iota(jnp.int32, (rblk, cols), 1)
+            free = b * rblk
+            key = free + lax.broadcasted_iota(jnp.int32, (rblk, cols - free), 1)
             parts = []
             for e in range(2):
                 sc = dot_nt(lane_part(q, e), keys)
-                sc = jnp.where(key <= limit, sc, -1e30)
+                tail = jnp.where(key <= limit, sc[:, free:], -1e30)
+                sc = jnp.concatenate([sc[:, :free], tail], axis=1) if free else tail
                 peak = jnp.max(sc, axis=-1, keepdims=True)
                 w = jnp.exp(sc - peak)
                 total = jnp.sum(w, axis=-1, keepdims=True)
@@ -420,8 +546,7 @@
             @pl.loop(0, per)
             def _(j):
                 rows = pl.ds(pl.multiple_of(j * rblk, rblk), rblk)
-                flat = pl.ds(pl.multiple_of((which * per + j) * rblk, rblk), rblk)
-                block = make_block(which, rows, flat)
+                block = make_block(pl.ds(pl.multiple_of((which * per + j) * rblk, rblk), rblk))
                 target[rows, :] = block if plus is None or target is away else block + plus[rows, :]
 
             if target is away:
@@ -448,7 +573,6 @@
 
     n2_c = [copy(N2.at[c], N2.at[c], cdev)]
     start(n2_c)
-    two_go(pw, 1)
     landed(n2_c)
     all_in(fw)
 
@@ -457,6 +581,10 @@
 
     @pl.loop(0, nrb * 2)
     def _(k):
+        @pl.when(k == 1)
+        def _():
+            two_go(pw, 1)
+
         b, i = k // nrb, k % nrb
         h, off = i // (half // rblk), i % (half // rblk)
         rows = pl.ds(pl.multiple_of(off * rblk, rblk), rblk)
@@ -468,13 +596,10 @@
         GPR[b, flat, :] = a * (1.0 + (1.0 - a) * (u * (2.0 * root + (2.0 * root * 0.134145) * uu)))
 
     def weight_grad(left_t, right, G, first, last):
-        @pl.loop(0, 4)
-        def _(k):
-            b, m = k // 2, k % 2
-            rows = pl.ds(pl.multiple_of(m * (width // 2), width // 2), width // 2)
-            g = dot(left_t[rows, :], right[b, :, first:last])
-            g = g.astype(LOW).reshape(ZN // 2, XN, width // GROUPS, last - first)
-            G[b, pl.ds(m * (ZN // 2), ZN // 2), :, :, first:last] = g
+        @pl.loop(0, 2)
+        def _(b):
+            g = dot(left_t[...], right[b, :, first:last])
+            G[b, :, :, :, first:last] = g.astype(LOW).reshape(ZN, XN, width // GROUPS, last - first)
 
     every = pl.ds(0, width)
     by_rows = [pairs[0] + (pl.ds(0, third), every), pairs[1] + (pl.ds(third, 2 * third), every)]
@@ -490,10 +615,12 @@
                 copy(G.at[oy, :, x, a, cols], A2.at[:, r, cols], ydev),
                 copy(G.at[y, :, ox, b, cols], B2.at[:, r, cols], xdev),
             ]
+            q = pl.ds(a.start, a.size + b.size)
             three = [
-                copy(G.at[y, (z + k) % ZN, x, q, cols], R3.at[k - 1, q, cols], zdev(k))
-                for k in range(1, ZN)
-                for q in (a, b)
+                Group(
+                    [(G.at[y, (z + k) % ZN, x, q, cols], R3.at[k - 1, q, cols], zdev(k)) for k in range(1, ZN)],
+                    R3.at[:, q, cols],
+                )
             ]
             steps.append((a, b, r, cols, one, two, three))
 
@@ -547,15 +674,25 @@
 
         return go, second, third_step, last
 
-    def reduce_wide(G, plan, A1, B1, A2, B2, A3, B3):
+    def reduce_wide(G, plan, A1, B1, A2, B2, A3, B3, EA, EB):
         steps = []
         for a, b, r, cols in plan:
             one = [
                 copy(G.at[oy, :, :, a, cols], A1.at[:, :, r, cols], ydev),
                 copy(G.at[:, :, ox, b, cols], B1.at[:, :, r, cols], xdev),
             ]
-            two = [copy(G.at[y, (z + k) % ZN, :, a, cols], A2.at[k - 1, :, r, cols], zdev(k)) for k in range(1, ZN)]
-            two += [copy(G.at[:, (z + k) % ZN, x, b, cols], B2.at[k - 1, :, r, cols], zdev(k)) for k in range(1, ZN)]
+            two = [
+                ZReduce(
+                    lambda i, a=a, cols=cols: G.at[y, i, :, a, cols],
+                    lambda k, r=r, cols=cols: A2.at[k, :, r, cols],
+                    EA.at[:, r, cols],
+                ),
+                ZReduce(
+                    lambda i, b=b, cols=cols: G.at[:, i, x, b, cols],
+                    lambda k, r=r, cols=cols: B2.at[k, :, r, cols],
+                    EB.at[:, r, cols],
+                ),
+            ]
             three = [
                 copy(G.at[y, z, ox, a, cols], A3.at[r, cols], xdev),
                 copy(G.at[oy, z, x, b, cols], B3.at[r, cols], ydev),
@@ -582,6 +719,10 @@
                     add(G.at[j, k, x, b, cols], [B1.at[j, k, r, cols]])
 
             start(two)
+
+        def middle(i):
+            for m in steps[i][5]:
+                m.middle()
 
         def third_step(i):
             a, b, r, cols, one, two, three = steps[i]
@@ -597,9 +738,10 @@
             for q, R in ((a, A3), (b, B3)):
                 out[q, cols] = G[y, z, x, q, cols].astype(FULL) + R[r, cols].astype(FULL)
 
-        return go, second, third_step, last
-
-    rp = reduce_wide(Gp, by_rows, RpA1, RpB1, RpA2, RpB2, RpA3, RpB3)
+        return go, second, third_step, last, middle
+
+    rp = reduce_wide(Gp, by_rows, RpA1, RpB1, RpA2, RpB2, RpA3, RpB3, RpEA, RpEB)
+    rf = reduce_copies(Gf, by_rows, RfA1, RfB1, RfA2, RfB2, Rf3)
     weight_grad(T0, H, Gp, 0, width)
     rp[0](0)
     transpose_all(N2, T1)
@@ -608,20 +750,18 @@
 
 
     def pair_nt(A, W, columns):
-        def block(h, rows, flat):
+        def block(flat):
             return dot_nt(A[0, flat, :columns], W[0].reshape(width, W.shape[-1])) + dot_nt(
                 A[1, flat, :columns], W[1].reshape(width, W.shape[-1])
             )
 
         return block
 
-    @pl.loop(0, nrb * 2)
+    @pl.loop(0, 4)
     def _(k):
-        b, i = k // nrb, k % nrb
-        h, off = i // (half // rblk), i % (half // rblk)
-        rows = pl.ds(pl.multiple_of(off * rblk, rblk), rblk)
-        flat = pl.ds(pl.multiple_of(i * rblk, rblk), rblk)
-        g = (dot(COT[h, rows, :], Wp[b].reshape(width, width)) * GPR[b, flat, :]).astype(LOW)
+        b, h = k // 2, k % 2
+        flat = pl.ds(pl.multiple_of(h * half, half), half)
+        g = (dot(COT[h], Wp[b].reshape(width, width)) * GPR[b, flat, :]).astype(LOW)
         PG[b, flat, :] = g
         VG[pl.ds(FCB + b, 1), :] += jnp.sum(g.astype(FULL), axis=0, keepdims=True)
 
@@ -629,7 +769,6 @@
     split_rows(pair_nt(PG, Wf, width), parts[3], parts[0], p2_c)
     rp[1](0)
     weight_grad(T1, PG, Gf, 0, width)
-    rf = reduce_copies(Gf, by_rows, RfA1, RfB1, RfA2, RfB2, Rf3)
     rf[0](0)
     rf[0](1)
     landed(p2_c)
@@ -663,9 +802,9 @@
 
     def vector_copies(first, last):
         r = pl.ds(first, last - first)
-        over_z = [copy(VG.at[r], VZ.at[k - 1, r], zdev(k)) for k in range(1, ZN)]
-        mine = VO.at[y * 2 + x, c, r]
-        return r, over_z, mine, [copy(mine, mine, d) for d in near]
+        over_z = [Group([(VG.at[r], VZ.at[k - 1, r], zdev(k)) for k in range(1, ZN)], VZ.at[:, r])]
+        mine = VO.at[(y * 2 + x) * 2 + c, r]
+        return r, over_z, mine, [Group([(mine, mine, d) for d in near], VO.at[pl.ds(0, 7), r])]
 
     def vector_second(v):
         r, over_z, mine, over_near = v
@@ -677,7 +816,7 @@
         r, over_z, mine, over_near = v
         landed(over_near)
         for core in range(2):
-            vo_ref[core, r, :] = VO[0, core, r, :] + VO[1, core, r, :] + VO[2, core, r, :] + VO[3, core, r, :]
+            vo_ref[core, r, :] = (VO[core, r, :] + VO[2 + core, r, :]) + (VO[4 + core, r, :] + VO[6 + core, r, :])
 
     late, early = vector_copies(0, 4), vector_copies(8, VEC)
     start(early[1])
@@ -727,8 +866,8 @@
     ro = [
         [copy(Go.at[:, :, oy], Ro1, ydev)],
         [copy(Go.at[:, ox, y], Ro2, xdev)],
-        [copy(Go.at[(z + k) % ZN, x, y], Ro3.at[k - 1], zdev(k)) for k in range(1, ZN)],
-        [copy(go_ref.at[t], go_ref.at[t], d) for d in (cdev, ydev, gdev)],
+        [Group([(Go.at[(z + k) % ZN, x, y], Ro3.at[k - 1], zdev(k)) for k in range(1, ZN)], Ro3)],
+        [Group([(go_ref.at[t], go_ref.at[t], d) for d in (cdev, ydev, gdev)], go_ref.at[pl.ds(0, 3)])],
     ]
     start(ro[0])
 
@@ -769,12 +908,14 @@
             queries, grads = QP[p, first:, :], DO[p, first:, :]
             key = b * rblk + lax.broadcasted_iota(jnp.int32, (rblk, 1), 0)
             limit = jnp.where(key < prefix, 0, key)
-            query = first + lax.broadcasted_iota(jnp.int32, (rblk, n), 1)
+            shut = (b + 1) * rblk - first
+            query = first + lax.broadcasted_iota(jnp.int32, (rblk, shut), 1)
             dk, dv = [], []
             for e in range(2):
                 ke, ve = lane_part(keys, e), lane_part(values, e)
                 sc = dot_nt(ke, queries) - LSER[2 * p + e, :, first:]
-                w = jnp.exp(jnp.where(query >= limit, sc, -1e30))
+                head = jnp.where(query >= limit, sc[:, :shut], -1e30)
+                w = jnp.exp(jnp.concatenate([head, sc[:, shut:]], axis=1) if shut < n else head)
                 dw = dot_nt(ve, grads) - DELR[2 * p + e, :, first:]
                 ds = (w * dw).astype(LOW)
                 dv.append(dot(w.astype(LOW), grads))
@@ -786,10 +927,10 @@
         QP[p, :, :] = (DQ[...] * 0.125).astype(LOW)
 
     away = {
-        (0, 0): [lambda: rf[1](0)],
+        (0, 0): [lambda: rp[4](0), lambda: rf[1](0)],
         (1, 0): [lambda: rf[1](1)],
-        (1, 1): [lambda: rf[2](0)],
-        (1, 2): [ro_second],
+        (1, 1): [lambda: rp[4](1)],
+        (1, 2): [lambda: rf[2](0), ro_second],
     }
 
     @pl.loop(0, 2)
@@ -815,7 +956,7 @@
     rq = reduce_copies(Wf, by_lanes, RqA1, RqB1, RqA2, RqB2, Rq3)
     rq[0](0)
     away = {
-        (2, 0): [lambda: rp[2](0), lambda: rf[2](1)],
+        (2, 0): [lambda: rf[2](1), lambda: rp[2](0)],
         (2, 1): [ro_third],
         (2, 3): [lambda: rq[1](0)],
     }
@@ -878,16 +1019,22 @@
     vector_second(late)
     vector_last(early)
     landed(ro[3])
+    out_c += [
+        pltpu.make_async_copy(a, b, ls.at[4 + i]) for i, (a, b) in enumerate(((go_ref, go_h), (gq_ref, gq_h), (vo_ref, vo_h)))
+    ]
+    out_c[4].start()
     rq[3](0, gq_ref)
     vector_last(late)
+    out_c[6].start()
     rq[3](1, gq_ref)
     rq[3](2, gq_ref)
+    out_c[5].start()
 
     waited = {id(m) for m in n2_c + pm_c + n1_c}
     for step in fw:
         for group in step:
             waited |= {id(m) for m in group}
-    sent([m for m in made if id(m) not in waited])
+    sent([m for m in pending if id(m) not in waited])
     for cp in out_c:
         cp.wait()
 
@@ -943,7 +1090,6 @@
     packed, own = 3 * cols + HD, 2 * cols
     hr = rows // 2
     ANY = pl.BlockSpec(memory_space=pl.ANY)
-    IN_VMEM = pl.BlockSpec(memory_space=pltpu.VMEM)
 
     def reduce_space(lanes):
         return [
@@ -977,6 +1123,8 @@
             pltpu.VMEM((ZN - 1, 2, hr, width), LOW),
             pltpu.VMEM((hr, width), LOW),
             pltpu.VMEM((hr, width), LOW),
+            pltpu.VMEM((XN, hr, width), LOW),
+            pltpu.VMEM((2, hr, width), LOW),
         ]
         + [
             pltpu.VMEM((ZN, XN, hr, own), LOW),
@@ -1015,7 +1163,13 @@
             pltpu.VMEM((VEC, width), FULL),
             pltpu.VMEM((ZN - 1, VEC, width), FULL),
         ]
-        + [pltpu.VMEM((4, 2, VEC, width), FULL)]
+        + [
+            pltpu.VMEM((8, VEC, width), FULL),
+            pltpu.VMEM((rows, packed), FULL),
+            pltpu.VMEM((4, hr, own), FULL),
+            pltpu.VMEM((2, VEC, width), FULL),
+            pltpu.SMEM(prefix.shape, prefix.dtype),
+        ]
         + [
             pltpu.SemaphoreType.DMA((SEMS,)),
             pltpu.SemaphoreType.DMA((SEMS,)),
@@ -1034,8 +1188,8 @@
     grown = pl.pallas_call(
         functools.partial(block_kernel, repeat, seq_len),
         out_shape=out_shape,
-        in_specs=[ANY, pl.BlockSpec(memory_space=pltpu.SMEM)] + [ANY] * 13,
-        out_specs=[ANY] * 2 + [IN_VMEM] * 2 + [ANY] * 2 + [IN_VMEM],
+        in_specs=[ANY] * 15,
+        out_specs=[ANY] * 7,
         scratch_shapes=scratch,
         compiler_params=pltpu.CompilerParams(
             collective_id=0, has_side_effects=True, vmem_limit_bytes=62 * 1024 * 1024
@@ -1043,7 +1197,6 @@
     )(tokens, prefix, cotangent, *params)
 
     vector = jax.ShapeDtypeStruct((rows,), FULL)
-    small = (2, 3, 5, 7, 8, 9, 11, 13)
     results = pl.pallas_call(
         functools.partial(unpack_kernel, repeat),
         out_shape=[
@@ -1063,7 +1216,7 @@
             vector,
         ],
         in_specs=[ANY] * 7,
-        out_specs=[IN_VMEM if i in small else ANY for i in range(14)],
+        out_specs=[ANY] * 14,
         scratch_shapes=[
             pltpu.VMEM((rows, packed), FULL),
             pltpu.VMEM((4, hr, own), FULL),
@@ -1074,7 +1227,10 @@
             pltpu.VMEM((half, width), LOW),
             pltpu.VMEM((rows, units), FULL),
             pltpu.VMEM((rows, units), FULL),
-            pltpu.SemaphoreType.DMA((13,)),
+            pltpu.VMEM((8, rows), FULL),
+            pltpu.VMEM((2, rows), FULL),
+            pltpu.VMEM((1, 4 * rows), FULL),
+            pltpu.SemaphoreType.DMA((21,)),
         ],
         compiler_params=pltpu.CompilerParams(vmem_limit_bytes=62 * 1024 * 1024),
     )(*grown)
@@ -1088,11 +1244,13 @@
 
 def unpack_kernel(
     repeat, bo, ig, gq_h, go_h, gf, gp, vo_h,
-    bo_out, ig_out, gain1, shift1, wq_h, qvb, wo_h, outb, gain2, shift2, wf, fcb, wp, projb,
-    gq, go, vo, wq, wo, b1, b2, w1, w2, sems,
+    bo_out, ig_out, gain1, shift1, wq_h, qvb_h, wo_h, outb, gain2, shift2, wf, fcb_h, wp, projb,
+    gq, go, vo, wq, wo, b1, b2, w1, w2, sv, sq, sf, sems,
 ):
     moves = [(vo_h, vo), (gq_h, gq), (go_h, go), (ig, b2), (bo, b1), (gf, w1), (gp, w2)]
     moves += [(wq, wq_h), (wo, wo_h), (b2, ig_out), (b1, bo_out), (w1, wf), (w2, wp)]
+    vectors = ((GAIN1, gain1), (SHIFT1, shift1), (OUTB, outb), (GAIN2, gain2), (SHIFT2, shift2), (PROJB, projb))
+    moves += [(sv.at[j], out) for j, (_, out) in enumerate(vectors)] + [(sq, qvb_h), (sf.at[0], fcb_h)]
     moves = [pltpu.make_async_copy(a, b, sems.at[i]) for i, (a, b) in enumerate(moves)]
     for cp in moves[:7]:
         cp.start()
@@ -1120,10 +1278,10 @@
     moves[0].wait()
     s = lax.axis_index("dp") // repeat
     width = vo.shape[2]
-    n = gain1.shape[0]
+    n = sv.shape[1]
     both = pltpu.roll(vo[0] + vo[1], (GROUPS - s) % GROUPS * n, 1)
-    for i, out in ((GAIN1, gain1), (SHIFT1, shift1), (OUTB, outb), (GAIN2, gain2), (SHIFT2, shift2), (PROJB, projb)):
-        out[...] = both[i, :n]
+    for j, (i, _) in enumerate(vectors):
+        sv[j : j + 1, :] = both[i : i + 1, :n]
     owner = s // 2
     core, b, odd = owner % 2, owner // 2, s % 2
     place = lax.broadcasted_iota(jnp.int32, (1, width), 1)
@@ -1136,11 +1294,13 @@
     q = lanes(row, 0, 128, 0) + lanes(row, 384, 448, -256)
     v = lanes(row, 256, 384, -256) + lanes(row, 512, 576, -384)
     back = (width - odd * n) % width
-    qvb[0:1, :] = pltpu.roll(q, back, 1)[:, :n]
-    qvb[1:2, :] = pltpu.roll(v, back, 1)[:, :n]
+    sq[0:1, :] = pltpu.roll(q, back, 1)[:, :n]
+    sq[1:2, :] = pltpu.roll(v, back, 1)[:, :n]
     row = vo[core, pl.ds(FCB + b, 1), :]
-    fcb[...] = pltpu.roll(row, odd * (width // 2), 1)[0, : width // 2]
-    for i in range(7, 13):
+    sf[...] = pltpu.roll(row, odd * (width // 2), 1)[:, : width // 2]
+    for i in range(13, 21):
+        moves[i].start()
+    for i in range(7, 21):
         moves[i].wait()
 
 

time: 149 us -> 142 us (0.953)
  Pallas kernels: 148 us -> 141 us
    pallas_call x1, Pallas kernels: 144 us -> 138 us  [on_device(): pl.pallas_call(functools.partial(block_kernel, repeat, seq_len), out_shap...]
where the time goes in v4:
time: 142 us
  Pallas kernels  141 us (99%)
    pallas_call x1, Pallas kernels, on_device(): pl.pallas_call(functools.partial(block_kernel, repeat, seq_len), out_shap...  138 us
    pallas_call x1, Pallas kernels, on_device(): pl.pallas_call(functools.partial(unpack_kernel, repeat), out_shape=[out_s...  3.14 us

profile of v4, /device:TPU:0, one launch (start us, length us, event | category | flops | bytes accessed | tf_op | source)
XLA Modules:
  0.0 142.3 jit_solution(7946665291590085729)
XLA Ops:
  0.7 138.3 %shard_map.254 = (bf16[512,768]{1,0:T(8,128)(2,1)}, bf16[512,768]{1,0:T(8,128)(2,1)}, f32[96,640]{1,0:T(8,128)}, f32[4,48,384]{2,1,0:T(8,128)}, f32[96,768]{1,0:...) custom-call(bf16[512,768]{1,0:T(8,128)(2,1)} %refs_0_.1, s32[2]{0:T(128)} %refs_1_.1, bf16[512,768]{1,0:T(8,128)(2,1)} %refs_2_.1, ...), custom_call_target="tpu_custom_call" | custom-call | tf_op jit(solution)/shard_map/pallas_call | solution.py:1188
  138.9 3.1 %shard_map.255 = (bf16[512,768]{1,0:T(8,128)(2,1)}, bf16[512,768]{1,0:T(8,128)(2,1)}, f32[96]{0:T(128)}, f32[96]{0:T(128)}, f32[3,96,192]{2,1,0:T(8,128)}, /*ind...) custom-call(bf16[512,768]{1,0:T(8,128)(2,1)} %get-tuple-element.35.b, ...), custom_call_target="tpu_custom_call" | custom-call | tf_op jit(solution)/shard_map/pallas_call | solution.py:1200

commit v5 on v4

--- a/solution.py
+++ b/solution.py
@@ -13,7 +13,7 @@
 EPSILON = 1e-05
 HD = 64
 GROUPS, ZN, XN = 8, 4, 2
-SEMS = 134
+SEMS = 140
 VEC = 16
 
 GAIN1, SHIFT1, QKVB, OUTB, GAIN2, SHIFT2, PROJB, FCB = 0, 1, 2, 8, 9, 10, 11, 12
@@ -40,7 +40,7 @@
         RqA1, RqB1, RqA2, RqB2, Rq3,
         RfA1, RfB1, RfA2, RfB2, Rf3,
         RpA1, RpB1, RpA2, RpB2, RpA3, RpB3, RpEA, RpEB,
-        Ro1, Ro2, Ro3,
+        Ro1A, Ro1B, Ro2A, Ro2B, Ro3,
         TOK, COT, N1F, N2F, RS, N1, N2, T0, T1,
         QP, KP, VP, CTX, DO, DQ, LSER, DELR,
         MID, V0, V1, H, GPR, PG,
@@ -293,11 +293,18 @@
             steps.append((near, zs, far))
         return steps
 
+    oa, ob = pl.ds(0, 2 * third), pl.ds(2 * third, third)
     ow = [
         (
             [Group([(Wo.at[z, x, y], Wo.at[z, x, y], zdev(k)) for k in range(1, ZN)], Wo.at[pl.ds(0, ZN - 1), x, y])],
-            [copy(Wo.at[:, x, y], Wo.at[:, x, y], xdev)],
-            [copy(Wo.at[:, :, y], Wo.at[:, :, y], ydev)],
+            [
+                copy(Wo.at[:, x, y, oa], Wo.at[:, x, y, oa], xdev),
+                copy(Wo.at[:, x, y, ob], Wo.at[:, x, y, ob], ydev),
+            ],
+            [
+                copy(Wo.at[:, :, y, oa], Wo.at[:, :, y, oa], ydev),
+                copy(Wo.at[:, x, :, ob], Wo.at[:, x, :, ob], xdev),
+            ],
         )
     ]
     qw, pw, fw = gather(Wq, thin), gather_wide(Wp), gather(Wf, thin)
@@ -818,22 +825,31 @@
         for core in range(2):
             vo_ref[core, r, :] = (VO[core, r, :] + VO[2 + core, r, :]) + (VO[4 + core, r, :] + VO[6 + core, r, :])
 
-    late, early = vector_copies(0, 4), vector_copies(8, VEC)
-    start(early[1])
+    late = vector_copies(0, 4)
+    er = pl.ds(8, VEC - 8)
+    early = [
+        [Group([(VG.at[er], VZ.at[k - 1, er], zdev(k)) for k in range(1, ZN)], VZ.at[:, er])],
+        [copy(VO.at[0, er], VO.at[1, er], xdev)],
+        [copy(VO.at[2, er], VO.at[3, er], ydev)],
+        [copy(vo_ref.at[c, er], vo_ref.at[c, er], cdev)],
+    ]
+    start(early[0])
+
+    def early_hop(i):
+        landed(early[i])
+        if i == 0:
+            VO[0, er, :] = VG[er, :] + VZ[0, er, :] + VZ[1, er, :] + VZ[2, er, :]
+        elif i == 1:
+            VO[2, er, :] = VO[0, er, :] + VO[1, er, :]
+        else:
+            vo_ref[c, er, :] = VO[2, er, :] + VO[3, er, :]
+        start(early[i + 1])
+
     pm_c = [copy(parts[1], V0, cdev)]
     split_rows(pair_nt(H, Wp, width), parts[1], MID, pm_c, MID)
     rp[1](1)
     transpose_all(N1, T1)
     landed(ag_c)
-    landed(pm_c)
-
-    @pl.loop(0, half // 128)
-    def _(i):
-        r = row_tile(i)
-        TOK[r, :] = (MID[r, :] + (V0[r, :] + vrow(PROJB))).astype(LOW)
-
-    out_c = [pltpu.make_async_copy(TOK, bo_h, ls.at[0]), pltpu.make_async_copy(N1.at[c], ig_h, ls.at[1])]
-    out_c[0].start()
 
     @pl.loop(0, nrb)
     def _(i):
@@ -864,12 +880,11 @@
         Go[pl.ds(m * (ZN // 2), ZN // 2)] = g
 
     ro = [
-        [copy(Go.at[:, :, oy], Ro1, ydev)],
-        [copy(Go.at[:, ox, y], Ro2, xdev)],
+        [copy(Go.at[:, :, oy, oa], Ro1A, ydev), copy(Go.at[:, ox, :, ob], Ro1B, xdev)],
+        [copy(Go.at[:, ox, y, oa], Ro2A, xdev), copy(Go.at[:, x, oy, ob], Ro2B, ydev)],
         [Group([(Go.at[(z + k) % ZN, x, y], Ro3.at[k - 1], zdev(k)) for k in range(1, ZN)], Ro3)],
         [Group([(go_ref.at[t], go_ref.at[t], d) for d in (cdev, ydev, gdev)], go_ref.at[pl.ds(0, 3)])],
     ]
-    start(ro[0])
 
     def ro_second():
         landed(ro[0])
@@ -877,7 +892,8 @@
         @pl.loop(0, ZN)
         def _(k):
             for i in range(XN):
-                Go[k, i, y] = (Go[k, i, y].astype(FULL) + Ro1[k, i].astype(FULL)).astype(LOW)
+                Go[k, i, y, oa] = (Go[k, i, y, oa].astype(FULL) + Ro1A[k, i].astype(FULL)).astype(LOW)
+                Go[k, x, i, ob] = (Go[k, x, i, ob].astype(FULL) + Ro1B[k, i].astype(FULL)).astype(LOW)
 
         start(ro[1])
 
@@ -886,7 +902,8 @@
 
         @pl.loop(0, ZN)
         def _(k):
-            Go[k, x, y] = (Go[k, x, y].astype(FULL) + Ro2[k].astype(FULL)).astype(LOW)
+            Go[k, x, y, oa] = (Go[k, x, y, oa].astype(FULL) + Ro2A[k].astype(FULL)).astype(LOW)
+            Go[k, x, y, ob] = (Go[k, x, y, ob].astype(FULL) + Ro2B[k].astype(FULL)).astype(LOW)
 
         start(ro[2])
 
@@ -928,9 +945,11 @@
 
     away = {
         (0, 0): [lambda: rp[4](0), lambda: rf[1](0)],
+        (0, 3): [lambda: start(ro[0]), lambda: early_hop(0)],
         (1, 0): [lambda: rf[1](1)],
         (1, 1): [lambda: rp[4](1)],
-        (1, 2): [lambda: rf[2](0), ro_second],
+        (1, 2): [lambda: rf[2](0)],
+        (1, 3): [lambda: early_hop(1)],
     }
 
     @pl.loop(0, 2)
@@ -955,10 +974,20 @@
     weight_grad(T1, H, Wf, 0, 384)
     rq = reduce_copies(Wf, by_lanes, RqA1, RqB1, RqA2, RqB2, Rq3)
     rq[0](0)
+    landed(pm_c)
+
+    @pl.loop(0, half // 128)
+    def _(i):
+        r = row_tile(i)
+        TOK[r, :] = (MID[r, :] + (V0[r, :] + vrow(PROJB))).astype(LOW)
+
+    out_c = [pltpu.make_async_copy(TOK, bo_h, ls.at[0]), pltpu.make_async_copy(N1.at[c], ig_h, ls.at[1])]
+    out_c[0].start()
+
     away = {
-        (2, 0): [lambda: rf[2](1), lambda: rp[2](0)],
-        (2, 1): [ro_third],
-        (2, 3): [lambda: rq[1](0)],
+        (2, 0): [lambda: rf[2](1)],
+        (2, 1): [lambda: early_hop(2), ro_second],
+        (2, 3): [lambda: rp[2](0)],
     }
     attention_back(2, away)
 
@@ -980,11 +1009,13 @@
     weight_grad(T1, H, Wf, 384, packed)
     rq[0](1)
     rq[0](2)
+    rq[1](0)
 
     p1_c = [copy(parts[1], V1, cdev)]
     sent(pm_c)
     split_rows(pair_nt(H, Wq, packed), parts[1], parts[2], p1_c)
     rp[2](1)
+    ro_third()
     landed(p1_c)
 
     sent(n1_c)
@@ -1002,10 +1033,8 @@
 
     start(late[1])
     rq[2](0)
-    vector_second(early)
     rq[1](1)
     rq[1](2)
-    ro_last()
     gp_ref, gf_ref = MID.at[pl.ds(0, 2 * hr)], MID.at[pl.ds(2 * hr, 2 * hr)]
     out_c += [pltpu.make_async_copy(gp_ref, gp_h, ls.at[2]), pltpu.make_async_copy(gf_ref, gf_h, ls.at[3])]
     rp[3](0, gp_ref)
@@ -1017,7 +1046,8 @@
     rq[2](1)
     rq[2](2)
     vector_second(late)
-    vector_last(early)
+    ro_last()
+    landed(early[3])
     landed(ro[3])
     out_c += [
         pltpu.make_async_copy(a, b, ls.at[4 + i]) for i, (a, b) in enumerate(((go_ref, go_h), (gq_ref, gq_h), (vo_ref, vo_h)))
@@ -1127,8 +1157,10 @@
             pltpu.VMEM((2, hr, width), LOW),
         ]
         + [
-            pltpu.VMEM((ZN, XN, hr, own), LOW),
-            pltpu.VMEM((ZN, hr, own), LOW),
+            pltpu.VMEM((ZN, XN, hr // 3 * 2, own), LOW),
+            pltpu.VMEM((ZN, 2, hr // 3, own), LOW),
+            pltpu.VMEM((ZN, hr // 3 * 2, own), LOW),
+            pltpu.VMEM((ZN, hr // 3, own), LOW),
             pltpu.VMEM((ZN - 1, hr, own), LOW),
         ]
         + [

time: 142 us -> 139 us (0.979)
  Pallas kernels: 141 us -> 138 us
    pallas_call x1, Pallas kernels: 138 us -> 135 us  [on_device(): pl.pallas_call(functools.partial(block_kernel, repeat, seq_len), out_shap...]
where the time goes in v5:
time: 139 us
  Pallas kernels  138 us (99%)
    pallas_call x1, Pallas kernels, on_device(): pl.pallas_call(functools.partial(block_kernel, repeat, seq_len), out_shap...  135 us
    pallas_call x1, Pallas kernels, on_device(): pl.pallas_call(functools.partial(unpack_kernel, repeat), out_shape=[out_s...  3.14 us

profile of v5, /device:TPU:0, one launch (start us, length us, event | category | flops | bytes accessed | tf_op | source)
XLA Modules:
  0.0 139.3 jit_solution(9228239481587912329)
XLA Ops:
  0.7 135.3 %shard_map.254 = (bf16[512,768]{1,0:T(8,128)(2,1)}, bf16[512,768]{1,0:T(8,128)(2,1)}, f32[96,640]{1,0:T(8,128)}, f32[4,48,384]{2,1,0:T(8,128)}, f32[96,768]{1,0:...) custom-call(bf16[512,768]{1,0:T(8,128)(2,1)} %refs_0_.1, s32[2]{0:T(128)} %refs_1_.1, bf16[512,768]{1,0:T(8,128)(2,1)} %refs_2_.1, ...), custom_call_target="tpu_custom_call" | custom-call | tf_op jit(solution)/shard_map/pallas_call | solution.py:1220
  135.9 3.1 %shard_map.255 = (bf16[512,768]{1,0:T(8,128)(2,1)}, bf16[512,768]{1,0:T(8,128)(2,1)}, f32[96]{0:T(128)}, f32[96]{0:T(128)}, f32[3,96,192]{2,1,0:T(8,128)}, /*ind...) custom-call(bf16[512,768]{1,0:T(8,128)(2,1)} %get-tuple-element.35.b, ...), custom_call_target="tpu_custom_call" | custom-call | tf_op jit(solution)/shard_map/pallas_call | solution.py:1232

commit v6 on v5

--- a/solution.py
+++ b/solution.py
@@ -13,7 +13,7 @@
 EPSILON = 1e-05
 HD = 64
 GROUPS, ZN, XN = 8, 4, 2
-SEMS = 140
+SEMS = 145
 VEC = 16
 
 GAIN1, SHIFT1, QKVB, OUTB, GAIN2, SHIFT2, PROJB, FCB = 0, 1, 2, 8, 9, 10, 11, 12
@@ -968,12 +968,13 @@
                 H[b, flat, k * 128 : (k + 1) * 128] = g
                 VG[QKVB + b : QKVB + b + 1, k * 128 : (k + 1) * 128] += jnp.sum(g.astype(FULL), axis=0, keepdims=True)
 
-    by_lanes = [(pl.ds(0, hr), pl.ds(hr, hr), pl.ds(0, hr), pl.ds(0, 384))]
-    rest = pl.ds(384, packed - 384)
+    main, rest = pl.ds(0, 384), pl.ds(384, packed - 384)
+    by_lanes = [pairs[0] + (pl.ds(0, third), main), pairs[1] + (pl.ds(third, 2 * third), main)]
     by_lanes += [pairs[1] + (pl.ds(third, 2 * third), rest), pairs[0] + (pl.ds(0, third), rest)]
     weight_grad(T1, H, Wf, 0, 384)
     rq = reduce_copies(Wf, by_lanes, RqA1, RqB1, RqA2, RqB2, Rq3)
     rq[0](0)
+    rq[0](1)
     landed(pm_c)
 
     @pl.loop(0, half // 128)
@@ -987,7 +988,7 @@
     away = {
         (2, 0): [lambda: rf[2](1)],
         (2, 1): [lambda: early_hop(2), ro_second],
-        (2, 3): [lambda: rp[2](0)],
+        (2, 3): [lambda: rp[2](0), lambda: rq[1](0)],
     }
     attention_back(2, away)
 
@@ -1007,13 +1008,14 @@
                 VG[QKVB + b : QKVB + b + 1, at_j] += jnp.sum(packs[b][j], axis=0, keepdims=True)
 
     weight_grad(T1, H, Wf, 384, packed)
-    rq[0](1)
     rq[0](2)
-    rq[1](0)
+    rq[0](3)
+    rq[1](1)
 
     p1_c = [copy(parts[1], V1, cdev)]
     sent(pm_c)
     split_rows(pair_nt(H, Wq, packed), parts[1], parts[2], p1_c)
+    rq[2](0)
     rp[2](1)
     ro_third()
     landed(p1_c)
@@ -1032,9 +1034,9 @@
     out_c[1].start()
 
     start(late[1])
-    rq[2](0)
-    rq[1](1)
+    rq[2](1)
     rq[1](2)
+    rq[1](3)
     gp_ref, gf_ref = MID.at[pl.ds(0, 2 * hr)], MID.at[pl.ds(2 * hr, 2 * hr)]
     out_c += [pltpu.make_async_copy(gp_ref, gp_h, ls.at[2]), pltpu.make_async_copy(gf_ref, gf_h, ls.at[3])]
     rp[3](0, gp_ref)
@@ -1043,8 +1045,8 @@
     rf[3](0, gf_ref)
     rf[3](1, gf_ref)
     out_c[3].start()
-    rq[2](1)
     rq[2](2)
+    rq[2](3)
     vector_second(late)
     ro_last()
     landed(early[3])
@@ -1054,10 +1056,11 @@
     ]
     out_c[4].start()
     rq[3](0, gq_ref)
+    rq[3](1, gq_ref)
     vector_last(late)
     out_c[6].start()
-    rq[3](1, gq_ref)
     rq[3](2, gq_ref)
+    rq[3](3, gq_ref)
     out_c[5].start()
 
     waited = {id(m) for m in n2_c + pm_c + n1_c}
@@ -1286,15 +1289,15 @@
     moves = [pltpu.make_async_copy(a, b, sems.at[i]) for i, (a, b) in enumerate(moves)]
     for cp in moves[:7]:
         cp.start()
-    for i in range(3, 7):
-        moves[i].wait()
-        moves[i + 6].start()
     moves[1].wait()
     for k in range(3):
         wq[k] = jnp.concatenate(
             [gq[:, k * 128 : (k + 1) * 128], gq[:, 384 + k * HD : 384 + (k + 1) * HD]], axis=1
         )
     moves[7].start()
+    for i in (3, 4):
+        moves[i].wait()
+        moves[i + 6].start()
     moves[2].wait()
     m = [jnp.concatenate([go[core], go[2 + core]], axis=0) for core in range(2)]
     wo[...] = jnp.concatenate(
@@ -1307,6 +1310,9 @@
         axis=1,
     )
     moves[8].start()
+    for i in (5, 6):
+        moves[i].wait()
+        moves[i + 6].start()
     moves[0].wait()
     s = lax.axis_index("dp") // repeat
     width = vo.shape[2]

time: 139 us -> 138 us (level)
  no operation moved by 1% of the time
where the time goes in v6:
time: 138 us
  Pallas kernels  137 us (99%)
    pallas_call x1, Pallas kernels, on_device(): pl.pallas_call(functools.partial(block_kernel, repeat, seq_len), out_shap...  134 us
    pallas_call x1, Pallas kernels, on_device(): pl.pallas_call(functools.partial(unpack_kernel, repeat), out_shape=[out_s...  3.04 us

profile of v6, /device:TPU:0, one launch (start us, length us, event | category | flops | bytes accessed | tf_op | source)
XLA Modules:
  0.0 137.8 jit_solution(5152258250092677674)
XLA Ops:
  0.7 133.9 %shard_map.254 = (bf16[512,768]{1,0:T(8,128)(2,1)}, bf16[512,768]{1,0:T(8,128)(2,1)}, f32[96,640]{1,0:T(8,128)}, f32[4,48,384]{2,1,0:T(8,128)}, f32[96,768]{1,0:...) custom-call(bf16[512,768]{1,0:T(8,128)(2,1)} %refs_0_.1, s32[2]{0:T(128)} %refs_1_.1, bf16[512,768]{1,0:T(8,128)(2,1)} %refs_2_.1, ...), custom_call_target="tpu_custom_call" | custom-call | tf_op jit(solution)/shard_map/pallas_call | solution.py:1223
  134.6 3.0 %shard_map.255 = (bf16[512,768]{1,0:T(8,128)(2,1)}, bf16[512,768]{1,0:T(8,128)(2,1)}, f32[96]{0:T(128)}, f32[96]{0:T(128)}, f32[3,96,192]{2,1,0:T(8,128)}, /*ind...) custom-call(bf16[512,768]{1,0:T(8,128)(2,1)} %get-tuple-element.35.b, ...), custom_call_target="tpu_custom_call" | custom-call | tf_op jit(solution)/shard_map/pallas_call | solution.py:1235

commit v7 on v6

--- a/solution.py
+++ b/solution.py
@@ -588,7 +588,7 @@
 
     @pl.loop(0, nrb * 2)
     def _(k):
-        @pl.when(k == 1)
+        @pl.when(k == 0)
         def _():
             two_go(pw, 1)
 
@@ -1050,13 +1050,13 @@
     vector_second(late)
     ro_last()
     landed(early[3])
-    landed(ro[3])
     out_c += [
         pltpu.make_async_copy(a, b, ls.at[4 + i]) for i, (a, b) in enumerate(((go_ref, go_h), (gq_ref, gq_h), (vo_ref, vo_h)))
     ]
-    out_c[4].start()
     rq[3](0, gq_ref)
     rq[3](1, gq_ref)
+    landed(ro[3])
+    out_c[4].start()
     vector_last(late)
     out_c[6].start()
     rq[3](2, gq_ref)

time: 138 us -> 138 us (level)
  no operation moved by 1% of the time
where the time goes in v7:
time: 138 us
  Pallas kernels  137 us (99%)
    pallas_call x1, Pallas kernels, on_device(): pl.pallas_call(functools.partial(block_kernel, repeat, seq_len), out_shap...  134 us
    pallas_call x1, Pallas kernels, on_device(): pl.pallas_call(functools.partial(unpack_kernel, repeat), out_shape=[out_s...  3.04 us

profile of v7, /device:TPU:0, one launch (start us, length us, event | category | flops | bytes accessed | tf_op | source)
XLA Modules:
  0.0 137.9 jit_solution(6405000960521462203)
XLA Ops:
  0.7 134.0 %shard_map.254 = (bf16[512,768]{1,0:T(8,128)(2,1)}, bf16[512,768]{1,0:T(8,128)(2,1)}, f32[96,640]{1,0:T(8,128)}, f32[4,48,384]{2,1,0:T(8,128)}, f32[96,768]{1,0:...) custom-call(bf16[512,768]{1,0:T(8,128)(2,1)} %refs_0_.1, s32[2]{0:T(128)} %refs_1_.1, bf16[512,768]{1,0:T(8,128)(2,1)} %refs_2_.1, ...), custom_call_target="tpu_custom_call" | custom-call | tf_op jit(solution)/shard_map/pallas_call | solution.py:1223
  134.7 3.0 %shard_map.255 = (bf16[512,768]{1,0:T(8,128)(2,1)}, bf16[512,768]{1,0:T(8,128)(2,1)}, f32[96]{0:T(128)}, f32[96]{0:T(128)}, f32[3,96,192]{2,1,0:T(8,128)}, /*ind...) custom-call(bf16[512,768]{1,0:T(8,128)(2,1)} %get-tuple-element.35.b, ...), custom_call_target="tpu_custom_call" | custom-call | tf_op jit(solution)/shard_map/pallas_call | solution.py:1235
